TPU v7x, 32 devices: a whole 2x2x4 slice. The times are simulated.
32 devices in a mesh: section: 2 (over x), ctx: 2 (over core), shard: 8 (over z, y).
Axes of the slice: x: 2, y: 2, z: 4, core: 2. Of those that a mesh axis runs over, the one named last changes fastest.
Arguments:
- tokens: bfloat16 [2, 1024, 1600], P(None, ('ctx', 'shard')), may hold values from -6 to 6
- block_order: int32 [16, 2], replicated, may hold values from 0 to 31, as said below
- cotangent: bfloat16 [2, 1024, 1600], P(None, ('ctx', 'shard')), may hold values from -6 to 6
- first_gain: bfloat16 [2, 1600], P('section', 'shard'), may hold values from 0.099609375 to 1.8984375
- first_shift: bfloat16 [2, 1600], P('section', 'shard'), may hold values from -1.75 to 1.75
- query_key_value_weight: bfloat16 [2, 1600, 4800], P('section', 'shard'), may hold values from -0.15625 to 0.15625
- input_bias: bfloat16 [2, 3200], P('section', 'shard'), may hold values from -1.75 to 1.75
- attention_out_weight: bfloat16 [2, 1600, 1600], P('section', 'shard'), may hold values from -1.75 to 1.75
- attention_out_bias: bfloat16 [2, 1600], P('section', 'shard'), may hold values from -1.75 to 1.75
- second_gain: bfloat16 [2, 1600], P('section', 'shard'), may hold values from 0.099609375 to 1.8984375
- second_shift: bfloat16 [2, 1600], P('section', 'shard'), may hold values from -1.75 to 1.75
- widen_weight: bfloat16 [2, 1600, 6400], P('section', 'shard'), may hold values from -0.15625 to 0.15625
- widen_bias: bfloat16 [2, 6400], P('section', 'shard'), may hold values from -1.75 to 1.75
- narrow_weight: bfloat16 [2, 6400, 1600], P('section', 'shard'), may hold values from -0.078125 to 0.078125
- narrow_bias: bfloat16 [2, 1600], P('section', 'shard'), may hold values from -1.75 to 1.75
Outputs:
- layer_out: float32 [2, 2, 1024, 1600], P('section', None, ('ctx', 'shard'))
- d_in: float32 [2, 2, 1024, 1600], P('section', None, ('ctx', 'shard'))
- grad_first_gain: float32 [2, 1600], P('section', 'shard')
- grad_first_shift: float32 [2, 1600], P('section', 'shard')
- grad_input_weight: float32 [2, 1600, 4800], P('section', 'shard')
- grad_input_bias: float32 [2, 3200], P('section', 'shard')
- grad_output_weight: float32 [2, 1600, 1600], P('section', 'shard')
- grad_output_bias: float32 [2, 1600], P('section', 'shard')
- grad_second_gain: float32 [2, 1600], P('section', 'shard')
- grad_second_shift: float32 [2, 1600], P('section', 'shard')
- grad_expand_weight: float32 [2, 1600, 6400], P('section', 'shard')
- grad_expand_bias: float32 [2, 6400], P('section', 'shard')
- grad_reduce_weight: float32 [2, 6400, 1600], P('section', 'shard')
- grad_reduce_bias: float32 [2, 1600], P('section', 'shard')
Inputs may be any that keep to these rules, and one draw needn't show every extreme that they name: `block_order`: row p names the two blocks of 32 positions in storage slot p: the first is below 16, the second equals 31 minus the first, and every block number occurs once in the table.
All inputs are finite; a program needn't handle non-finite values.
Results may differ from a plain program's by a relative error of at most 0.034.
Values may be sent and summed in bfloat16 or wider, within the bound.
A program may use at most 384 MiB of HBM per device.

v0:
```python
from functools import partial

import jax
import jax.numpy as jnp
from jax import lax
from jax.sharding import PartitionSpec as P

HEADS = 25
HD = 64


EPSILON = 1e-05
MASKED = -1e30


def from_behind(value, axis, by):
    peers = lax.axis_size(axis)
    pairs = [(i, i + by) for i in range(peers) if 0 <= i + by < peers]
    return lax.ppermute(value, axis, pairs)


def layer_norm(values, norm_gain, norm_shift):
    center = values - jnp.mean(values, axis=-1, keepdims=True)
    spread = jnp.mean(center * center, axis=-1, keepdims=True)
    return center * lax.rsqrt(spread + EPSILON) * norm_gain + norm_shift


def gelu_tanh(values):
    return jax.nn.gelu(values, approximate=True)


def block_size(piece_rows):
    step_rows = min(piece_rows, 1024)
    while piece_rows % step_rows:
        step_rows = step_rows - 1
    return step_rows


def positions(order_flat, first_row, row_count, block_rows):
    row_ids = first_row + jnp.arange(row_count, dtype=jnp.int32)
    block_index = row_ids // block_rows
    block_ids = jnp.arange(order_flat.shape[0], dtype=jnp.int32)
    chosen = jnp.sum(
        jnp.where(block_index[:, None] == block_ids[None, :], order_flat[None, :], 0), axis=1
    )
    return chosen * block_rows + row_ids % block_rows


def to_heads(values):
    return values.reshape(values.shape[0], HEADS, HD).transpose(1, 0, 2)


def from_heads(values):
    return values.transpose(1, 0, 2).reshape(values.shape[1], HEADS * HD)


def reorder(values, axis_pos, groups):
    old_shape = values.shape
    new_shape = (
        old_shape[:axis_pos]
        + (groups, 2, old_shape[axis_pos] // (2 * groups))
        + old_shape[axis_pos + 1 :]
    )
    return jnp.swapaxes(values.reshape(new_shape), axis_pos, axis_pos + 1).reshape(old_shape)


def split_pairs(fetched, model_width):
    piece_rows = fetched.shape[0]
    step_rows = block_size(piece_rows)
    step_count = piece_rows // step_rows
    key_blocks = fetched[:, :model_width].reshape(step_count, step_rows, HEADS, HD)
    value_blocks = fetched[:, model_width:].reshape(step_count, step_rows, HEADS, HD)
    first_rows = step_rows * jnp.arange(step_count, dtype=jnp.int32)
    return ((key_blocks, value_blocks, first_rows), step_rows)


def forward_layer(input_to_layer, weights, query_pos, order_flat, block_rows):
    (
        first_gain,
        first_shift,
        query_key_value_weight,
        input_bias,
        attention_out_weight,
        attention_out_bias,
        second_gain,
        second_shift,
        widen_weight,
        widen_bias,
        narrow_weight,
        narrow_bias,
    ) = weights
    row_count, model_width = input_to_layer.shape
    head_scale = HD ** (-0.5)
    first_normalized = layer_norm(
        input_to_layer, first_gain.astype(jnp.float32), first_shift.astype(jnp.float32)
    ).astype(jnp.bfloat16)
    attention_projected = jnp.dot(
        first_normalized, query_key_value_weight, preferred_element_type=jnp.float32
    )
    bias_full = input_bias.astype(jnp.float32)
    queries = (attention_projected[:, :model_width] + bias_full[:model_width]).astype(jnp.bfloat16)
    key_low = attention_projected[:, model_width : 2 * model_width].astype(jnp.bfloat16)
    values = (attention_projected[:, 2 * model_width :] + bias_full[model_width:]).astype(
        jnp.bfloat16
    )
    query_heads = to_heads(queries)
    initial = (
        jnp.full((HEADS, row_count), MASKED, jnp.float32),
        jnp.zeros((HEADS, row_count), jnp.float32),
        jnp.zeros((HEADS, row_count, HD), jnp.float32),
    )
    running = initial
    blocks, step_rows = split_pairs(
        lax.all_gather(
            jnp.concatenate([key_low, values], axis=1), ("ctx", "shard"), axis=0, tiled=True
        ),
        model_width,
    )

    def absorb_step(running, current):
        key_block, value_block, first_row = current
        run_max, denominator, weighted = running
        key_pos = positions(order_flat, first_row, step_rows, block_rows)
        allowed = (query_pos[:, None] >= key_pos[None, :])[None]
        scores = (
            jnp.einsum("hqd,khd->hqk", query_heads, key_block, preferred_element_type=jnp.float32)
            * head_scale
        )
        scores = jnp.where(allowed, scores, MASKED)
        new_max = jnp.maximum(run_max, jnp.max(scores, axis=-1))
        exponent = jnp.where(allowed, jnp.exp(scores - new_max[..., None]), 0.0)
        rescale = jnp.exp(run_max - new_max)
        denominator = denominator * rescale + jnp.sum(exponent, axis=-1)
        weighted = weighted * rescale[..., None] + jnp.einsum(
            "hqk,khd->hqd",
            exponent.astype(jnp.bfloat16),
            value_block,
            preferred_element_type=jnp.float32,
        )
        return ((new_max, denominator, weighted), None)

    run_max, denominator, weighted = lax.scan(absorb_step, running, blocks)[0]
    log_total = run_max + jnp.log(denominator)
    attended = from_heads(weighted / denominator[..., None])
    attention_lower = attended.astype(jnp.bfloat16)
    residual_stream = (
        input_to_layer
        + jnp.dot(attention_lower, attention_out_weight, preferred_element_type=jnp.float32)
        + attention_out_bias.astype(jnp.float32)
    )
    second_normalized = layer_norm(
        residual_stream, second_gain.astype(jnp.float32), second_shift.astype(jnp.float32)
    ).astype(jnp.bfloat16)
    hidden_before_gelu = jnp.dot(
        second_normalized, widen_weight, preferred_element_type=jnp.float32
    ) + widen_bias.astype(jnp.float32)
    hidden_units = gelu_tanh(hidden_before_gelu).astype(jnp.bfloat16)
    result = (
        residual_stream
        + jnp.dot(hidden_units, narrow_weight, preferred_element_type=jnp.float32)
        + narrow_bias.astype(jnp.float32)
    )
    return (
        result,
        (
            input_to_layer,
            first_normalized,
            queries,
            key_low,
            values,
            attended,
            log_total,
            attention_lower,
            residual_stream,
            second_normalized,
            hidden_before_gelu,
            hidden_units,
        ),
    )


def backward_layer(out_grad, stored_items, weights, query_pos, order_flat, block_rows):
    (
        first_gain,
        first_shift,
        query_key_value_weight,
        input_bias,
        attention_out_weight,
        attention_out_bias,
        second_gain,
        second_shift,
        widen_weight,
        widen_bias,
        narrow_weight,
        narrow_bias,
    ) = weights
    (
        input_to_layer,
        first_normalized,
        queries,
        key_low,
        values,
        attended,
        log_total,
        attention_lower,
        residual_stream,
        second_normalized,
        hidden_before_gelu,
        hidden_units,
    ) = stored_items
    row_count, model_width = input_to_layer.shape
    head_scale = HD ** (-0.5)
    out_low = out_grad.astype(jnp.bfloat16)
    hidden_grad = jnp.dot(out_low, narrow_weight.T, preferred_element_type=jnp.float32)
    pre_grad = jax.vjp(gelu_tanh, hidden_before_gelu)[1](hidden_grad)[0].astype(jnp.bfloat16)
    normed_grad = jnp.dot(pre_grad, widen_weight.T, preferred_element_type=jnp.float32)
    resid_part, second_gain_grad, second_shift_grad = jax.vjp(
        layer_norm,
        residual_stream,
        second_gain.astype(jnp.float32),
        second_shift.astype(jnp.float32),
    )[1](normed_grad)
    resid_grad = out_grad + resid_part
    resid_low = resid_grad.astype(jnp.bfloat16)
    att_grad = jnp.dot(
        resid_low, attention_out_weight.T, preferred_element_type=jnp.float32
    ).astype(jnp.bfloat16)
    query_heads = to_heads(queries)
    grad_heads = to_heads(att_grad)
    correction = jnp.sum(
        att_grad.astype(jnp.float32).reshape(row_count, HEADS, HD)
        * attended.reshape(row_count, HEADS, HD),
        axis=-1,
    ).T
    key_value = jnp.concatenate([key_low, values], axis=1)
    query_init = jnp.zeros((HEADS, row_count, HD), jnp.float32)

    def query_terms(key_block, value_block, first_row, step_rows):
        key_pos = positions(order_flat, first_row, step_rows, block_rows)
        allowed = (query_pos[:, None] >= key_pos[None, :])[None]
        scores = (
            jnp.einsum("hqd,khd->hqk", query_heads, key_block, preferred_element_type=jnp.float32)
            * head_scale
        )
        probability = jnp.where(allowed, jnp.exp(scores - log_total[..., None]), 0.0)
        prob_grad = jnp.einsum(
            "hqd,khd->hqk", grad_heads, value_block, preferred_element_type=jnp.float32
        )
        score_grad = (probability * (prob_grad - correction[..., None])).astype(jnp.bfloat16)
        return (probability, score_grad)

    query_acc = query_init
    blocks, step_rows = split_pairs(
        lax.all_gather(key_value, ("ctx", "shard"), axis=0, tiled=True), model_width
    )

    def reach_step(query_acc, current):
        key_block, value_block, first_row = current
        probability, score_grad = query_terms(key_block, value_block, first_row, step_rows)
        return (
            query_acc
            + jnp.einsum("hqk,khd->hqd", score_grad, key_block, preferred_element_type=jnp.float32)
            * head_scale,
            None,
        )

    query_acc = lax.scan(reach_step, query_acc, blocks)[0]
    stats = jnp.concatenate([log_total.T, correction.T], axis=1)
    high_part = stats.astype(jnp.bfloat16)
    rest_part = stats - high_part.astype(jnp.float32)
    middle_part = rest_part.astype(jnp.bfloat16)
    tail_part = (rest_part - middle_part.astype(jnp.float32)).astype(jnp.bfloat16)
    packed_stats = jnp.concatenate([high_part, middle_part, tail_part], axis=1)
    key_heads = to_heads(key_low)
    value_heads = to_heads(values)
    running = (query_init, query_init)
    side_rows = lax.all_gather(
        jnp.concatenate([queries, att_grad], axis=1), ("ctx", "shard"), axis=0, tiled=True
    )
    packed_rows = lax.all_gather(packed_stats, ("ctx", "shard"), axis=0, tiled=True)
    piece_rows = side_rows.shape[0]
    toward_step_rows = block_size(piece_rows)
    step_count = piece_rows // toward_step_rows
    widened = packed_rows.astype(jnp.float32)
    stat_rows = (
        widened[:, : 2 * HEADS] + widened[:, 2 * HEADS : 4 * HEADS] + widened[:, 4 * HEADS :]
    )
    query_blocks = side_rows[:, :model_width].reshape(step_count, toward_step_rows, HEADS, HD)
    grad_blocks = side_rows[:, model_width:].reshape(step_count, toward_step_rows, HEADS, HD)
    stat_blocks = stat_rows.reshape(step_count, toward_step_rows, 2 * HEADS)
    first_rows = toward_step_rows * jnp.arange(step_count, dtype=jnp.int32)

    def toward_step(running, current):
        key_acc, value_acc = running
        query_block, grad_block, stat_block, first_row = current
        query_places = positions(order_flat, first_row, toward_step_rows, block_rows)
        allowed = (query_places[:, None] >= query_pos[None, :])[None]
        scores = (
            jnp.einsum("qhd,hkd->hqk", query_block, key_heads, preferred_element_type=jnp.float32)
            * head_scale
        )
        probability = jnp.where(allowed, jnp.exp(scores - stat_block[:, :HEADS].T[..., None]), 0.0)
        prob_grad = jnp.einsum(
            "qhd,hkd->hqk", grad_block, value_heads, preferred_element_type=jnp.float32
        )
        score_grad = (probability * (prob_grad - stat_block[:, HEADS:].T[..., None])).astype(
            jnp.bfloat16
        )
        key_acc = (
            key_acc
            + jnp.einsum(
                "hqk,qhd->hkd", score_grad, query_block, preferred_element_type=jnp.float32
            )
            * head_scale
        )
        value_acc = value_acc + jnp.einsum(
            "hqk,qhd->hkd",
            probability.astype(jnp.bfloat16),
            grad_block,
            preferred_element_type=jnp.float32,
        )
        return ((key_acc, value_acc), None)

    key_acc, value_acc = lax.scan(
        toward_step, running, (query_blocks, grad_blocks, stat_blocks, first_rows)
    )[0]
    key_grad_low = from_heads(key_acc).astype(jnp.bfloat16)
    value_grad_low = from_heads(value_acc).astype(jnp.bfloat16)
    query_grad_low = from_heads(query_acc).astype(jnp.bfloat16)
    triple = jnp.concatenate([query_grad_low, key_grad_low, value_grad_low], axis=1)
    input_norm_grad = jnp.dot(triple, query_key_value_weight.T, preferred_element_type=jnp.float32)
    input_part, first_gain_grad, first_shift_grad = jax.vjp(
        layer_norm, input_to_layer, first_gain.astype(jnp.float32), first_shift.astype(jnp.float32)
    )[1](input_norm_grad)
    input_grad = resid_grad + input_part
    return (
        input_grad,
        (
            first_normalized,
            triple,
            attention_lower,
            resid_low,
            second_normalized,
            pre_grad,
            hidden_units,
            out_low,
            first_gain_grad,
            first_shift_grad,
            second_gain_grad,
            second_shift_grad,
        ),
    )


def on_device(
    tokens,
    block_order,
    cotangent,
    first_gain,
    first_shift,
    query_key_value_weight,
    input_bias,
    attention_out_weight,
    attention_out_bias,
    second_gain,
    second_shift,
    widen_weight,
    widen_bias,
    narrow_weight,
    narrow_bias,
):
    section_index = lax.axis_index("section")
    upper_section = section_index == 1
    gathered = (
        lax.all_gather(first_gain, "shard", axis=1, tiled=True),
        lax.all_gather(first_shift, "shard", axis=1, tiled=True),
        lax.all_gather(query_key_value_weight, "shard", axis=1, tiled=True),
        lax.all_gather(input_bias, "shard", axis=1, tiled=True),
        lax.all_gather(attention_out_weight, "shard", axis=1, tiled=True),
        lax.all_gather(attention_out_bias, "shard", axis=1, tiled=True),
        lax.all_gather(second_gain, "shard", axis=1, tiled=True),
        lax.all_gather(second_shift, "shard", axis=1, tiled=True),
        lax.all_gather(widen_weight, "shard", axis=1, tiled=True),
        lax.all_gather(widen_bias, "shard", axis=1, tiled=True),
        lax.all_gather(narrow_weight, "shard", axis=1, tiled=True),
        lax.all_gather(narrow_bias, "shard", axis=1, tiled=True),
    )
    weights = tuple((member[0] for member in gathered))
    seq_count, row_count, model_width = tokens.shape
    block_rows = row_count // 2
    order_flat = block_order.reshape(-1)
    query_pos = positions(
        order_flat, lax.axis_index(("ctx", "shard")) * row_count, row_count, block_rows
    )
    coming = jnp.zeros((row_count, model_width), jnp.float32)
    results = []
    stored = []
    for step_index in range(seq_count + 1):
        input_to_layer = jnp.where(
            upper_section, coming, tokens[min(step_index, seq_count - 1)].astype(jnp.float32)
        )
        result, stored_items = forward_layer(
            input_to_layer, weights, query_pos, order_flat, block_rows
        )
        results.append(result)
        stored.append(stored_items)
        if step_index < seq_count:
            coming = from_behind(result.astype(jnp.bfloat16), "section", 1).astype(result.dtype)
    grad_coming = jnp.zeros((row_count, model_width), jnp.float32)
    input_grads = []
    saved = []
    for step_index in range(seq_count + 1):
        seed_grad = cotangent[max(seq_count - 1 - step_index, 0)].astype(jnp.float32)
        out_grad = jnp.where(upper_section, seed_grad, grad_coming)
        input_grad, saved_items = backward_layer(
            out_grad, stored[seq_count - step_index], weights, query_pos, order_flat, block_rows
        )
        input_grads.append(input_grad)
        saved.append(saved_items)
        if step_index < seq_count:
            grad_coming = from_behind(input_grad.astype(jnp.bfloat16), "section", -1).astype(
                input_grad.dtype
            )
    layer_out = jnp.stack(
        [
            jnp.where(upper_section, results[seq_index + 1], results[seq_index])
            for seq_index in range(seq_count)
        ]
    )[None]
    d_in = jnp.stack(
        [
            jnp.where(
                upper_section,
                input_grads[seq_count - 1 - seq_index],
                input_grads[seq_count - seq_index],
            )
            for seq_index in range(seq_count)
        ]
    )[None]
    real_rounds = [
        tuple(
            (
                jnp.where(upper_section, saved[seq_index][item_pos], saved[seq_index + 1][item_pos])
                for item_pos in range(12)
            )
        )
        for seq_index in range(seq_count)
    ]

    def joined(item_pos):
        return jnp.concatenate([member[item_pos] for member in real_rounds], axis=0)

    def added(item_pos):
        return jnp.sum(jnp.stack([member[item_pos] for member in real_rounds]), axis=0)

    arrange = partial(reorder, groups=lax.axis_size("shard"))
    normed_all = joined(0)
    triple_all = joined(1)
    att_all = joined(2)
    resid_all = joined(3)
    normed_two_all = joined(4)
    pre_all = joined(5)
    hidden_all = joined(6)
    out_all = joined(7)
    triple_sums = jnp.sum(triple_all.astype(jnp.float32), axis=0)
    grads = [
        arrange(added(8), 0),
        arrange(added(9), 0),
        jnp.einsum(
            "tc,te->ce", arrange(normed_all, 1), triple_all, preferred_element_type=jnp.float32
        ),
        arrange(jnp.concatenate([triple_sums[:model_width], triple_sums[2 * model_width :]]), 0),
        jnp.einsum("tc,te->ce", arrange(att_all, 1), resid_all, preferred_element_type=jnp.float32),
        arrange(jnp.sum(resid_all.astype(jnp.float32), axis=0), 0),
        arrange(added(10), 0),
        arrange(added(11), 0),
        jnp.einsum(
            "tc,te->ce", arrange(normed_two_all, 1), pre_all, preferred_element_type=jnp.float32
        ),
        arrange(jnp.sum(pre_all.astype(jnp.float32), axis=0), 0),
        jnp.einsum(
            "tc,te->ce", arrange(hidden_all, 1), out_all, preferred_element_type=jnp.float32
        ),
        arrange(jnp.sum(out_all.astype(jnp.float32), axis=0), 0),
    ]
    spread = (
        lax.psum_scatter(grads[0], ("ctx", "shard"), scatter_dimension=0, tiled=True),
        lax.psum_scatter(grads[1], ("ctx", "shard"), scatter_dimension=0, tiled=True),
        lax.psum_scatter(grads[2], ("ctx", "shard"), scatter_dimension=0, tiled=True),
        lax.psum_scatter(grads[3], ("ctx", "shard"), scatter_dimension=0, tiled=True),
        lax.psum_scatter(grads[4], ("ctx", "shard"), scatter_dimension=0, tiled=True),
        lax.psum_scatter(grads[5], ("ctx", "shard"), scatter_dimension=0, tiled=True),
        lax.psum_scatter(grads[6], ("ctx", "shard"), scatter_dimension=0, tiled=True),
        lax.psum_scatter(grads[7], ("ctx", "shard"), scatter_dimension=0, tiled=True),
        lax.psum_scatter(grads[8], ("ctx", "shard"), scatter_dimension=0, tiled=True),
        lax.psum_scatter(grads[9], ("ctx", "shard"), scatter_dimension=0, tiled=True),
        lax.psum_scatter(grads[10], ("ctx", "shard"), scatter_dimension=0, tiled=True),
        lax.psum_scatter(grads[11], ("ctx", "shard"), scatter_dimension=0, tiled=True),
    )
    totals = (
        lax.all_gather(spread[0].astype(jnp.bfloat16), "ctx", axis=0, tiled=True).astype(
            jnp.float32
        ),
        lax.all_gather(spread[1].astype(jnp.bfloat16), "ctx", axis=0, tiled=True).astype(
            jnp.float32
        ),
        lax.all_gather(spread[2].astype(jnp.bfloat16), "ctx", axis=0, tiled=True).astype(
            jnp.float32
        ),
        lax.all_gather(spread[3].astype(jnp.bfloat16), "ctx", axis=0, tiled=True).astype(
            jnp.float32
        ),
        lax.all_gather(spread[4].astype(jnp.bfloat16), "ctx", axis=0, tiled=True).astype(
            jnp.float32
        ),
        lax.all_gather(spread[5].astype(jnp.bfloat16), "ctx", axis=0, tiled=True).astype(
            jnp.float32
        ),
        lax.all_gather(spread[6].astype(jnp.bfloat16), "ctx", axis=0, tiled=True).astype(
            jnp.float32
        ),
        lax.all_gather(spread[7].astype(jnp.bfloat16), "ctx", axis=0, tiled=True).astype(
            jnp.float32
        ),
        lax.all_gather(spread[8].astype(jnp.bfloat16), "ctx", axis=0, tiled=True).astype(
            jnp.float32
        ),
        lax.all_gather(spread[9].astype(jnp.bfloat16), "ctx", axis=0, tiled=True).astype(
            jnp.float32
        ),
        lax.all_gather(spread[10].astype(jnp.bfloat16), "ctx", axis=0, tiled=True).astype(
            jnp.float32
        ),
        lax.all_gather(spread[11].astype(jnp.bfloat16), "ctx", axis=0, tiled=True).astype(
            jnp.float32
        ),
    )
    return (
        layer_out,
        d_in,
        totals[0][None],
        totals[1][None],
        totals[2][None],
        totals[3][None],
        totals[4][None],
        totals[5][None],
        totals[6][None],
        totals[7][None],
        totals[8][None],
        totals[9][None],
        totals[10][None],
        totals[11][None],
    )


def solution(mesh):
    in_specs = (
        P(None, ("ctx", "shard"), None),
        P(),
        P(None, ("ctx", "shard"), None),
        P("section", "shard"),
        P("section", "shard"),
        P("section", "shard", None),
        P("section", "shard"),
        P("section", "shard", None),
        P("section", "shard"),
        P("section", "shard"),
        P("section", "shard"),
        P("section", "shard", None),
        P("section", "shard"),
        P("section", "shard", None),
        P("section", "shard"),
    )
    out_specs = (
        P("section", None, ("ctx", "shard"), None),
        P("section", None, ("ctx", "shard"), None),
        P("section", "shard"),
        P("section", "shard"),
        P("section", "shard", None),
        P("section", "shard"),
        P("section", "shard", None),
        P("section", "shard"),
        P("section", "shard"),
        P("section", "shard"),
        P("section", "shard", None),
        P("section", "shard"),
        P("section", "shard", None),
        P("section", "shard"),
    )
    return jax.shard_map(
        on_device, mesh=mesh, in_specs=in_specs, out_specs=out_specs, check_vma=False
    )
```

profile of v0, /device:TPU:0, one launch (start us, length us, event | category | flops | bytes accessed | tf_op | source)
XLA Modules:
  0.0 4119.4 jit_solution(10350184128726578473)
XLA Ops:
  18.6 40.9 all-reduce.31
  62.0 164.8 %all-gather.17.cloned.1.call-done = bf16[1,1600,4800]{2,1,0:T(8,128)(2,1)} async-done(((bf16[1,200,4800]{2,1,0:T(8,128)(2,1)}), bf16[1,1600,4800]{2,1,0:T(8,128)(2,1)}) %all-gather.17.cloned.1.call-update) | async-done | bytes 15360016 | tf_op jit(solution)/shard_map/all_gather | solution.py:377
  226.8 7.9 fusion.37
  241.5 56.8 %all-gather.19.cloned.1.call-done = bf16[1024,3200]{1,0:T(8,128)(2,1)} async-done(((bf16[64,3200]{1,0:T(8,128)(2,1)}), bf16[1024,3200]{1,0:T(8,128)(2,1)}) %all-gather.19.cloned.1.call-update) | async-done | bytes 6553616 | tf_op jit(solution)/shard_map/all_gather | solution.py:114
  325.9 60.4 %all-gather.21.cloned.1.call-done = bf16[1,1600,1600]{2,1,0:T(8,128)(2,1)} async-done(((bf16[1,200,1600]{2,1,0:T(8,128)(2,1)}), bf16[1,1600,1600]{2,1,0:T(8,128)(2,1)}) %all-gather.21.cloned.1.call-update) | async-done | bytes 5120016 | tf_op jit(solution)/shard_map/all_gather | solution.py:379
  390.2 388.3 %all-gather.23.cloned.1.call-done = bf16[1,1600,6400]{2,1,0:T(8,128)(2,1)} async-done(((bf16[1,200,6400]{2,1,0:T(8,128)(2,1)}), bf16[1,1600,6400]{2,1,0:T(8,128)(2,1)}) %all-gather.23.cloned.1.call-update) | async-done | bytes 20480016 | tf_op jit(solution)/shard_map/all_gather | solution.py:383
  778.5 8.9 fusion.39
  787.4 400.4 %all-gather.25.cloned.1.call-done = bf16[1,6400,1600]{2,1,0:T(8,128)(2,1)} async-done(((bf16[1,800,1600]{2,1,0:T(8,128)(2,1)}), bf16[1,6400,1600]{2,1,0:T(8,128)(2,1)}) %all-gather.25.cloned.1.call-update) | async-done | bytes 20480016 | tf_op jit(solution)/shard_map/all_gather | solution.py:385
  1187.8 9.9 fusion.424
  1206.9 7.8 fusion.35
  1217.2 63.5 %all-gather.27.cloned.1.call-done = bf16[1024,3200]{1,0:T(8,128)(2,1)} async-done(((bf16[64,3200]{1,0:T(8,128)(2,1)}), bf16[1024,3200]{1,0:T(8,128)(2,1)}) %all-gather.27.cloned.1.call-update) | async-done | bytes 6553616 | tf_op jit(solution)/shard_map/all_gather | solution.py:114
  1288.3 14.1 copy.293
  1327.5 9.2 fusion.42
  1350.2 7.8 fusion.33
  1360.3 62.6 %all-gather.29.cloned.1.call-done = bf16[1024,3200]{1,0:T(8,128)(2,1)} async-done(((bf16[64,3200]{1,0:T(8,128)(2,1)}), bf16[1024,3200]{1,0:T(8,128)(2,1)}) %all-gather.29.cloned.1.call-update) | async-done | bytes 6553616 | tf_op jit(solution)/shard_map/all_gather | solution.py:114
  1457.4 11.8 broadcast_select_fusion.1
  1469.2 11.9 fusion.203
  1481.1 12.4 multiply_reduce_fusion.5
  1505.1 8.0 fusion.261
  1514.7 38.5 all_gather.118
  1554.9 10.7 all-gather.31.cloned.1.call-done
  1590.2 8.5 fusion.264
  1604.0 11.0 multiply_reduce_fusion.8
  1617.5 8.0 collective-permute-done.2
  1625.5 11.0 fusion.196
  1636.5 11.2 multiply_reduce_fusion.4
  1660.8 8.8 fusion.260
  1672.1 38.2 all_gather.120
  1713.2 8.3 all-gather.33.cloned.1.call-done
  1746.1 8.5 fusion.263
  1760.8 11.0 multiply_reduce_fusion.7
  1782.7 11.7 broadcast_select_fusion.3
  1794.5 11.1 multiply_reduce_fusion.3
  1811.2 16.2 fusion.265
  1827.4 898.3 %fusion.2 = f32[104,6400]{1,0:T(8,128)} fusion(f32[1600,6400]{1,0:T(8,128)} %fusion.265), kind=kCustom, calls=%all-reduce-scatter.2 | all-reduce-scatter fusion | flops 10649601 | bytes 43622912
  2730.0 17.2 collective-permute-done.7
  2747.2 11.4 concatenate.109
  2767.1 16.8 fusion.320
  2793.3 10.0 fusion.259
  2804.8 36.1 all_gather.122
  2849.1 7.8 fusion.414
  2892.1 12.7 fusion.276
  2904.7 1035.2 %fusion.406 = (f32[104,4800]{1,0:T(8,128)}, f32[112,1600]{1,0:T(8,128)}) fusion(f32[1600,4800]{1,0:T(8,128)} %fusion.276, f32[1600,1600]{1,0:T(8,128)} %fusion.321), kind=kCustom, calls=%all-reduce-scatter.3 | all-reduce-scatter fusion | flops 10854402 | bytes 43674112
  3946.8 11.8 collective-permute-done.4
  3958.6 11.6 concatenate.107
  3977.9 10.2 fusion.180
  4000.6 10.9 fusion.405
  4015.5 61.1 %all-reduce.30 = (bf16[1600]{0:T(1024)(128)(2,1)S(1)}, bf16[1600]{0:T(1024)(128)(2,1)S(1)}, bf16[3200]{0:T(1024)(128)(2,1)S(1)}, bf16[1600]{0:T(1024)(128)(2,1)S...) all-reduce(f32[1600]{0:T(1024)S(1)} %reshape.772, ...), channel_id=2, replica_groups=mesh['section'=2,'ctx'=2,'shard'=8] {'ctx','shard'}, use_global_device_ids=true, to_apply=%region_38.39.clone | all-reduce | flops 19200 | bytes 115200
  (775 shorter events, 383.7 us)
Async XLA Ops:
  7.2 219.6 %all-gather.17.cloned.1.call-start = ((), (), s32[]{:S(2)}) async-start(), calls=%async_computation.1 | async-start | bytes 17510400 | tf_op jit(solution)/shard_map/all_gather | solution.py:377
  7.9 290.4 %all-gather.19.cloned.1.call-start = ((), (), s32[]{:S(2)}) async-start(), calls=%async_computation.2 | async-start | bytes 6963200 | tf_op jit(solution)/shard_map/all_gather | solution.py:114
  59.6 1290.6 %copy-start.110 = (f32[1600]{0:T(1024)}, f32[1600]{0:T(1024)S(1)}, u32[]{:S(2)}) copy-start(f32[1600]{0:T(1024)S(1)} %add.759) | copy-start | bytes 19204
  59.7 175.2 %copy-start.121 = (f32[1600]{0:T(1024)}, f32[1600]{0:T(1024)S(1)}, u32[]{:S(2)}) copy-start(f32[1600]{0:T(1024)S(1)} %get-tuple-element.234) | copy-start | bytes 19204
  59.7 175.2 %copy-start.123 = (f32[1600]{0:T(1024)}, f32[1600]{0:T(1024)S(1)}, u32[]{:S(2)}) copy-start(f32[1600]{0:T(1024)S(1)} %get-tuple-element.235) | copy-start | bytes 19204
  60.8 173.9 %copy-start.147 = (f32[64]{0:T(128)}, f32[64]{0:T(128)S(1)}, u32[]{:S(2)}) copy-start(f32[64]{0:T(128)S(1)} %broadcast_multiply_fusion.5) | copy-start | bytes 772
  62.0 172.7 %copy-start.177 = (f32[64]{0:T(128)}, f32[64]{0:T(128)S(1)}, u32[]{:S(2)}) copy-start(f32[64]{0:T(128)S(1)} %multiply_reduce_fusion.20) | copy-start | bytes 772
  62.0 172.7 %copy-start.159 = (f32[64]{0:T(128)}, f32[64]{0:T(128)S(1)}, u32[]{:S(2)}) copy-start(f32[64]{0:T(128)S(1)} %fusion.363) | copy-start | bytes 772
  236.5 149.8 %all-gather.21.cloned.1.call-start = ((), (), s32[]{:S(2)}) async-start(), calls=%async_computation.3 | async-start | bytes 5990400 | tf_op jit(solution)/shard_map/all_gather | solution.py:379
  237.3 541.2 %all-gather.23.cloned.1.call-start = ((), (), s32[]{:S(2)}) async-start(), calls=%async_computation.4 | async-start | bytes 23040000 | tf_op jit(solution)/shard_map/all_gather | solution.py:383
  237.8 950.0 %all-gather.25.cloned.1.call-start = ((), (), s32[]{:S(2)}) async-start(), calls=%async_computation.5 | async-start | bytes 23961600 | tf_op jit(solution)/shard_map/all_gather | solution.py:385
  238.4 1042.3 %all-gather.27.cloned.1.call-start = ((), (), s32[]{:S(2)}) async-start(), calls=%async_computation.6 | async-start | bytes 6963200 | tf_op jit(solution)/shard_map/all_gather | solution.py:114
  240.1 64.8 %copy-start.171 = (s32[64]{0:T(128)}, s32[64]{0:T(128)S(1)}, u32[]{:S(2)}) copy-start(s32[64]{0:T(128)S(1)} %fusion.362) | copy-start | bytes 772
  322.4 63.9 %copy-start.125 = (f32[1600]{0:T(1024)S(1)}, f32[1600]{0:T(1024)}, u32[]{:S(2)}) copy-start(f32[1600]{0:T(1024)} %add.760) | copy-start | bytes 19204
  325.9 64.3 %copy-start.103 = (bf16[64,25,64]{0,2,1:T(8,128)(2,1)}, bf16[64,25,64]{0,2,1:T(8,128)(2,1)S(1)}, u32[]{:S(2)}) copy-start(bf16[64,25,64]{0,2,1:T(8,128)(2,1)S(1)} %get-tuple-element.405) | copy-start | bytes 614404
  390.0 936.6 %copy-start.10 = (f32[64,1600]{1,0:T(8,128)}, f32[64,1600]{1,0:T(8,128)S(1)}, u32[]{:S(2)}) copy-start(f32[64,1600]{1,0:T(8,128)S(1)} %get-tuple-element.408) | copy-start | bytes 1228804
  390.0 936.5 %copy-start.153 = (f32[64]{0:T(128)}, f32[64]{0:T(128)S(1)}, u32[]{:S(2)}) copy-start(f32[64]{0:T(128)S(1)} %broadcast_multiply_fusion.4) | copy-start | bytes 772
  390.2 388.3 %copy-start.179 = (f32[64]{0:T(128)}, f32[64]{0:T(128)S(1)}, u32[]{:S(2)}) copy-start(f32[64]{0:T(128)S(1)} %multiply_reduce_fusion.19) | copy-start | bytes 772
  390.2 936.3 %copy-start.157 = (f32[64]{0:T(128)}, f32[64]{0:T(128)S(1)}, u32[]{:S(2)}) copy-start(f32[64]{0:T(128)S(1)} %fusion.364) | copy-start | bytes 772
  390.2 797.6 %copy-start.128 = (f32[1600]{0:T(1024)S(1)}, f32[1600]{0:T(1024)}, u32[]{:S(2)}) copy-start(f32[1600]{0:T(1024)} %add.763) | copy-start | bytes 19204
  787.4 418.6 %copy-start.148 = (f32[64]{0:T(128)S(1)}, f32[64]{0:T(128)}, u32[]{:S(2)}) copy-start(f32[64]{0:T(128)} %copy-done.147) | copy-start | bytes 772
  787.4 418.6 %copy-start.160 = (f32[64]{0:T(128)S(1)}, f32[64]{0:T(128)}, u32[]{:S(2)}) copy-start(f32[64]{0:T(128)} %copy-done.159) | copy-start | bytes 772
  1197.7 7.9 collective-permute-start
  1205.6 116.9 %copy-start.23 = (bf16[64,1600]{1,0:T(8,128)(2,1)}, bf16[64,1600]{1,0:T(8,128)(2,1)S(1)}, u32[]{:S(2)}) copy-start(bf16[64,1600]{1,0:T(8,128)(2,1)S(1)} %collective-permute-done) | copy-start | bytes 614404
  1214.9 73.4 %copy-start.70 = (bf16[64,1600]{1,0:T(8,128)(2,1)}, bf16[64,1600]{1,0:T(8,128)(2,1)S(1)}, u32[]{:S(2)}) copy-start(bf16[64,1600]{1,0:T(8,128)(2,1)S(1)} %get-tuple-element.365) | copy-start | bytes 614404
  1214.9 73.4 %copy-start.72 = (bf16[64,1600]{1,0:T(8,128)(2,1)}, bf16[64,1600]{1,0:T(8,128)(2,1)S(1)}, u32[]{:S(2)}) copy-start(bf16[64,1600]{1,0:T(8,128)(2,1)S(1)} %get-tuple-element.364) | copy-start | bytes 614404
  1215.0 73.3 %copy-start.79 = (bf16[64,1600]{1,0:T(8,128)(2,1)}, bf16[64,1600]{1,0:T(8,128)(2,1)S(1)}, u32[]{:S(2)}) copy-start(bf16[64,1600]{1,0:T(8,128)(2,1)S(1)} %slice.366) | copy-start | bytes 614404
  1215.9 207.0 %all-gather.29.cloned.1.call-start = ((), (), s32[]{:S(2)}) async-start(), calls=%async_computation.7 | async-start | bytes 6963200 | tf_op jit(solution)/shard_map/all_gather | solution.py:114
  1341.5 8.3 collective-permute-start.1
  1358.1 72.5 %copy-start.75 = (bf16[64,1600]{1,0:T(8,128)(2,1)}, bf16[64,1600]{1,0:T(8,128)(2,1)S(1)}, u32[]{:S(2)}) copy-start(bf16[64,1600]{1,0:T(8,128)(2,1)S(1)} %get-tuple-element.362) | copy-start | bytes 614404
  1359.8 205.7 %all-gather.31.cloned.1.call-start = ((), (), s32[]{:S(2)}) async-start(), calls=%async_computation.8 | async-start | bytes 6963200 | tf_op jit(solution)/shard_map/all_gather | solution.py:277
  1493.8 121.6 %copy-start.170 = (f32[64]{0:T(128)}, f32[64]{0:T(128)S(1)}, u32[]{:S(2)}) copy-start(f32[64]{0:T(128)S(1)} %negate_multiply_fusion.5) | copy-start | bytes 772
  1497.3 224.2 %all-gather.33.cloned.1.call-start = ((), (), s32[]{:S(2)}) async-start(), calls=%async_computation.9 | async-start | bytes 6963200 | tf_op jit(solution)/shard_map/all_gather | solution.py:277
  1497.4 92.7 %copy-start.131 = (pred[1024,64]{0,1:T(8,128)(4,1)}, pred[1024,64]{0,1:T(8,128)(4,1)S(1)}, u32[]{:S(2)}) copy-start(pred[1024,64]{0,1:T(8,128)(4,1)S(1)} %broadcast_compare_fusion) | copy-start | bytes 196612
  1616.1 9.4 collective-permute-start.2
  1652.3 1196.8 %all-gather.35.cloned.1.call-start = ((), (), s32[]{:S(2)}) async-start(), calls=%async_computation.10 | async-start | bytes 6963200 | tf_op jit(solution)/shard_map/all_gather | solution.py:277
  1773.1 9.6 collective-permute-start.3
  1811.1 2181.8 %all-gather.41.cloned.1.call-start = ((), (), s32[]{:S(2)}) async-start(), calls=%async_computation.14 | async-start | bytes 3993600 | tf_op jit(solution)/shard_map/all_gather | solution.py:525
  1827.4 901.3 %copy-start.173 = (u32[32]{0:T(128)S(1)}, u32[32]{0:T(128)}, u32[]{:S(2)}) copy-start(u32[32]{0:T(128)} %constant.443) | copy-start | bytes 388
  2727.3 19.8 collective-permute-start.7
  2761.3 1236.2 %reduce-scatter.8.cloned.1.call-start = ((), (), s32[]{:S(2)}) async-start(), calls=%async_computation.11 | async-start | bytes 45260800 | tf_op jit(solution)/shard_map/reduce_scatter | solution.py:497
  2783.9 1320.0 %all-gather.39.cloned.1.call-start = ((), (), s32[]{:S(2)}) async-start(), calls=%async_computation.13 | async-start | bytes 3035136 | tf_op jit(solution)/shard_map/all_gather | solution.py:507
  3941.4 17.2 collective-permute-start.4
  3972.6 135.5 %all-gather.37.cloned.1.call-start = ((), (), s32[]{:S(2)}) async-start(), calls=%async_computation.12 | async-start | bytes 3993600 | tf_op jit(solution)/shard_map/all_gather | solution.py:531
  4011.6 74.4 %copy-start.31 = (f32[64,1600]{1,0:T(8,128)S(1)}, f32[64,1600]{1,0:T(8,128)}, u32[]{:S(2)}) copy-start(f32[64,1600]{1,0:T(8,128)} %copy-done.29) | copy-start | bytes 1228804
  4011.6 74.4 %copy-start.44 = (f32[64,1600]{1,0:T(8,128)S(1)}, f32[64,1600]{1,0:T(8,128)}, u32[]{:S(2)}) copy-start(f32[64,1600]{1,0:T(8,128)} %copy-done.43) | copy-start | bytes 1228804
  4082.5 9.6 collective-permute-start.6
  4084.1 10.3 collective-permute-start.5
  (174 other events, 1436.7 us)
Sparse Core Ops, SparseCore 0:
  10.2 216.5 all-gather.16
  236.7 61.5 all-gather.18
  300.5 85.8 all-gather.20
  387.7 390.7 all-gather.22
  779.9 407.8 all-gather.24
  1216.1 64.5 all-gather.26
  1359.9 62.9 all-gather.28
  1497.4 68.1 all-gather.30
  1652.4 69.0 all-gather.32
  1811.2 148.0 all-gather.34
  2761.4 11.4 all-gather.40
  2784.0 814.6 reduce-scatter.7
  3972.7 8.8 all-gather.38
  4000.6 9.5 all-gather.36
where the time goes:
time: 4130 us; the launch traced here: 4120 us
  blocking collectives  2150 us (52%)
  waiting for transfers between devices  1270 us (31%)
  matrix products  349 us (8%)
  local copies, waits for them, and re-layouts  243 us (6%)
  other arithmetic  61.4 us (1%)
    unnamed x5, blocking collectives  2040 us
    all_gather x1, waiting for transfers between devices, on_device(): lax.all_gather(narrow_weight, 'shard', axis=1, tiled=True)  400 us
    all_gather x1, waiting for transfers between devices, on_device(): lax.all_gather(widen_weight, 'shard', axis=1, tiled=True)  388 us
    all_gather x3, waiting for transfers between devices, forward_layer(): lax.all_gather(jnp.concatenate([key_low, values], axis=1), ('ctx', 'shard...  183 us
    all_gather x1, waiting for transfers between devices, on_device(): lax.all_gather(query_key_value_weight, 'shard', axis=1, tiled=True)  165 us
    all_gather x3, blocking collectives, backward_layer(): lax.all_gather(packed_stats, ('ctx', 'shard'), axis=0, tiled=True)  113 us
  transfers between devices with their start and end apart: 22, of which 16 were waited for; matrix products, arithmetic and copies ran while one was open for 55% of the time, Pallas kernels for 0%

commit v1 on v0

v1 whole, which is shorter than its diff:
```python
import functools

import jax
import jax.numpy as jnp
from jax import lax
from jax.experimental import pallas as pl
from jax.experimental.pallas import tpu as pltpu
from jax.sharding import PartitionSpec as P

HEADS = 25
HD = 64
EPSILON = 1e-05
MASKED = -1e30
LOG2E = 1.4426950408889634
GELU_A = 0.7978845608028654
GELU_B = 0.044715
MESH = pl.DeviceIdType.MESH
F32 = jnp.float32
BF16 = jnp.bfloat16
VMEM_SPEC = pl.BlockSpec(memory_space=pltpu.VMEM)
ANY_SPEC = pl.BlockSpec(memory_space=pl.ANY)
DMA = pltpu.SemaphoreType.DMA
VMEM_LIMIT = 56 * 2**20
HALVES = 2


def params(collective_id=None):
    if collective_id is None:
        return pltpu.CompilerParams(vmem_limit_bytes=VMEM_LIMIT)
    return pltpu.CompilerParams(
        collective_id=collective_id, has_side_effects=True, vmem_limit_bytes=VMEM_LIMIT
    )


def remote(src, dst, send_sem, recv_sem, device):
    return pltpu.make_async_remote_copy(
        src_ref=src,
        dst_ref=dst,
        send_sem=send_sem,
        recv_sem=recv_sem,
        device_id=device,
        device_id_type=MESH,
    )


class Place:
    def __init__(self, n):
        self.s = lax.axis_index("section")
        self.c = lax.axis_index("ctx")
        self.h = lax.axis_index("shard")
        self.n = n
        self.zn = n // 2
        self.y = lax.rem(self.h, 2)
        self.z = lax.div(self.h, 2)
        self.far_y = self.y + self.c - 2 * self.y * self.c

    def dev(self, z, y):
        return (self.s, self.c, z * 2 + y)

    @property
    def pair(self):
        return self.dev(self.z, 1 - self.y)

    @property
    def above(self):
        return self.dev(self.z + 1, self.y)

    @property
    def below(self):
        return self.dev(self.z - 1, self.y)

    @property
    def over(self):
        return (1 - self.s, self.c, self.h)

    @property
    def sibling(self):
        return (self.s, 1 - self.c, self.h)


def greet(p, line=False, spread=False, over=False, sibling=False):
    bar = pltpu.get_barrier_semaphore()
    peers = 0

    def signal(device):
        pl.semaphore_signal(bar, inc=1, device_id=device, device_id_type=MESH)

    if line:
        signal(p.pair)

        @pl.when(p.z < p.zn - 1)
        def _():
            signal(p.above)

        @pl.when(p.z > 0)
        def _():
            signal(p.below)

        peers = 1 + (p.z + p.zn - 1) // p.zn + (2 * p.zn - 2 - p.z) // p.zn
    if spread:
        for dz in range(1, p.zn):
            signal(p.dev(lax.rem(p.z + dz, p.zn), p.far_y))

        @pl.when(p.c == 1)
        def _():
            signal(p.dev(p.z, p.far_y))

        peers = peers + p.zn - 1 + p.c
    if over:
        signal(p.over)
        peers = peers + 1
    if sibling:
        signal(p.sibling)
        peers = peers + 1
    pl.semaphore_wait(bar, peers)


class Gather:
    def __init__(self, p, own_ref, out_ref, ss, rs, ls):
        self.p, self.own_ref, self.out_ref = p, own_ref, out_ref
        self.ss, self.rs, self.ls = ss, rs, ls
        self.hr = own_ref.shape[0] // HALVES

    def blk(self, half, zz, yy):
        row = (half * self.p.n + zz * 2 + yy) * self.hr
        return self.out_ref.at[pl.ds(pl.multiple_of(row, 16), self.hr)]

    def own(self, half):
        return self.own_ref.at[pl.ds(half * self.hr, self.hr)]

    def up(self, t, half, src):
        p = self.p
        sems = (self.ss.at[0, t, half], self.rs.at[0, t, half])
        return remote(src, self.blk(half, p.z - (t - 1), p.y), *sems, p.above)

    def down(self, t, half, src):
        p = self.p
        sems = (self.ss.at[1, t, half], self.rs.at[1, t, half])
        return remote(src, self.blk(half, p.z + (t - 1), p.y), *sems, p.below)

    def across(self, kind, t, half, zz, src):
        p = self.p
        sems = (self.ss.at[2 + kind, t, half], self.rs.at[2 + kind, t, half])
        return remote(src, self.blk(half, zz, p.y), *sems, p.pair)

    def local(self, half):
        p = self.p
        return pltpu.make_async_copy(
            self.own(half), self.blk(half, p.z, p.y), self.ls.at[half]
        )

    def start(self, halves=range(HALVES)):
        p = self.p
        for half in halves:
            src = self.own(half)

            @pl.when(p.z < p.zn - 1)
            def _():
                self.up(1, half, src).start()

            @pl.when(p.z > 0)
            def _():
                self.down(1, half, src).start()

            self.across(0, 0, half, p.z, src).start()
            self.local(half).start()

    def step(self, t, half):
        p = self.p
        z, zn = p.z, p.zn

        @pl.when(z >= t)
        def _():
            block = self.blk(half, z - t, p.y)
            self.up(t, half, block).wait_recv()
            if t < zn - 1:

                @pl.when(z < zn - 1)
                def _():
                    self.up(t + 1, half, block).start()

            self.across(0, t, half, z - t, block).start()

        @pl.when(z <= zn - 1 - t)
        def _():
            block = self.blk(half, z + t, p.y)
            self.down(t, half, block).wait_recv()
            if t < zn - 1:

                @pl.when(z > 0)
                def _():
                    self.down(t + 1, half, block).start()

            self.across(1, t, half, z + t, block).start()

    def steps(self):
        return [
            functools.partial(self.step, t, half)
            for t in range(1, self.p.zn)
            for half in range(HALVES)
        ]

    def finish(self):
        p = self.p
        z, zn = p.z, p.zn
        for half in range(HALVES):
            self.across(0, 0, half, z, self.own(half)).wait_recv()
            for t in range(1, zn):

                @pl.when(z >= t)
                def _():
                    self.across(0, t, half, z - t, self.own(half)).wait_recv()

                @pl.when(z <= zn - 1 - t)
                def _():
                    self.across(1, t, half, z + t, self.own(half)).wait_recv()

        for half in range(HALVES):
            self.local(half).wait()
            self.across(0, 0, half, z, self.own(half)).wait_send()
            for t in range(1, zn):

                @pl.when((z < zn - 1) & (z >= t - 1))
                def _():
                    self.up(t, half, self.own(half)).wait_send()

                @pl.when((z > 0) & (z <= zn - t))
                def _():
                    self.down(t, half, self.own(half)).wait_send()

                @pl.when(z >= t)
                def _():
                    self.across(0, t, half, z - t, self.own(half)).wait_send()

                @pl.when(z <= zn - 1 - t)
                def _():
                    self.across(1, t, half, z + t, self.own(half)).wait_send()


class Scatter:
    def __init__(self, p, part_ref, ybuf, rbuf, sbuf, ss, rs):
        self.p, self.part_ref = p, part_ref
        self.ybuf, self.rbuf, self.sbuf, self.ss, self.rs = ybuf, rbuf, sbuf, ss, rs
        self.hr = ybuf.shape[3]

    def blk(self, half, zz, yy):
        row = (half * self.p.n + zz * 2 + yy) * self.hr
        return self.part_ref.at[pl.ds(pl.multiple_of(row, 16), self.hr)]

    def across(self, k, t, half):
        p = self.p
        zz = p.z + t if k == 0 else p.z - t
        sems = (self.ss.at[k, t, half], self.rs.at[k, t, half])
        return remote(self.blk(half, zz, 1 - p.y), self.ybuf.at[k, t, half], *sems, p.pair)

    def along(self, k, t, half, slot):
        p = self.p
        sems = (self.ss.at[2 + k, t, half], self.rs.at[2 + k, slot, half])
        target = p.above if k == 0 else p.below
        return remote(self.sbuf.at[k, t, half], self.rbuf.at[k, slot, half], *sems, target)

    def ok(self, k, t):
        return self.p.z <= self.p.zn - 1 - t if k == 0 else self.p.z >= t

    def has(self, k):
        return self.p.z > 0 if k == 0 else self.p.z < self.p.zn - 1

    def start(self):
        for t in range(self.p.zn - 1, 0, -1):
            for half in range(HALVES):
                for k in range(2):

                    @pl.when(self.ok(k, t))
                    def _():
                        self.across(k, t, half).start()

        for half in range(HALVES):
            self.across(0, 0, half).start()

    def step(self, t, half, k):
        p = self.p
        zz = p.z + t if k == 0 else p.z - t

        @pl.when(self.ok(k, t))
        def _():
            self.across(k, t, half).wait_recv()
            total = self.blk(half, zz, p.y)[...].astype(F32)
            total = total + self.ybuf[k, t, half].astype(F32)
            if t < p.zn - 1:

                @pl.when(self.has(k))
                def _():
                    self.along(k, t, half, t).wait_recv()
                    more = total + self.rbuf[k, t, half].astype(F32)
                    self.sbuf[k, t, half] = more.astype(BF16)

                @pl.when(jnp.logical_not(self.has(k)))
                def _():
                    self.sbuf[k, t, half] = total.astype(BF16)

            else:
                self.sbuf[k, t, half] = total.astype(BF16)
            self.along(k, t, half, t - 1).start()

    def steps(self):
        return [
            functools.partial(self.step, t, half, k)
            for t in range(self.p.zn - 1, 0, -1)
            for half in range(HALVES)
            for k in range(2)
        ]

    def result(self, half):
        p = self.p
        self.across(0, 0, half).wait_recv()
        for k in range(2):

            @pl.when(self.has(k))
            def _():
                self.along(k, 0, half, 0).wait_recv()

            @pl.when(jnp.logical_not(self.has(k)))
            def _():
                self.rbuf[k, 0, half] = jnp.zeros(self.rbuf.shape[3:], BF16)

        total = self.blk(half, p.z, p.y)[...].astype(F32) + self.ybuf[0, 0, half].astype(F32)
        return total + self.rbuf[0, 0, half].astype(F32) + self.rbuf[1, 0, half].astype(F32)

    def finish(self):
        for half in range(HALVES):
            self.across(0, 0, half).wait_send()
            for t in range(1, self.p.zn):
                for k in range(2):

                    @pl.when(self.ok(k, t))
                    def _():
                        self.across(k, t, half).wait_send()
                        self.along(k, t, half, t - 1).wait_send()


class Spread:
    def __init__(self, p, src, dst, ss, rs, ls):
        self.p, self.src, self.dst, self.ss, self.rs, self.ls = p, src, dst, ss, rs, ls

    def source(self, dz):
        return lax.rem(self.p.z + self.p.zn - dz, self.p.zn) * 2 + self.p.far_y

    def out(self, dz):
        p = self.p
        target = lax.rem(p.z + dz, p.zn) * 2 + p.far_y
        sems = (self.ss.at[0, dz], self.rs.at[0, dz])
        return remote(self.src.at[target], self.dst.at[p.s, p.h], *sems, (p.s, p.c, target))

    def aside(self, dz):
        block = self.dst.at[self.p.s, self.source(dz)]
        return remote(block, block, self.ss.at[1, dz], self.rs.at[1, dz], self.p.sibling)

    def cross(self, dz):
        block = self.dst.at[self.p.s, self.source(dz)]
        return remote(block, block, self.ss.at[2, dz], self.rs.at[2, dz], self.p.over)

    def cross_own(self):
        p = self.p
        sems = (self.ss.at[2, 0], self.rs.at[2, 0])
        return remote(self.src.at[p.h], self.dst.at[p.s, p.h], *sems, p.over)

    def cross_aside(self, dz):
        block = self.dst.at[1 - self.p.s, self.source(dz)]
        return remote(block, block, self.ss.at[3, dz], self.rs.at[3, dz], self.p.sibling)

    def local(self):
        p = self.p
        return pltpu.make_async_copy(self.src.at[p.h], self.dst.at[p.s, p.h], self.ls)

    def start(self):
        @pl.when(self.p.c == 1)
        def _():
            self.out(0).start()

        @pl.when(self.p.c == 0)
        def _():
            self.cross_own().start()

        for dz in range(1, self.p.zn):
            self.out(dz).start()
        self.local().start()

    def arrived(self, dz):
        self.out(dz).wait_recv()
        self.cross(dz).start()
        self.aside(dz).start()

    def crossed(self, dz):
        self.cross(dz).wait_recv()
        self.cross_aside(dz).start()

    def first(self):
        @pl.when(self.p.c == 1)
        def _():
            self.arrived(0)

    def steps(self):
        found = [self.first]
        found += [functools.partial(self.arrived, dz) for dz in range(1, self.p.zn)]
        return found + [functools.partial(self.crossed, dz) for dz in range(self.p.zn)]

    def finish(self):
        self.local().wait()

        @pl.when(self.p.c == 0)
        def _():
            self.aside(0).wait_recv()
            self.cross_own().wait_send()

        @pl.when(self.p.c == 1)
        def _():
            self.out(0).wait_send()
            self.aside(0).wait_send()
            self.cross(0).wait_send()

        for dz in range(self.p.zn):
            if dz:
                self.aside(dz).wait_recv()
                self.aside(dz).wait_send()
                self.out(dz).wait_send()
                self.cross(dz).wait_send()
            self.cross_aside(dz).wait_recv()
            self.cross_aside(dz).wait_send()


class RowSwap:
    def __init__(self, p, src, dst, ss, rs, ls):
        self.p, self.src, self.dst, self.ss, self.rs, self.ls = p, src, dst, ss, rs, ls
        self.split = src.shape[0] % 32 == 0

    def piece(self, which):
        if not self.split:
            return self.src, self.dst.at[which]
        half = self.src.shape[0] // 2
        rows = pl.ds(pl.multiple_of(self.p.c * half, 16), half)
        return self.src.at[rows], self.dst.at[which, rows]

    def cross(self):
        src, dst = self.piece(self.p.s)
        return remote(src, dst, self.ss.at[0], self.rs.at[0], self.p.over)

    def aside(self):
        block = self.piece(1 - self.p.s)[1]
        return remote(block, block, self.ss.at[1], self.rs.at[1], self.p.sibling)

    def local(self):
        return pltpu.make_async_copy(self.src, self.dst.at[self.p.s], self.ls)

    def start(self):
        self.cross().start()
        self.local().start()

    def step(self):
        self.cross().wait_recv()
        if self.split:
            self.aside().start()

    def finish(self):
        self.local().wait()
        self.cross().wait_send()
        if self.split:
            self.aside().wait_recv()
            self.aside().wait_send()


class Cross:
    def __init__(self, p, src, dst, ss, rs, source):
        self.p, self.source = p, source
        self.copy = remote(src, dst, ss, rs, p.over)

    def start(self):
        @pl.when(self.p.s == self.source)
        def _():
            self.copy.start()

    def finish(self):
        @pl.when(self.p.s == self.source)
        def _():
            self.copy.wait_send()

        @pl.when(self.p.s != self.source)
        def _():
            self.copy.wait_recv()


def greet_all(p):
    bar = pltpu.get_barrier_semaphore()
    for a in range(2):
        for b in range(p.n):
            if (a, b) != (0, 0):
                other = (lax.rem(p.s + a, 2), p.c, lax.rem(p.h + b, p.n))
                pl.semaphore_signal(bar, inc=1, device_id=other, device_id_type=MESH)
    pl.semaphore_signal(bar, inc=1, device_id=p.sibling, device_id_type=MESH)
    pl.semaphore_wait(bar, 2 * p.n)


def others(n):
    return [(a, b) for a in range(2) for b in range(n) if (a, b) != (0, 0)]


def start_kernel(n, tok_ref, pack_ref, qkv_ref, out_ref, *refs):
    tok_all, pack_all, qkv_all, out_all = refs[:4]
    g_ss, g_rs, g_ls, p_ss, p_rs, a_ss, a_rs, o_ss, o_rs, l_sem = refs[4:]
    p = Place(n)
    s, c, h = p.s, p.c, p.h
    greet_all(p)

    def pack_copy(a, b):
        target = (lax.rem(s + a, 2), c, lax.rem(h + b, n))
        return remote(pack_ref, pack_all.at[s, h], p_ss.at[a, b], p_rs.at[a, b], target)

    for a, b in others(n):
        pack_copy(a, b).start()
    pack_own = pltpu.make_async_copy(pack_ref, pack_all.at[s, h], l_sem.at[0])
    pack_own.start()
    tokens = Gather(p, tok_ref, tok_all, g_ss, g_rs, g_ls)
    qkv = Spread(p, qkv_ref, qkv_all, a_ss, a_rs, l_sem.at[1])
    out = RowSwap(p, out_ref, out_all, o_ss, o_rs, l_sem.at[2])
    tokens.start()
    qkv.start()
    out.start()
    qkv_steps = qkv.steps()
    for step in tokens.steps():
        step()
        if qkv_steps:
            qkv_steps.pop(0)()
    for step in qkv_steps:
        step()
    out.step()
    pack_own.wait()
    for a, b in others(n):
        pack_copy(a, b).wait_recv()
        pack_copy(a, b).wait_send()
    tokens.finish()
    qkv.finish()
    out.finish()


def start_call(n, tok, pack, qkv, out):
    rows, width = tok.shape
    zn = n // 2
    shapes = [
        jax.ShapeDtypeStruct((n * rows, width), BF16),
        jax.ShapeDtypeStruct((2, n) + pack.shape, BF16),
        jax.ShapeDtypeStruct((2,) + qkv.shape, BF16),
        jax.ShapeDtypeStruct((2,) + out.shape, BF16),
    ]
    return pl.pallas_call(
        functools.partial(start_kernel, n),
        out_shape=shapes,
        in_specs=[ANY_SPEC] * 4,
        out_specs=[ANY_SPEC] * 4,
        scratch_shapes=[
            DMA((4, zn, HALVES)),
            DMA((4, zn, HALVES)),
            DMA((HALVES,)),
            DMA((2, n)),
            DMA((2, n)),
            DMA((4, zn)),
            DMA((4, zn)),
            DMA((2,)),
            DMA((2,)),
            DMA((3,)),
        ],
        compiler_params=params(0),
        name="start",
    )(tok, pack, qkv, out)


def lay_out_kernel(low, share, qkv_ref, widen_ref, out_ref, narrow_ref, *outs):
    qkv_to, widen_to, out_to, narrow_to = outs
    n, padded, hide = widen_to.shape
    width = qkv_ref.shape[1] // 3
    sh = qkv_to.shape[2] // 3
    gap = padded - share
    for j in range(n):
        for t in range(3):
            first = t * width + HD * low[j]
            qkv_to[j, :share, t * sh : (t + 1) * sh] = qkv_ref[:, first : first + sh]
        widen_to[j, :share] = widen_ref[:, j * hide : (j + 1) * hide]
        if gap:
            qkv_to[j, share:] = jnp.zeros((gap, 3 * sh), BF16)
            widen_to[j, share:] = jnp.zeros((gap, hide), BF16)
    spread = []
    for ref in (out_ref, narrow_ref):
        rows = ref.shape[0]
        pieces = []
        for j in range(n):
            pieces.append(ref[:, j * share : (j + 1) * share])
            if gap:
                pieces.append(jnp.zeros((rows, gap), BF16))
        spread.append(jnp.concatenate(pieces, axis=1))
    narrow_to[...] = spread[1]
    out_to[...] = spread[0]


def lay_out_call(low, slots, padded, qkv, widen, out, narrow):
    n = len(low)
    share, hidden = widen.shape
    sh = slots * HD
    return pl.pallas_call(
        functools.partial(lay_out_kernel, low, share),
        out_shape=[
            jax.ShapeDtypeStruct((n, padded, 3 * sh), BF16),
            jax.ShapeDtypeStruct((n, padded, hidden // n), BF16),
            jax.ShapeDtypeStruct((share, n * padded), BF16),
            jax.ShapeDtypeStruct((narrow.shape[0], n * padded), BF16),
        ],
        in_specs=[VMEM_SPEC] * 4,
        out_specs=[VMEM_SPEC] * 4,
        compiler_params=params(),
        name="lay_out",
    )(qkv, widen, out, narrow)


def settle_kernel(low, share, qkv_ref, widen_ref, out_ref, narrow_ref, *outs):
    qkv_to, widen_to, out_to, narrow_to = outs
    n, padded, hide = widen_ref.shape
    width = qkv_to.shape[1] // 3
    sh = qkv_ref.shape[2] // 3
    qkv_to[...] = jnp.zeros_like(qkv_to)
    for j in range(n):
        for t in range(3):
            first = t * width + HD * low[j]
            qkv_to[:, first : first + sh] += qkv_ref[j, :share, t * sh : (t + 1) * sh].astype(F32)
    for j in range(n):
        widen_to[:, j * hide : (j + 1) * hide] = widen_ref[j, :share].astype(F32)
        for ref, to in ((out_ref, out_to), (narrow_ref, narrow_to)):
            piece = ref[: to.shape[0], j * padded : j * padded + share]
            to[:, j * share : (j + 1) * share] = piece.astype(F32)


def settle_call(low, share, qkv, widen, out, narrow):
    n, _, hide = widen.shape
    width = n * share
    return pl.pallas_call(
        functools.partial(settle_kernel, low, share),
        out_shape=[
            jax.ShapeDtypeStruct((share, 3 * width), F32),
            jax.ShapeDtypeStruct((share, n * hide), F32),
            jax.ShapeDtypeStruct((share, width), F32),
            jax.ShapeDtypeStruct((hide, width), F32),
        ],
        in_specs=[VMEM_SPEC] * 4,
        out_specs=[VMEM_SPEC] * 4,
        compiler_params=params(),
        name="settle",
    )(qkv, widen, out, narrow)


def unit_rows(values, mask, width):
    center = (values - jnp.sum(values, axis=-1, keepdims=True) * (1.0 / width)) * mask
    spread = jnp.sum(center * center, axis=-1, keepdims=True) * (1.0 / width)
    scale = lax.rsqrt(spread + EPSILON)
    return center * scale, scale


def norm_back(grad, unit, scale, gain, width):
    inner = grad * gain
    mean = jnp.sum(inner, axis=-1, keepdims=True) * (1.0 / width)
    along = jnp.sum(inner * unit, axis=-1, keepdims=True) * (1.0 / width)
    return (inner - mean - unit * along) * scale


FORWARD_KINDS = ("mid", "end")


def phase_kernel(n, kind, width, side, *refs):
    forward = kind in FORWARD_KINDS
    gathers = kind != "first"
    ins = 6 if forward else 5
    outs = (1 if forward else 2) + (1 if gathers else 0)
    in_refs, refs = refs[:ins], refs[ins:]
    if side:
        side_in, refs = refs[0], refs[1:]
    out_refs, refs = refs[:outs], refs[outs:]
    if side:
        side_out, refs = refs[0], refs[1:]
    ybuf, rbuf, sbuf, s_ss, s_rs = refs[:5]
    refs = refs[5:]
    if gathers:
        own, g_ss, g_rs, g_ls = refs[:4]
        refs = refs[4:]
    p = Place(n)
    greet(p, line=True, over=bool(side), sibling=side == "swap")
    scatter = Scatter(p, in_refs[0], ybuf, rbuf, sbuf, s_ss, s_rs)
    scatter.start()
    job = None
    if side == "swap":
        job = RowSwap(p, side_in, side_out, *refs[:3])
        job.start()
    elif side:
        job = Cross(p, side_in, side_out, *refs[:2], int(side[-1]))
        job.start()
    gather = None
    if gathers:
        gather = Gather(p, own, out_refs[-1], g_ss, g_rs, g_ls)
    for step in scatter.steps():
        step()
    hr = ybuf.shape[3]
    sums = [jnp.zeros((1, in_refs[0].shape[1]), F32)] * 3
    for half in range(HALVES):
        rows = slice(half * hr, (half + 1) * hr)
        total = scatter.result(half)
        if forward:
            value = in_refs[1][rows] + (total + in_refs[2][...])
            out_refs[0][rows] = value
            gain, shift, mask = (ref[...] for ref in in_refs[3:])
            own[rows] = (unit_rows(value, mask, width)[0] * gain + shift).astype(BF16)
        else:
            base, grad, gain, mask = in_refs[1][rows], in_refs[2][rows], in_refs[3], in_refs[4]
            unit, scale = unit_rows(base, mask[...], width)
            value = grad + norm_back(total, unit, scale, gain[...], width)
            out_refs[0][rows] = value
            low = value.astype(BF16)
            if gathers:
                own[rows] = low
            for item, term in enumerate((total * unit, total, low.astype(F32))):
                sums[item] = sums[item] + jnp.sum(term, axis=0, keepdims=True)
        if gathers:
            gather.start([half])
    if not forward:
        out_refs[1][...] = jnp.concatenate(sums, axis=0)
    if gathers:
        for step in gather.steps():
            step()
    if side == "swap":
        job.step()
    if gathers:
        gather.finish()
    scatter.finish()
    if job is not None:
        job.finish()


def scatter_scratch(n, rows, full):
    zn = n // 2
    return [pltpu.VMEM((2, zn, HALVES, rows // HALVES, full), BF16)] * 3 + [
        DMA((4, zn, HALVES)),
        DMA((4, zn, HALVES)),
    ]


def gather_scratch(n):
    zn = n // 2
    return [DMA((4, zn, HALVES)), DMA((4, zn, HALVES)), DMA((HALVES,))]


def phase_call(n, kind, collective_id, width, part, *local, side=None, carried=None):
    total_rows, full = part.shape
    rows = total_rows // n
    forward = kind in FORWARD_KINDS
    gathers = kind != "first"
    shapes = [jax.ShapeDtypeStruct((rows, full), F32)]
    if not forward:
        shapes.append(jax.ShapeDtypeStruct((3, full), F32))
    scratch = scatter_scratch(n, rows, full)
    if gathers:
        shapes.append(jax.ShapeDtypeStruct((total_rows, full), BF16))
        scratch += [pltpu.VMEM((rows, full), BF16)] + gather_scratch(n)
    in_specs = [VMEM_SPEC] * (1 + len(local))
    out_specs = [VMEM_SPEC] * len(shapes)
    args = (part,) + local
    if side:
        args += (carried,)
        in_specs.append(ANY_SPEC)
        out_specs.append(ANY_SPEC)
        lead = (2,) if side == "swap" else ()
        shapes.append(jax.ShapeDtypeStruct(lead + carried.shape, BF16))
        scratch += [DMA((2,)), DMA((2,)), DMA] if side == "swap" else [DMA, DMA]
    return pl.pallas_call(
        functools.partial(phase_kernel, n, kind, width, side),
        out_shape=shapes,
        in_specs=in_specs,
        out_specs=out_specs,
        scratch_shapes=scratch,
        compiler_params=params(collective_id),
        name="phase_" + kind,
    )(*args)


def dot_t(a, b):
    return lax.dot_general(a, b, (((1,), (1,)), ((), ())), preferred_element_type=F32)


def dot_n(a, b):
    return lax.dot_general(a, b, (((1,), (0,)), ((), ())), preferred_element_type=F32)


def in_blocks(rows, step, chunk, between):
    count = rows // step
    if count <= 2:
        for b in range(count):
            chunk(b * step, between)
    else:

        def body(b, carry):
            chunk(pl.multiple_of(b * step, step), [])
            return carry

        lax.fori_loop(0, count, body, 0)


def run_next(between):
    if between:
        between.pop(0)()


def attend_kernel(n, slots, step, side, own_ref, kpos_ref, qpos_ref, carried, *refs):
    att_ref, low_ref, lse_ref, oth_ref, carried_to, kv_ss, kv_rs = refs[:7]
    p = Place(n)
    rows = own_ref.shape[0]
    sh = slots * HD
    power = HD**-0.5 * LOG2E
    if side == "spread":
        greet(p, spread=True, over=True, sibling=True)
    else:
        greet(p, line=True, sibling=True)
    swap = remote(own_ref.at[:, pl.ds(sh, 2 * sh)], oth_ref, kv_ss, kv_rs, p.sibling)
    swap.start()
    job = (Spread if side == "spread" else Gather)(p, carried, carried_to, *refs[7:])
    job.start()
    swap.wait_recv()

    def at(base, slot):
        return slice(base + slot * HD, base + (slot + 1) * HD)

    def chunk(first, between):
        q_rows = pl.ds(first, step)
        qpos = qpos_ref[:, q_rows]
        for slot in range(slots):
            queries = own_ref[q_rows, at(0, slot)]
            keys = (own_ref[:, at(sh, slot)], oth_ref[:, at(0, slot)])
            values = (own_ref[:, at(2 * sh, slot)], oth_ref[:, at(sh, slot)])
            scores = []
            for part in range(2):
                allowed = kpos_ref[part * rows : (part + 1) * rows] <= qpos
                scores.append(jnp.where(allowed, dot_t(keys[part], queries), MASKED))
            top = jnp.maximum(
                jnp.max(scores[0], axis=0, keepdims=True), jnp.max(scores[1], axis=0, keepdims=True)
            )
            total = jnp.zeros_like(top)
            weighted = jnp.zeros((HD, step), F32)
            exps = []
            for part in range(2):
                e = jnp.exp2((scores[part] - top) * power)
                total = total + jnp.sum(e, axis=0, keepdims=True)
                exps.append(e)
            inverse = 1.0 / total
            for part in range(2):
                probs = (exps[part] * inverse).astype(BF16)
                weighted = weighted + dot_n(values[part].T, probs)
            att_ref[at(0, slot), q_rows] = weighted
            low_ref[q_rows, at(0, slot)] = weighted.T.astype(BF16)
            lse_ref[slot : slot + 1, q_rows] = top * power + jnp.log(total) * LOG2E
            run_next(between)

    between = job.steps()
    in_blocks(rows, step, chunk, between)
    for rest in between:
        rest()
    swap.wait_send()
    job.finish()


def attend_call(n, collective_id, slots, qkv, kpos, qpos, side, carried):
    rows = qkv.shape[0]
    zn = n // 2
    sh = slots * HD
    step = min(rows, 256)
    if side == "spread":
        moved = jax.ShapeDtypeStruct((2,) + carried.shape, BF16)
        scratch = [DMA((4, zn)), DMA((4, zn)), DMA]
    else:
        moved = jax.ShapeDtypeStruct((n * carried.shape[0], carried.shape[1]), BF16)
        scratch = gather_scratch(n)
    return pl.pallas_call(
        functools.partial(attend_kernel, n, slots, step, side),
        out_shape=[
            jax.ShapeDtypeStruct((sh, rows), F32),
            jax.ShapeDtypeStruct((rows, sh), BF16),
            jax.ShapeDtypeStruct((slots, rows), F32),
            jax.ShapeDtypeStruct((rows, 2 * sh), BF16),
            moved,
        ],
        in_specs=[VMEM_SPEC] * 3 + [ANY_SPEC],
        out_specs=[VMEM_SPEC] * 4 + [ANY_SPEC],
        scratch_shapes=[DMA, DMA] + scratch,
        compiler_params=params(collective_id),
        name="attend_" + side,
    )(qkv, kpos, qpos, carried)


def attend_back_kernel(n, slots, step, last, *refs):
    own_ref, oth_ref, grad_ref, att_ref, lse_ref, kpos_ref, qpos_ref = refs[:7]
    refs = refs[7:]
    if last:
        part_ref, base_ref, bias_ref = refs[:3]
        refs = refs[3:]
    triple_ref, refs = refs[0], refs[1:]
    if last:
        value_ref, refs = refs[0], refs[1:]
    dq_t, dkv_own, dkv_oth, came, kv_ss, kv_rs = refs[:6]
    p = Place(n)
    rows = own_ref.shape[0]
    sh = slots * HD
    scale = HD**-0.5
    greet(p, line=last, sibling=True)
    between = []
    if last:
        scatter = Scatter(p, part_ref, *refs[6:])
        scatter.start()
        between = scatter.steps()

    def at(base, slot):
        return slice(base + slot * HD, base + (slot + 1) * HD)

    dq_t[...] = jnp.zeros_like(dq_t)
    swap = remote(dkv_oth, came, kv_ss, kv_rs, p.sibling)
    for part in (1, 0):
        dkv = (dkv_own, dkv_oth)[part]
        src = (own_ref, oth_ref)[part]
        base = (sh, 0)[part]
        dkv[...] = jnp.zeros_like(dkv)

        def chunk(first, between):
            q_rows = pl.ds(first, step)
            qpos = qpos_ref[:, q_rows]
            for slot in range(slots):
                queries = own_ref[q_rows, at(0, slot)]
                grads = grad_ref[q_rows, at(0, slot)]
                keys, values = src[:, at(base, slot)], src[:, at(base + sh, slot)]
                lse = lse_ref[slot : slot + 1, q_rows]
                correction = jnp.sum(
                    grads.astype(F32).T * att_ref[at(0, slot), q_rows], axis=0, keepdims=True
                )
                allowed = kpos_ref[part * rows : (part + 1) * rows] <= qpos
                scores = dot_t(keys, queries)
                probs = jnp.where(allowed, jnp.exp2(scores * (scale * LOG2E) - lse), 0.0)
                prob_grad = dot_t(values, grads)
                score_grad = (probs * (prob_grad - correction)).astype(BF16)
                dkv[:, at(0, slot)] += dot_n(score_grad, queries) * scale
                dkv[:, at(sh, slot)] += dot_n(probs.astype(BF16), grads)
                dq_t[at(0, slot), q_rows] += dot_n(keys.T, score_grad)
                run_next(between)

        in_blocks(rows, step, chunk, between)
        if part:
            swap.start()
    triple_ref[:, :sh] = (dq_t[...].T * scale).astype(BF16)
    for rest in between:
        rest()
    if last:
        hr = base_ref.shape[0] // HALVES
        for half in range(HALVES):
            part_rows = slice(half * hr, (half + 1) * hr)
            total = scatter.result(half)
            value_ref[part_rows] = base_ref[part_rows] + (total + bias_ref[...])
        scatter.finish()
    swap.wait_recv()
    triple_ref[:, sh:] = (dkv_own[...] + came[...]).astype(BF16)
    swap.wait_send()


def attend_back_call(n, collective_id, slots, *args, last=()):
    qkv = args[0]
    rows = qkv.shape[0]
    sh = slots * HD
    step = min(rows, 256)
    shapes = [jax.ShapeDtypeStruct((rows, 3 * sh), BF16)]
    scratch = [pltpu.VMEM((sh, rows), F32)] + [pltpu.VMEM((rows, 2 * sh), F32)] * 3
    scratch += [DMA, DMA]
    if last:
        shapes.append(jax.ShapeDtypeStruct(last[1].shape, F32))
        scratch += scatter_scratch(n, *last[1].shape)
    return pl.pallas_call(
        functools.partial(attend_back_kernel, n, slots, step, bool(last)),
        out_shape=shapes,
        in_specs=[VMEM_SPEC] * (len(args) + len(last)),
        out_specs=[VMEM_SPEC] * len(shapes),
        scratch_shapes=scratch,
        compiler_params=params(collective_id),
        name="attend_back",
    )(*args, *last)


def fold_kernel(n, count, *refs):
    blocks, rows = refs[:2]
    blocks_to, rows_to = refs[2:4]
    blocks_in, rows_in, ss, rs = refs[4:]
    p = Place(n)
    zn = p.zn
    greet(p, sibling=True)
    near_y = 1 - p.far_y
    half = rows_to.shape[0]

    def mine(first):
        return pl.ds(pl.multiple_of(first * half, 8), half)

    copies = [
        remote(blocks.at[z * 2 + near_y], blocks_in.at[z], ss.at[z], rs.at[z], p.sibling)
        for z in range(zn)
    ]
    copies.append(remote(rows.at[mine(1 - p.c)], rows_in, ss.at[zn], rs.at[zn], p.sibling))
    for copy in copies:
        copy.start()
    for z in range(zn):
        copies[z].wait_recv()
        own = blocks[z * 2 + p.far_y].astype(F32)
        blocks_to[z] = (own + blocks_in[z].astype(F32)).astype(BF16)
    copies[zn].wait_recv()
    rows_to[...] = (rows[mine(p.c)].astype(F32) + rows_in[...].astype(F32)).astype(BF16)
    for copy in copies:
        copy.wait_send()


def fold_call(n, collective_id, blocks, rows):
    zn = n // 2
    halves = (rows.shape[0] // 2, rows.shape[1])
    some = (zn,) + blocks.shape[1:]
    return pl.pallas_call(
        functools.partial(fold_kernel, n, 1),
        out_shape=[jax.ShapeDtypeStruct(some, BF16), jax.ShapeDtypeStruct(halves, BF16)],
        in_specs=[VMEM_SPEC] * 2,
        out_specs=[VMEM_SPEC] * 2,
        scratch_shapes=[
            pltpu.VMEM(some, BF16),
            pltpu.VMEM(halves, BF16),
            DMA((zn + 1,)),
            DMA((zn + 1,)),
        ],
        compiler_params=params(collective_id),
        name="fold",
    )(blocks, rows)


def finish_kernel(n, *refs):
    widen, narrow, qkv, qkv_far, out, out_far, vec, streams = refs[:8]
    widen_to, narrow_to, qkv_to, out_to, vec_to, streams_to = refs[8:14]
    qkv_in, qkv_sum, out_in, out_sum, vec_in, vec_sum, vec_sib = refs[14:21]
    a_ss, a_rs, x_ss, x_rs, v_ss, v_rs, r_ss, r_rs, ls = refs[21:]
    p = Place(n)
    s, c, h, z, zn = p.s, p.c, p.h, p.z, p.zn
    greet_all(p)

    def vec_copy(a, b):
        l, i = lax.rem(s + a, 2), lax.rem(h + b, n)
        return remote(vec.at[l, i], vec_in.at[s, h], v_ss.at[a, b], v_rs.at[a, b], (l, c, i))

    def x_block(dz):
        far = lax.rem(z + dz, zn)
        return remote(qkv_far.at[far], qkv_in.at[far], x_ss.at[dz], x_rs.at[dz], p.over)

    out_cross = remote(out_far, out_in, x_ss.at[zn], x_rs.at[zn], p.over)
    stream_cross = remote(streams, streams_to, x_ss.at[zn + 1], x_rs.at[zn + 1], p.over)
    spreads = ((widen, widen_to), (qkv_sum, qkv_to))

    def send(w, dz):
        far = lax.rem(z + dz, zn)
        src, dst = spreads[w]
        target = (s, c, far * 2 + p.far_y)
        return remote(src.at[far], dst.at[h], a_ss.at[0, w, dz], a_rs.at[0, w, dz], target)

    def keep(w):
        src, dst = spreads[w]
        return pltpu.make_async_copy(src.at[z], dst.at[h], ls.at[w])

    def aside(w, dz):
        block = spreads[w][1].at[lax.rem(z + zn - dz, zn) * 2 + p.far_y]
        return remote(block, block, a_ss.at[1, w, dz], a_rs.at[1, w, dz], p.sibling)

    def start_zero(w):
        @pl.when(c == 1)
        def _():
            send(w, 0).start()

        @pl.when(c == 0)
        def _():
            keep(w).start()

    def row_copies(w, src, dst):
        half = src.shape[0]
        piece = dst.at[pl.ds(pl.multiple_of(c * half, 8), half)]
        return (
            pltpu.make_async_copy(src, piece, ls.at[2 + w]),
            remote(src, piece, r_ss.at[w], r_rs.at[w], p.sibling),
        )

    order = list(range(1, zn)) + [0]
    for dz in order:
        x_block(dz).start()
    out_cross.start()
    stream_cross.start()
    for a, b in others(n):
        vec_copy(a, b).start()
    for dz in range(1, zn):
        send(0, dz).start()
    start_zero(0)
    narrow_copies = row_copies(0, narrow, narrow_to)
    for copy in narrow_copies:
        copy.start()
    for dz in order:
        x_block(dz).wait_recv()
        far = lax.rem(z + dz, zn)
        qkv_sum[far] = (qkv[far].astype(F32) + qkv_in[far].astype(F32)).astype(BF16)
        if dz:
            send(1, dz).start()
        else:
            start_zero(1)
    out_cross.wait_recv()
    out_sum[...] = (out[...].astype(F32) + out_in[...].astype(F32)).astype(BF16)
    out_copies = row_copies(1, out_sum, out_to)
    for copy in out_copies:
        copy.start()
    total = vec[s, h]
    for a, b in others(n):
        vec_copy(a, b).wait_recv()
        total = total + vec_in[lax.rem(s + a, 2), lax.rem(h + n - b, n)]
    vec_sum[...] = total
    vec_share = remote(vec_sum, vec_sib, r_ss.at[2], r_rs.at[2], p.sibling)
    vec_share.start()
    for w in range(2):

        @pl.when(c == 1)
        def _():
            send(w, 0).wait_recv()

        @pl.when(c == 0)
        def _():
            keep(w).wait()

        for dz in range(zn):
            if dz:
                send(w, dz).wait_recv()
            aside(w, dz).start()
    vec_share.wait_recv()
    vec_to[...] = total + vec_sib[...]
    vec_share.wait_send()
    for w in range(2):

        @pl.when(c == 1)
        def _():
            send(w, 0).wait_send()

        for dz in range(zn):
            if dz:
                send(w, dz).wait_send()
            aside(w, dz).wait_recv()
            aside(w, dz).wait_send()
    for copies in (narrow_copies, out_copies):
        copies[0].wait()
        copies[1].wait_recv()
        copies[1].wait_send()
    for a, b in others(n):
        vec_copy(a, b).wait_send()
    for dz in range(zn):
        x_block(dz).wait_send()
    out_cross.wait_send()
    stream_cross.wait_recv()
    stream_cross.wait_send()


def finish_call(n, collective_id, widen, narrow, qkv, qkv_far, out, out_far, vec, streams):
    zn = n // 2
    piece = vec.shape[2:]
    return pl.pallas_call(
        functools.partial(finish_kernel, n),
        out_shape=[
            jax.ShapeDtypeStruct((n,) + widen.shape[1:], BF16),
            jax.ShapeDtypeStruct((2 * narrow.shape[0], narrow.shape[1]), BF16),
            jax.ShapeDtypeStruct((n,) + qkv.shape[1:], BF16),
            jax.ShapeDtypeStruct((2 * out.shape[0], out.shape[1]), BF16),
            jax.ShapeDtypeStruct(piece, F32),
            jax.ShapeDtypeStruct(streams.shape, BF16),
        ],
        in_specs=[VMEM_SPEC] * 8,
        out_specs=[ANY_SPEC] * 4 + [VMEM_SPEC] * 2,
        scratch_shapes=[
            pltpu.VMEM(qkv.shape, BF16),
            pltpu.VMEM(qkv.shape, BF16),
            pltpu.VMEM(out.shape, BF16),
            pltpu.VMEM(out.shape, BF16),
            pltpu.VMEM((2, n) + piece, F32),
            pltpu.VMEM(piece, F32),
            pltpu.VMEM(piece, F32),
            DMA((2, 2, zn)),
            DMA((2, 2, zn)),
            DMA((zn + 2,)),
            DMA((zn + 2,)),
            DMA((2, n)),
            DMA((2, n)),
            DMA((3,)),
            DMA((3,)),
            DMA((4,)),
        ],
        compiler_params=params(collective_id),
        name="finish",
    )(widen, narrow, qkv, qkv_far, out, out_far, vec, streams)


def windows(width, n):
    share = width // n
    low = [j * share // HD for j in range(n)]
    slots = max(((j + 1) * share - 1) // HD - low[j] + 1 for j in range(n))
    return [min(first, HEADS - slots) for first in low], slots


def pick(table, index):
    return lax.dynamic_index_in_dim(table, index, 0, keepdims=False)


def on_device(n, tokens, block_order, cotangent, *vectors_and_weights):
    (
        first_gain,
        first_shift,
        qkv_weight,
        input_bias,
        out_weight,
        out_bias,
        second_gain,
        second_shift,
        widen_weight,
        widen_bias,
        narrow_weight,
        narrow_bias,
    ) = (member[0] for member in vectors_and_weights)
    s = lax.axis_index("section")
    c = lax.axis_index("ctx")
    h = lax.axis_index("shard")
    _, rows, width = tokens.shape
    hidden = widen_weight.shape[1]
    share = width // n
    hide = hidden // n
    padded = -(-share // 16) * 16
    full = n * padded
    low, slots = windows(width, n)
    sh = slots * HD
    total_rows = n * rows
    half_rows = rows // HALVES

    def pad_features(values):
        lead = values.shape[:-1]
        parts = values.reshape(lead + (n, share))
        parts = jnp.pad(parts, [(0, 0)] * len(lead) + [(0, 0), (0, padded - share)])
        return parts.reshape(lead + (full,))

    def cut_features(values):
        lead = values.shape[:-1]
        return values.reshape(lead + (n, padded))[..., :share].reshape(lead + (width,))

    mask = pad_features(jnp.ones((1, width), F32))
    offsets = jnp.array([j * share - HD * low[j] for j in range(n)], jnp.int32)
    offset = pick(offsets, h)

    qkv_send, widen_send, out_rows, narrow_send = lay_out_call(
        low, slots, padded, qkv_weight, widen_weight, out_weight, narrow_weight
    )
    out_send = lax.dynamic_update_slice(
        jnp.zeros((sh, full), BF16), out_rows, (offset, jnp.int32(0))
    )
    lanes = max(-(-hide // 128) * 128, -(-2 * share // 128) * 128)

    def lane(vector):
        return jnp.pad(vector, (0, lanes - vector.shape[0]))

    pack = jnp.stack(
        [
            lane(member)
            for member in (
                first_gain,
                first_shift,
                out_bias,
                second_gain,
                second_shift,
                narrow_bias,
                input_bias,
                widen_bias,
            )
        ]
    )
    pack = jnp.pad(pack, [(0, 8), (0, 0)])
    own_tokens = pad_features(jnp.where(s == 0, tokens[0], tokens[1]))
    own_cot = pad_features(jnp.where(s == 0, cotangent[0], cotangent[1]))
    tok_all, packs, qkv_all, out_all = start_call(n, own_tokens, pack, qkv_send, out_send)

    order = block_order.reshape(2, n, HALVES).transpose(0, 2, 1)
    places = order[..., None] * half_rows + jnp.arange(half_rows, dtype=jnp.int32)
    places = places.reshape(2, total_rows)
    own_places = jnp.where(c == 0, places[0], places[1])
    oth_places = jnp.where(c == 0, places[1], places[0])
    kpos = jnp.concatenate([own_places, oth_places])[:, None]
    qpos = own_places[None, :]

    layers = []
    for layer in range(2):
        vec = packs[layer].astype(F32)

        def feature(row):
            return jnp.pad(vec[:, row, :share], [(0, 0), (0, padded - share)]).reshape(1, full)

        bias = vec[:, 6, : 2 * share].reshape(2, width)
        bias_windows = jnp.stack([bias[:, HD * f : HD * f + sh] for f in low])
        bias_own = pick(bias_windows, h)
        qkv_bias = jnp.concatenate([bias_own[0], jnp.zeros((sh,), F32), bias_own[1]])
        layers.append(
            dict(
                gain1=feature(0),
                shift1=feature(1),
                out_bias=feature(2),
                gain2=feature(3),
                shift2=feature(4),
                narrow_bias=feature(5),
                qkv_bias=qkv_bias,
                widen_bias=pick(vec[:, 7, :hide], h),
                qkv=qkv_all[layer].reshape(full, 3 * sh),
                out=out_all[layer],
            )
        )

    x = own_tokens.astype(F32)
    unit = unit_rows(tok_all.astype(F32), mask, width)[0]
    normed = (unit * layers[0]["gain1"] + layers[0]["shift1"]).astype(BF16)
    stored = []
    layer_outs = []
    for layer in range(2):
        w = layers[layer]
        qkv = (dot_n(normed, w["qkv"]) + w["qkv_bias"]).astype(BF16)
        side, carried = ("gather", own_cot) if layer else ("spread", widen_send)
        att, att_low, lse, other, moved = attend_call(
            n, 1 + layer, slots, qkv, kpos, qpos, side, carried
        )
        if layer:
            out_low_all = moved
        else:
            for member in range(2):
                layers[member]["widen"] = moved[member].reshape(full, hide)
        part = dot_n(att_low, w["out"]).astype(BF16)
        found = phase_call(
            n,
            "mid",
            3 + layer,
            width,
            part,
            x,
            w["out_bias"],
            w["gain2"],
            w["shift2"],
            mask,
            side=None if layer else "swap",
            carried=narrow_send,
        )
        residual, normed_two = found[:2]
        if not layer:
            for member in range(2):
                layers[member]["narrow"] = found[2][member]
        hidden_pre = dot_n(normed_two, w["widen"]) + w["widen_bias"]
        act = jnp.tanh(GELU_A * (hidden_pre + GELU_B * hidden_pre**3))
        hidden_low = (0.5 * hidden_pre * (1.0 + act)).astype(BF16)
        part = dot_n(hidden_low, w["narrow"]).astype(BF16)
        stored.append((x, normed, qkv, other, att, att_low, lse, residual, normed_two))
        stored[-1] += (hidden_pre, hidden_low)
        if layer == 0:
            nxt = layers[1]
            x, normed = phase_call(
                n,
                "end",
                5,
                width,
                part,
                residual,
                w["narrow_bias"],
                nxt["gain1"],
                nxt["shift1"],
                mask,
            )
            layer_outs.append(x)
        else:
            last = (part, residual, w["narrow_bias"])

    def over_rows(a, b):
        found = lax.dot_general(a, b, (((0,), (0,)), ((), ())), preferred_element_type=F32)
        return found.astype(BF16)

    def column_sums(values):
        return jnp.sum(values.astype(F32), axis=0)

    out_grad = own_cot.astype(F32)
    out_sums = column_sums(own_cot)[None]
    vec_grads, d_ins, early, late, came = {}, {}, {}, {}, {}
    for layer in (1, 0):
        w = layers[layer]
        x, normed, qkv, other, att, att_low, lse, residual, normed_two = stored[layer][:9]
        hidden_pre, hidden_low = stored[layer][9:]
        hidden_grad = dot_t(out_low_all, w["narrow"])
        square = hidden_pre * hidden_pre
        act = jnp.tanh(GELU_A * (hidden_pre + GELU_B * hidden_pre * square))
        slope = 0.5 * (1.0 + act) + 0.5 * hidden_pre * (1.0 - act * act) * GELU_A * (
            1.0 + 3.0 * GELU_B * square
        )
        pre_grad = (hidden_grad * slope).astype(BF16)
        part = dot_t(pre_grad, w["widen"]).astype(BF16)
        early[layer] = fold_call(
            n,
            7 + layer,
            over_rows(normed_two, pre_grad).reshape(n, padded, hide),
            jnp.pad(over_rows(hidden_low, out_low_all), [(0, -hide % 32), (0, 0)]),
        )
        source = f"cross{1 - layer}"
        resid_grad, sums_two, resid_low_all, narrow_came = phase_call(
            n,
            "resid",
            9 + layer,
            width,
            part,
            residual,
            out_grad,
            w["gain2"],
            mask,
            side=source,
            carried=early[layer][1],
        )
        att_grad = dot_t(resid_low_all, w["out"]).astype(BF16)
        found = attend_back_call(
            n,
            11 + layer,
            slots,
            qkv,
            other,
            att_grad,
            att,
            lse,
            kpos,
            qpos,
            last=last if layer else (),
        )
        triple = found[0]
        if layer:
            layer_outs.append(found[1])
        part = dot_t(triple, w["qkv"]).astype(BF16)
        found = phase_call(
            n,
            "input" if layer else "first",
            13 + layer,
            width,
            part,
            x,
            resid_grad,
            w["gain1"],
            mask,
            side=source,
            carried=early[layer][0],
        )
        d_in, sums_one = found[:2]
        d_ins[layer] = d_in
        came[layer] = (found[-1], narrow_came)
        out_full = over_rows(att_low, resid_low_all)
        late[layer] = fold_call(
            n,
            15 + layer,
            over_rows(normed, triple).reshape(n, padded, 3 * sh),
            lax.dynamic_slice_in_dim(jnp.pad(out_full, [(0, sh), (0, 0)]), offset, sh, 0),
        )
        triple_sums = column_sums(triple)
        spots = [
            jnp.pad(
                jnp.stack([triple_sums[:sh], triple_sums[2 * sh :]]),
                [(0, 0), (HD * f, width - sh - HD * f)],
            )
            for f in low
        ]
        slot_sums = pick(jnp.stack(spots), h)
        hide_sums = jnp.where(
            jnp.arange(n, dtype=jnp.int32)[:, None] == h, column_sums(pre_grad)[None], 0.0
        )
        features = jnp.concatenate([sums_one[:2], sums_two[2:], sums_two[:2], out_sums])
        features = features.reshape(6, n, padded).transpose(1, 0, 2)
        vec_grads[layer] = jnp.concatenate(
            [
                jnp.pad(features, [(0, 0), (0, 0), (0, lanes - padded)]),
                jnp.pad(slot_sums.reshape(n, 1, 2 * share), [(0, 0), (0, 0), (0, lanes - 2 * share)]),
                jnp.pad(hide_sums[:, None], [(0, 0), (0, 0), (0, lanes - hide)]),
            ],
            axis=1,
        )
        out_grad = d_in
        out_sums = sums_one[2:]
        if layer:
            out_low_all = found[2]

    def own(first, second):
        return jnp.where(s == 0, first, second)

    def added(item):
        return own(
            early[0][item].astype(F32) + came[0][item].astype(F32),
            early[1][item].astype(F32) + came[1][item].astype(F32),
        ).astype(BF16)

    streams = jnp.stack(
        [own(layer_outs[1], layer_outs[0]), own(d_ins[1], d_ins[0])]
    ).astype(BF16)
    widen_back, narrow_back, qkv_back, out_back, vec, streams_came = finish_call(
        n,
        17,
        added(0),
        added(1),
        own(late[0][0], late[1][0]),
        own(late[1][0], late[0][0]),
        own(late[0][1], late[1][1]),
        own(late[1][1], late[0][1]),
        jnp.stack([vec_grads[0], vec_grads[1]]),
        streams,
    )
    grads = settle_call(low, share, qkv_back, widen_back, out_back, narrow_back)
    qkv_grad, widen_grad, out_grad_w, narrow_grad = grads

    def joined(mine, theirs):
        theirs = theirs.astype(F32)
        return cut_features(jnp.stack([own(mine, theirs), own(theirs, mine)]))[None]

    layer_out = joined(own(layer_outs[0], layer_outs[1]), streams_came[0])
    d_in = joined(own(d_ins[0], d_ins[1]), streams_came[1])

    def vector(row, size):
        return vec[row, :size][None]

    return (
        layer_out,
        d_in,
        vector(0, share),
        vector(1, share),
        qkv_grad[None],
        vector(6, 2 * share),
        out_grad_w[None],
        vector(2, share),
        vector(3, share),
        vector(4, share),
        widen_grad[None],
        vector(7, hide),
        narrow_grad[None],
        vector(5, share),
    )


def solution(mesh):
    rows = P(None, ("ctx", "shard"), None)
    vector = P("section", "shard")
    matrix = P("section", "shard", None)
    order = (
        vector,
        vector,
        matrix,
        vector,
        matrix,
        vector,
        vector,
        vector,
        matrix,
        vector,
        matrix,
        vector,
    )
    streams = P("section", None, ("ctx", "shard"), None)
    return jax.shard_map(
        functools.partial(on_device, mesh.shape["shard"]),
        mesh=mesh,
        in_specs=(rows, P(), rows) + order,
        out_specs=(streams, streams) + order,
        check_vma=False,
    )
```

time: 4130 us -> 841 us (0.20)
  blocking collectives: 2150 us -> 0 us
  waiting for transfers between devices: 1270 us -> 0 us
  Pallas kernels: 0 us -> 658 us
  matrix products: 349 us -> 84.8 us
  local copies, waits for them, and re-layouts: 243 us -> 55.2 us
    unnamed x5 -> x0, blocking collectives: 2040 us -> none
    all_gather x13 -> x0, waiting for transfers between devices: 1220 us -> none  [the longest x1 400 us: on_device(): lax.all_gather(narrow_weight, 'shard', axis=1, tiled=True)]
    pallas_call x0 -> x19, Pallas kernels: none -> 658 us  [the longest x7 348 us: phase_call(): pl.pallas_call(functools.partial(phase_kernel, n, kind, width, side), out...]
    dot_general x46 -> x24, matrix products: 349 us -> 84.8 us  [the longest x8 30.4 us: dot_t(): lax.dot_general(a, b, (((1,), (1,)), ((), ())), preferred_element_type=F32)]
    all_gather x4 -> x0, blocking collectives: 117 us -> none  [the longest x3 113 us: backward_layer(): lax.all_gather(packed_stats, ('ctx', 'shard'), axis=0, tiled=True)]
    slice x23 -> x22, local copies, waits for them, and re-layouts: 119 us -> 13.6 us  [the longest x1 4.3 us: on_device(): qkv_all[layer].reshape(full, 3 * sh)]
    unnamed x453 -> x152, local copies, waits for them, and re-layouts: 52.1 us -> 6.74 us
  transfers between devices with their start and end apart: 22 -> 0, of which waited for: 16 -> 0; matrix products, arithmetic and copies ran while one was open for 55% -> 0% of each run, Pallas kernels for 0% -> 0%
where the time goes in v1:
time: 841 us; the launch traced here: 828 us
  Pallas kernels  658 us (78%)
  matrix products  84.8 us (10%)
  local copies, waits for them, and re-layouts  55.2 us (7%)
  other arithmetic  28.2 us (3%)
    pallas_call x7, Pallas kernels, phase_call(): pl.pallas_call(functools.partial(phase_kernel, n, kind, width, side), out...  348 us
    pallas_call x2, Pallas kernels, attend_call(): pl.pallas_call(functools.partial(attend_kernel, n, slots, step, side), ou...  83.4 us
    pallas_call x1, Pallas kernels, finish_call(): pl.pallas_call(functools.partial(finish_kernel, n), out_shape=[jax.ShapeD...  74 us
    pallas_call x1, Pallas kernels, start_call(): pl.pallas_call(functools.partial(start_kernel, n), out_shape=shapes, in_s...  63.6 us
    pallas_call x2, Pallas kernels, attend_back_call(): pl.pallas_call(functools.partial(attend_back_kernel, n, slots, step, bool...  34.6 us
    pallas_call x4, Pallas kernels, fold_call(): pl.pallas_call(functools.partial(fold_kernel, n, 1), out_shape=[jax.Shape...  33.7 us
    dot_general x8, matrix products, dot_t(): lax.dot_general(a, b, (((1,), (1,)), ((), ())), preferred_element_type=F32)  30.4 us
    dot_general x8, matrix products, over_rows(): lax.dot_general(a, b, (((0,), (0,)), ((), ())), preferred_element_type=F32)  27.5 us

profile of v1, /device:TPU:0, one launch (start us, length us, event | category | flops | bytes accessed | tf_op | source)
XLA Modules:
  0.0 828.4 jit_solution(14596559273974536094)
XLA Ops:
  15.5 9.4 %lay_out.1 = (bf16[8,208,768]{2,1,0:T(8,128)(2,1)}, bf16[8,208,800]{2,1,0:T(8,128)(2,1)}, bf16[200,1664]{1,0:T(8,128)(2,1)}, bf16[800,1664]{1,0:T(8,128)(2,1)}) custom-call(bf16[200,4800]{1,0:T(8,128)(2,1)} %bitcast.273, bf16[200,6400]{1,0:T(8,128)(2,1)} %bitcast.266, bf16[200,1600]{1,0:T(8,128)(2,1)} %bitcast.274, bf16[800,1600]{1,0:T(8,128)(2,1)} %bitcast.265), custom_call_target="tpu_custom_call" | custom-call | tf_op jit(solution)/shard_map/lay_out/pallas_call | solution.py:606
  27.1 63.6 %start.1 = (bf16[512,1664]{1,0:T(8,128)(2,1)}, bf16[2,8,16,896]{3,2,1,0:T(8,128)(2,1)}, bf16[2,8,208,768]{3,2,1,0:T(8,128)(2,1)}, bf16[2,256,1664]{2,1,0:T(8,128)(2,1)}) custom-call(bf16[64,1664]{1,0:T(8,128)(2,1)} %copy-done.15, bf16[16,896]{1,0:T(8,128)(2,1)} %pad.178.pack_ref, bf16[8,208,768]{2,1,0:T(8,128)(2,1)} %get-tuple-element.74.qkv_ref, ...), custom_call_target="tpu_custom_call" | custom-call | tf_op jit(solution)/shard_map/start/pallas_call | solution.py:553
  102.6 4.3 fusion.73
  108.4 2.8 add_convert_fusion.1.own_ref.refs_0_
  111.2 58.7 %attend_spread.1 = (f32[256,512]{1,0:T(8,128)}, bf16[512,256]{1,0:T(8,128)(2,1)}, f32[4,512]{1,0:T(4,128)}, bf16[512,512]{1,0:T(8,128)(2,1)}, bf16[2,8,208,800]{3,2,1,0:T(8,128)(2,1)}) custom-call(bf16[512,768]{1,0:T(8,128)(2,1)} %add_convert_fusion.1.own_ref.refs_0_, s32[1024,1]{1,0:T(8,128)} %copy.34.kpos_ref.refs_5_, ...), custom_call_target="tpu_custom_call" | custom-call | tf_op jit(solution)/shard_map/attend_spread/pallas_call | solution.py:882
  169.9 3.4 fusion.72
  173.3 2.1 convolution_convert_fusion.13.refs_0_
  175.5 86.4 %phase_mid.2 = (f32[64,1664]{1,0:T(8,128)}, bf16[512,1664]{1,0:T(8,128)(2,1)}, bf16[2,800,1664]{2,1,0:T(8,128)(2,1)}) custom-call(bf16[512,1664]{1,0:T(8,128)(2,1)} %convolution_convert_fusion.13.refs_0_, f32[64,1664]{1,0:T(8,128)} %convert_element_type.227.refs_1_, f32[1,1664]{1,0:T(1,128)} %reshape.281.refs_2_, f32[1,1664]{1,0:T(1,128)} %reshape.282.refs_3_, ...), custom_call_target="tpu_custom_call" | custom-call | tf_op jit(solution)/shard_map/phase_mid/pallas_call | solution.py:776
  261.9 3.3 fusion.79
  266.4 3.5 convolution_convert_fusion.12.refs_0_
  270.0 50.9 %phase_end.1 = (f32[64,1664]{1,0:T(8,128)}, bf16[512,1664]{1,0:T(8,128)(2,1)}) custom-call(bf16[512,1664]{1,0:T(8,128)(2,1)} %convolution_convert_fusion.12.refs_0_, f32[64,1664]{1,0:T(8,128)} %get-tuple-element.86.refs_1_, f32[1,1664]{1,0:T(1,128)} %reshape.284.refs_2_, f32[1,1664]{1,0:T(1,128)} %reshape.285.refs_3_, f32[1,1664]{1,0:T(1,128)} %reshape.286.refs_4_, ...), custom_call_target="tpu_custom_call" | custom-call | tf_op jit(solution)/shard_map/phase_end/pallas_call | solution.py:776
  320.9 3.9 add_convert_fusion.own_ref.refs_0_
  324.9 24.7 %attend_gather.1 = (f32[256,512]{1,0:T(8,128)}, bf16[512,256]{1,0:T(8,128)(2,1)}, f32[4,512]{1,0:T(4,128)}, bf16[512,512]{1,0:T(8,128)(2,1)}, bf16[512,1664]{1,0:T(8,128)(2,1)}) custom-call(bf16[512,768]{1,0:T(8,128)(2,1)} %add_convert_fusion.own_ref.refs_0_, s32[1024,1]{1,0:T(8,128)} %copy.34.kpos_ref.refs_5_, s32[1,512]{1,0:T(1,128)} %select_n.176.qpos_ref.refs_6_, ...), custom_call_target="tpu_custom_call" | custom-call | tf_op jit(solution)/shard_map/attend_gather/pallas_call | solution.py:882
  349.6 3.1 convolution_convert_fusion.11.refs_0_
  352.7 42.2 %phase_mid.3 = (f32[64,1664]{1,0:T(8,128)}, bf16[512,1664]{1,0:T(8,128)(2,1)}) custom-call(bf16[512,1664]{1,0:T(8,128)(2,1)} %convolution_convert_fusion.11.refs_0_, f32[64,1664]{1,0:T(8,128)} %get-tuple-element.87.refs_1_, f32[1,1664]{1,0:T(1,128)} %reshape.288.refs_2_, f32[1,1664]{1,0:T(1,128)} %reshape.289.refs_3_, f32[1,1664]{1,0:T(1,128)} %reshape.290.refs_4_, ...), custom_call_target="tpu_custom_call" | custom-call | tf_op jit(solution)/shard_map/phase_mid/pallas_call | solution.py:776
  394.9 3.3 fusion.80
  398.2 4.9 convert_reduce_fusion.1
  403.1 3.3 convolution_convert_fusion.10.refs_0_
  406.4 3.2 convolution_convert_fusion.1
  409.5 5.6 copy.36
  415.1 5.7 convolution_convert_fusion.3.refs_1_
  420.8 10.0 %fold.4 = (bf16[4,208,800]{2,1,0:T(8,128)(2,1)}, bf16[400,1664]{1,0:T(8,128)(2,1)}) custom-call(bf16[8,208,800]{2,1,0:T(8,128)(2,1)} %bitcast.260, bf16[800,1664]{1,0:T(8,128)(2,1)} %convolution_convert_fusion.3.refs_1_), custom_call_target="tpu_custom_call" | custom-call | tf_op jit(solution)/shard_map/fold/pallas_call | solution.py:1026
  430.8 4.9 convolution_convert_fusion.9.refs_7_
  435.7 43.9 %phase_resid.2 = (f32[64,1664]{1,0:T(8,128)}, f32[3,1664]{1,0:T(4,128)}, bf16[512,1664]{1,0:T(8,128)(2,1)}, bf16[400,1664]{1,0:T(8,128)(2,1)}) custom-call(bf16[512,1664]{1,0:T(8,128)(2,1)} %convolution_convert_fusion.10.refs_0_, f32[64,1664]{1,0:T(8,128)} %get-tuple-element.93.refs_1_.refs_8_, f32[64,1664]{1,0:T(8,128)} %convert_element_type.236.refs_2_, ...), custom_call_target="tpu_custom_call" | custom-call | tf_op jit(solution)/shard_map/phase_resid/pallas_call | solution.py:776
  481.3 2.8 convolution_convert_fusion.17.refs_2_
  484.2 25.3 %attend_back.2 = (bf16[512,768]{1,0:T(8,128)(2,1)}, f32[64,1664]{1,0:T(8,128)}) custom-call(bf16[512,768]{1,0:T(8,128)(2,1)} %add_convert_fusion.own_ref.refs_0_, bf16[512,512]{1,0:T(8,128)(2,1)} %get-tuple-element.89.refs_1_, bf16[512,256]{1,0:T(8,128)(2,1)} %convolution_convert_fusion.17.refs_2_, f32[256,512]{1,0:T(8,128)} %get-tuple-element.96.refs_3_, ...), custom_call_target="tpu_custom_call" | custom-call | tf_op jit(solution)/shard_map/attend_back/pallas_call | solution.py:981
  511.3 4.1 convolution_convert_fusion.8.refs_0_
  515.5 3.0 convolution_convert_fusion.4
  518.9 42.0 %phase_input.1 = (f32[64,1664]{1,0:T(8,128)}, f32[3,1664]{1,0:T(4,128)}, bf16[512,1664]{1,0:T(8,128)(2,1)}, bf16[4,208,800]{2,1,0:T(8,128)(2,1)}) custom-call(bf16[512,1664]{1,0:T(8,128)(2,1)} %convolution_convert_fusion.8.refs_0_, f32[64,1664]{1,0:T(8,128)} %get-tuple-element.87.refs_1_, f32[64,1664]{1,0:T(8,128)} %get-tuple-element.100.refs_2_, ...), custom_call_target="tpu_custom_call" | custom-call | tf_op jit(solution)/shard_map/phase_input/pallas_call | solution.py:776
  560.9 5.0 convert_reduce_fusion.2
  565.9 3.4 convolution_convert_fusion.7.refs_0_
  570.2 4.9 convolution_convert_fusion
  575.1 5.3 copy.38
  580.4 5.5 convolution_convert_fusion.2.refs_1_
  585.9 9.8 %fold.5 = (bf16[4,208,800]{2,1,0:T(8,128)(2,1)}, bf16[400,1664]{1,0:T(8,128)(2,1)}) custom-call(bf16[8,208,800]{2,1,0:T(8,128)(2,1)} %bitcast.259, bf16[800,1664]{1,0:T(8,128)(2,1)} %convolution_convert_fusion.2.refs_1_), custom_call_target="tpu_custom_call" | custom-call | tf_op jit(solution)/shard_map/fold/pallas_call | solution.py:1026
  595.7 44.3 %phase_resid.3 = (f32[64,1664]{1,0:T(8,128)}, f32[3,1664]{1,0:T(4,128)}, bf16[512,1664]{1,0:T(8,128)(2,1)}, bf16[400,1664]{1,0:T(8,128)(2,1)}) custom-call(bf16[512,1664]{1,0:T(8,128)(2,1)} %convolution_convert_fusion.7.refs_0_, f32[64,1664]{1,0:T(8,128)} %get-tuple-element.86.refs_1_, f32[64,1664]{1,0:T(8,128)} %get-tuple-element.105.refs_2_, ...), custom_call_target="tpu_custom_call" | custom-call | tf_op jit(solution)/shard_map/phase_resid/pallas_call | solution.py:776
  640.0 2.8 convolution_convert_fusion.16.refs_2_
  642.9 9.3 %attend_back.3 = bf16[512,768]{1,0:T(8,128)(2,1)} custom-call(bf16[512,768]{1,0:T(8,128)(2,1)} %add_convert_fusion.1.own_ref.refs_0_, bf16[512,512]{1,0:T(8,128)(2,1)} %get-tuple-element.104.refs_1_, bf16[512,256]{1,0:T(8,128)(2,1)} %convolution_convert_fusion.16.refs_2_, f32[256,512]{1,0:T(8,128)} %get-tuple-element.108.refs_3_, ...), custom_call_target="tpu_custom_call" | custom-call | tf_op jit(solution)/shard_map/attend_back/pallas_call | solution.py:981
  652.2 4.1 convolution_convert_fusion.6.refs_0_
  658.1 38.5 %phase_first.1 = (f32[64,1664]{1,0:T(8,128)}, f32[3,1664]{1,0:T(4,128)}, bf16[4,208,800]{2,1,0:T(8,128)(2,1)}) custom-call(bf16[512,1664]{1,0:T(8,128)(2,1)} %convolution_convert_fusion.6.refs_0_, f32[64,1664]{1,0:T(8,128)} %convert_element_type.227.refs_1_, f32[64,1664]{1,0:T(8,128)} %get-tuple-element.110.refs_2_, f32[1,1664]{1,0:T(1,128)} %reshape.294.refs_3_, ...), custom_call_target="tpu_custom_call" | custom-call | tf_op jit(solution)/shard_map/phase_first/pallas_call | solution.py:776
  696.7 3.3 select_convert_fusion.refs_0_
  701.8 4.0 convolution_convert_fusion.5
  713.5 6.9 fold.6
  720.5 7.0 fold.7
  727.6 3.0 broadcast_select_fusion
  731.6 74.0 %finish.1 = (bf16[8,208,800]{2,1,0:T(8,128)(2,1)}, bf16[800,1664]{1,0:T(8,128)(2,1)}, bf16[8,208,768]{2,1,0:T(8,128)(2,1)}, bf16[256,1664]{1,0:T(8,128)(2,1)}, f...) custom-call(bf16[4,208,800]{2,1,0:T(8,128)(2,1)} %select_convert_fusion.refs_0_, ...), custom_call_target="tpu_custom_call" | custom-call | tf_op jit(solution)/shard_map/finish/pallas_call | solution.py:1171
  805.6 2.2 convert_select_fusion.1
  817.3 10.7 %settle.1 = (f32[200,4800]{1,0:T(8,128)}, f32[200,6400]{1,0:T(8,128)}, f32[200,1600]{1,0:T(8,128)}, f32[800,1600]{1,0:T(8,128)}) custom-call(bf16[8,208,768]{2,1,0:T(8,128)(2,1)} %get-tuple-element.126.qkv_ref, bf16[8,208,800]{2,1,0:T(8,128)(2,1)} %get-tuple-element.127.widen_ref, bf16[256,1664]{1,0:T(8,128)(2,1)} %get-tuple-element.128.out_ref, ...), custom_call_target="tpu_custom_call" | custom-call | tf_op jit(solution)/shard_map/settle/pallas_call | solution.py:641
  (304 shorter events, 57.8 us)
Async XLA Ops:
  0.6 11.3 %copy-start.35 = (bf16[2,64,1600]{2,1,0:T(8,128)(2,1)S(1)}, bf16[2,64,1600]{2,1,0:T(8,128)(2,1)}, u32[]{:S(2)}) copy-start(bf16[2,64,1600]{2,1,0:T(8,128)(2,1)} %param.18) | copy-start | bytes 1228804
  12.0 2.5 copy-start.15
  12.8 12.1 %copy-start.16 = (bf16[64,1664]{1,0:T(8,128)(2,1)}, bf16[64,1664]{1,0:T(8,128)(2,1)S(1)}, u32[]{:S(2)}) copy-start(bf16[64,1664]{1,0:T(8,128)(2,1)S(1)} %reshape.287.carried) | copy-start | bytes 638980
  90.7 2.0 copy-start
  90.7 2.7 copy-start.34
  93.3 13.6 %copy-start.44 = (f32[512]{0:T(512)}, f32[512]{0:T(512)S(1)}, u32[]{:S(2)}) copy-start(f32[512]{0:T(512)S(1)} %add_rsqrt_fusion) | copy-start | bytes 6148
  101.8 5.1 copy-start.40
  102.6 4.3 copy-start.41
  169.9 3.4 copy-start.17
  169.9 3.4 copy-start.30
  173.3 88.6 %copy-start.9 = (bf16[1,8,208,800]{3,2,1,0:T(8,128)(2,1)}, bf16[1,8,208,800]{3,2,1,0:T(8,128)(2,1)S(1)}, u32[]{:S(2)}) copy-start(bf16[1,8,208,800]{3,2,1,0:T(8,128)(2,1)S(1)} %get-tuple-element.135) | copy-start | bytes 7987204
  261.9 4.5 copy-start.46
  266.4 54.5 %copy-start.13 = (bf16[1,8,208,768]{3,2,1,0:T(8,128)(2,1)S(1)}, bf16[1,8,208,768]{3,2,1,0:T(8,128)(2,1)}, u32[]{:S(2)}) copy-start(bf16[1,8,208,768]{3,2,1,0:T(8,128)(2,1)} %get-tuple-element.136) | copy-start | bytes 7667716
  394.9 3.3 copy-start.48
  398.1 4.9 copy-start.52
  403.1 3.3 copy-start.49
  409.5 21.2 %slice-start = ((s8[5324800]{0:T(1024)(128)(4,1)}), s8[1130496]{0:T(1024)(128)(4,1)S(1)}, s32[]{:S(2)}) async-start(s8[5324800]{0:T(1024)(128)(4,1)} %bitcast.298), calls=%async_computation | async-start | bytes 2260992
  415.1 15.6 %slice-start.1 = ((s8[5324800]{0:T(1024)(128)(4,1)}), s8[4194304]{0:T(1024)(128)(4,1)S(1)}, s32[]{:S(2)}) async-start(s8[5324800]{0:T(1024)(128)(4,1)} %bitcast.298), calls=%async_computation.1 | async-start | bytes 8388608
  435.7 45.6 %copy-start.18 = (bf16[2,256,1664]{2,1,0:T(8,128)(2,1)S(1)}, bf16[2,256,1664]{2,1,0:T(8,128)(2,1)}, u32[]{:S(2)}) copy-start(bf16[2,256,1664]{2,1,0:T(8,128)(2,1)} %get-tuple-element.81) | copy-start | bytes 5111812
  484.2 25.4 %copy-start.21 = (bf16[512,1664]{1,0:T(8,128)(2,1)S(1)}, bf16[512,1664]{1,0:T(8,128)(2,1)}, u32[]{:S(2)}) copy-start(bf16[512,1664]{1,0:T(8,128)(2,1)} %get-tuple-element.95) | copy-start | bytes 5111812
  484.2 25.4 %copy-start.32 = (bf16[512,256]{1,0:T(8,128)(2,1)S(1)}, bf16[512,256]{1,0:T(8,128)(2,1)}, u32[]{:S(2)}) copy-start(bf16[512,256]{1,0:T(8,128)(2,1)} %get-tuple-element.91) | copy-start | bytes 786436
  511.3 4.1 copy-start.33
  511.3 4.3 copy-start.47
  518.9 42.0 %copy-start.43 = (f32[8,2,1600]{2,1,0:T(2,128)}, f32[8,2,1600]{2,1,0:T(2,128)S(1)}, u32[]{:S(2)}) copy-start(f32[8,2,1600]{2,1,0:T(2,128)S(1)} %constant_dynamic-update-slice_fusion.24) | copy-start | bytes 307204
  518.9 42.0 %copy-start.51 = (f32[512,800]{0,1:T(8,128)S(1)}, f32[512,800]{0,1:T(8,128)}, u32[]{:S(2)}) copy-start(f32[512,800]{0,1:T(8,128)} %copy-done.50) | copy-start | bytes 4915204
  560.9 5.0 copy-start.10
  565.9 3.4 copy-start.53
  565.9 3.4 copy-start.39
  565.9 3.6 copy-start.45
  595.7 44.3 %copy-start.19 = (bf16[2,256,1664]{2,1,0:T(8,128)(2,1)S(1)}, bf16[2,256,1664]{2,1,0:T(8,128)(2,1)}, u32[]{:S(2)}) copy-start(bf16[2,256,1664]{2,1,0:T(8,128)(2,1)} %get-tuple-element.81) | copy-start | bytes 5111812
  642.9 9.3 %copy-start.12 = (bf16[1,8,208,768]{3,2,1,0:T(8,128)(2,1)S(1)}, bf16[1,8,208,768]{3,2,1,0:T(8,128)(2,1)}, u32[]{:S(2)}) copy-start(bf16[1,8,208,768]{3,2,1,0:T(8,128)(2,1)} %copy-done.11) | copy-start | bytes 7667716
  652.2 4.1 copy-start.4
  652.2 4.1 copy-start.5
  652.2 4.1 copy-start.27
  652.2 4.1 copy-start.28
  656.3 40.3 %copy-start.26 = (bf16[4,208,800]{2,1,0:T(8,128)(2,1)S(1)}, bf16[4,208,800]{2,1,0:T(8,128)(2,1)}, u32[]{:S(2)}) copy-start(bf16[4,208,800]{2,1,0:T(8,128)(2,1)} %get-tuple-element.112) | copy-start | bytes 3993604
  658.1 38.6 %copy-start.2 = (bf16[4,208,800]{2,1,0:T(8,128)(2,1)S(1)}, bf16[4,208,800]{2,1,0:T(8,128)(2,1)}, u32[]{:S(2)}) copy-start(bf16[4,208,800]{2,1,0:T(8,128)(2,1)} %get-tuple-element.101.refs_5_) | copy-start | bytes 3993604
  658.1 38.6 %copy-start.3 = (bf16[4,208,800]{2,1,0:T(8,128)(2,1)S(1)}, bf16[4,208,800]{2,1,0:T(8,128)(2,1)}, u32[]{:S(2)}) copy-start(bf16[4,208,800]{2,1,0:T(8,128)(2,1)} %get-tuple-element.103.refs_5_) | copy-start | bytes 3993604
  696.7 3.3 copy-start.8
  696.7 3.5 copy-start.38
  696.7 3.5 copy-start.42
  705.8 3.9 copy-start.1
  705.8 3.9 copy-start.6
  705.8 3.9 copy-start.22
  705.8 3.9 copy-start.23
  720.5 7.0 copy-start.29
  727.5 3.0 copy-start.36
  727.6 3.0 copy-start.37
  (8 other events, 11.8 us)

commit v2 on v1

v2 whole, which is shorter than its diff:
```python
import functools

import jax
import jax.numpy as jnp
import numpy as np
from jax import lax
from jax.experimental import pallas as pl
from jax.experimental.pallas import tpu as pltpu
from jax.sharding import PartitionSpec as P

HEADS = 25
HD = 64
EPSILON = 1e-05
MASKED = -1e30
LOG2E = 1.4426950408889634
GELU_A = 0.7978845608028654
GELU_B = 0.044715
MESH = pl.DeviceIdType.MESH
F32 = jnp.float32
BF16 = jnp.bfloat16
VMEM_SPEC = pl.BlockSpec(memory_space=pltpu.VMEM)
ANY_SPEC = pl.BlockSpec(memory_space=pl.ANY)
DMA = pltpu.SemaphoreType.DMA
VMEM_LIMIT = 60 * 2**20
HALVES = 2


def params(collective_id=None):
    if collective_id is None:
        return pltpu.CompilerParams(vmem_limit_bytes=VMEM_LIMIT)
    return pltpu.CompilerParams(
        collective_id=collective_id, has_side_effects=True, vmem_limit_bytes=VMEM_LIMIT
    )


def remote(src, dst, send_sem, recv_sem, device):
    return pltpu.make_async_remote_copy(
        src_ref=src,
        dst_ref=dst,
        send_sem=send_sem,
        recv_sem=recv_sem,
        device_id=device,
        device_id_type=MESH,
    )


class Place:
    def __init__(self, n):
        self.s = lax.axis_index("section")
        self.c = lax.axis_index("ctx")
        self.h = lax.axis_index("shard")
        self.n = n
        self.zn = n // 2
        self.y = lax.rem(self.h, 2)
        self.z = lax.div(self.h, 2)
        self.far_y = self.y + self.c - 2 * self.y * self.c

    def flip(self, k):
        found = self.z
        for bit in range(self.zn.bit_length()):
            if k >> bit & 1:
                found = found + (1 - 2 * lax.rem(self.z // 2**bit, 2)) * 2**bit
        return found

    def dev(self, z, y):
        return (self.s, self.c, z * 2 + y)

    @property
    def pair(self):
        return self.dev(self.z, 1 - self.y)

    @property
    def above(self):
        return self.dev(self.z + 1, self.y)

    @property
    def below(self):
        return self.dev(self.z - 1, self.y)

    @property
    def over(self):
        return (1 - self.s, self.c, self.h)

    @property
    def sibling(self):
        return (self.s, 1 - self.c, self.h)


def greet(p, line=False, spread=False, over=False, sibling=False):
    bar = pltpu.get_barrier_semaphore()
    peers = 0

    def signal(device):
        pl.semaphore_signal(bar, inc=1, device_id=device, device_id_type=MESH)

    if line:
        signal(p.pair)

        @pl.when(p.z < p.zn - 1)
        def _():
            signal(p.above)

        @pl.when(p.z > 0)
        def _():
            signal(p.below)

        peers = 1 + (p.z + p.zn - 1) // p.zn + (2 * p.zn - 2 - p.z) // p.zn
    if spread:
        for dz in range(1, p.zn):
            signal(p.dev(lax.rem(p.z + dz, p.zn), p.far_y))

        @pl.when(p.c == 1)
        def _():
            signal(p.dev(p.z, p.far_y))

        peers = peers + p.zn - 1 + p.c
    if over:
        signal(p.over)
        peers = peers + 1
    if sibling:
        signal(p.sibling)
        peers = peers + 1
    pl.semaphore_wait(bar, peers)


class Gather:
    def __init__(self, p, own_ref, out_ref, ss, rs, ls):
        self.p, self.own_ref, self.out_ref = p, own_ref, out_ref
        self.ss, self.rs, self.ls = ss, rs, ls
        self.hr = own_ref.shape[0] // HALVES

    def blk(self, half, zz, yy):
        row = (half * self.p.n + zz * 2 + yy) * self.hr
        return self.out_ref.at[pl.ds(pl.multiple_of(row, 16), self.hr)]

    def own(self, half):
        return self.own_ref.at[pl.ds(half * self.hr, self.hr)]

    def up(self, t, half, src):
        p = self.p
        sems = (self.ss.at[0, t, half], self.rs.at[0, t, half])
        return remote(src, self.blk(half, p.z - (t - 1), p.y), *sems, p.above)

    def down(self, t, half, src):
        p = self.p
        sems = (self.ss.at[1, t, half], self.rs.at[1, t, half])
        return remote(src, self.blk(half, p.z + (t - 1), p.y), *sems, p.below)

    def across(self, kind, t, half, zz, src):
        p = self.p
        sems = (self.ss.at[2 + kind, t, half], self.rs.at[2 + kind, t, half])
        return remote(src, self.blk(half, zz, p.y), *sems, p.pair)

    def local(self, half):
        p = self.p
        return pltpu.make_async_copy(
            self.own(half), self.blk(half, p.z, p.y), self.ls.at[half]
        )

    def start(self, halves=range(HALVES)):
        p = self.p
        for half in halves:
            src = self.own(half)

            @pl.when(p.z < p.zn - 1)
            def _():
                self.up(1, half, src).start()

            @pl.when(p.z > 0)
            def _():
                self.down(1, half, src).start()

            self.across(0, 0, half, p.z, src).start()
            self.local(half).start()

    def step(self, t, half):
        p = self.p
        z, zn = p.z, p.zn

        @pl.when(z >= t)
        def _():
            block = self.blk(half, z - t, p.y)
            self.up(t, half, block).wait_recv()
            if t < zn - 1:

                @pl.when(z < zn - 1)
                def _():
                    self.up(t + 1, half, block).start()

            self.across(0, t, half, z - t, block).start()

        @pl.when(z <= zn - 1 - t)
        def _():
            block = self.blk(half, z + t, p.y)
            self.down(t, half, block).wait_recv()
            if t < zn - 1:

                @pl.when(z > 0)
                def _():
                    self.down(t + 1, half, block).start()

            self.across(1, t, half, z + t, block).start()

    def steps(self):
        return [
            functools.partial(self.step, t, half)
            for t in range(1, self.p.zn)
            for half in range(HALVES)
        ]

    def finish(self):
        p = self.p
        z, zn = p.z, p.zn
        for half in range(HALVES):
            self.across(0, 0, half, z, self.own(half)).wait_recv()
            for t in range(1, zn):

                @pl.when(z >= t)
                def _():
                    self.across(0, t, half, z - t, self.own(half)).wait_recv()

                @pl.when(z <= zn - 1 - t)
                def _():
                    self.across(1, t, half, z + t, self.own(half)).wait_recv()

        for half in range(HALVES):
            self.local(half).wait()
            self.across(0, 0, half, z, self.own(half)).wait_send()
            for t in range(1, zn):

                @pl.when((z < zn - 1) & (z >= t - 1))
                def _():
                    self.up(t, half, self.own(half)).wait_send()

                @pl.when((z > 0) & (z <= zn - t))
                def _():
                    self.down(t, half, self.own(half)).wait_send()

                @pl.when(z >= t)
                def _():
                    self.across(0, t, half, z - t, self.own(half)).wait_send()

                @pl.when(z <= zn - 1 - t)
                def _():
                    self.across(1, t, half, z + t, self.own(half)).wait_send()


class Scatter:
    def __init__(self, p, part_ref, ybuf, rbuf, sbuf, ss, rs):
        self.p, self.part_ref = p, part_ref
        self.ybuf, self.rbuf, self.sbuf, self.ss, self.rs = ybuf, rbuf, sbuf, ss, rs
        self.hr = ybuf.shape[2]

    def blk(self, half, zz, yy):
        row = (half * self.p.n + zz * 2 + yy) * self.hr
        return self.part_ref.at[pl.ds(pl.multiple_of(row, 16), self.hr)]

    def goal(self, k, t):
        return self.p.z + t if k == 0 else self.p.z - t

    def across(self, k, t, half):
        p = self.p
        zz = self.goal(k, t)
        sems = (self.ss.at[k, t, half], self.rs.at[k, t, half])
        return remote(self.blk(half, zz, 1 - p.y), self.ybuf.at[zz, half], *sems, p.pair)

    def along(self, k, t, half, slot):
        p = self.p
        zz = self.goal(k, t)
        sems = (self.ss.at[2 + k, t, half], self.rs.at[2 + k, slot, half])
        target = p.above if k == 0 else p.below
        return remote(self.sbuf.at[zz, half], self.rbuf.at[zz + 1 - k, half], *sems, target)

    def ok(self, k, t):
        return self.p.z <= self.p.zn - 1 - t if k == 0 else self.p.z >= t

    def has(self, k):
        return self.p.z > 0 if k == 0 else self.p.z < self.p.zn - 1

    def start(self):
        for t in range(self.p.zn - 1, 0, -1):
            for half in range(HALVES):
                for k in range(2):

                    @pl.when(self.ok(k, t))
                    def _():
                        self.across(k, t, half).start()

        for half in range(HALVES):
            self.across(0, 0, half).start()

    def step(self, t, half, k):
        p = self.p
        zz = self.goal(k, t)

        @pl.when(self.ok(k, t))
        def _():
            self.across(k, t, half).wait_recv()
            total = self.blk(half, zz, p.y)[...].astype(F32)
            total = total + self.ybuf[zz, half].astype(F32)
            if t < p.zn - 1:

                @pl.when(self.has(k))
                def _():
                    self.along(k, t, half, t).wait_recv()
                    more = total + self.rbuf[zz + 1 - k, half].astype(F32)
                    self.sbuf[zz, half] = more.astype(BF16)

                @pl.when(jnp.logical_not(self.has(k)))
                def _():
                    self.sbuf[zz, half] = total.astype(BF16)

            else:
                self.sbuf[zz, half] = total.astype(BF16)
            self.along(k, t, half, t - 1).start()

    def steps(self):
        return [
            functools.partial(self.step, t, half, k)
            for t in range(self.p.zn - 1, 0, -1)
            for half in range(HALVES)
            for k in range(2)
        ]

    def result(self, half):
        p = self.p
        z = p.z
        self.across(0, 0, half).wait_recv()
        for k in range(2):

            @pl.when(self.has(k))
            def _():
                self.along(k, 0, half, 0).wait_recv()

            @pl.when(jnp.logical_not(self.has(k)))
            def _():
                self.rbuf[z + 1 - k, half] = jnp.zeros(self.rbuf.shape[2:], BF16)

        total = self.blk(half, z, p.y)[...].astype(F32) + self.ybuf[z, half].astype(F32)
        return total + self.rbuf[z + 1, half].astype(F32) + self.rbuf[z, half].astype(F32)

    def finish(self):
        for half in range(HALVES):
            self.across(0, 0, half).wait_send()
            for t in range(1, self.p.zn):
                for k in range(2):

                    @pl.when(self.ok(k, t))
                    def _():
                        self.across(k, t, half).wait_send()
                        self.along(k, t, half, t - 1).wait_send()


class Spread:
    def __init__(self, p, src, dst, ss, rs, ls):
        self.p, self.src, self.dst, self.ss, self.rs, self.ls = p, src, dst, ss, rs, ls

    def source(self, dz):
        return self.p.flip(dz) * 2 + self.p.far_y

    def out(self, dz):
        p = self.p
        target = self.source(dz)
        sems = (self.ss.at[0, dz], self.rs.at[0, dz])
        return remote(self.src.at[target], self.dst.at[p.s, p.h], *sems, (p.s, p.c, target))

    def aside(self, dz):
        block = self.dst.at[self.p.s, self.source(dz)]
        return remote(block, block, self.ss.at[1, dz], self.rs.at[1, dz], self.p.sibling)

    def cross(self, dz):
        block = self.dst.at[self.p.s, self.source(dz)]
        return remote(block, block, self.ss.at[2, dz], self.rs.at[2, dz], self.p.over)

    def cross_own(self):
        p = self.p
        sems = (self.ss.at[2, 0], self.rs.at[2, 0])
        return remote(self.src.at[p.h], self.dst.at[p.s, p.h], *sems, p.over)

    def cross_aside(self, dz):
        block = self.dst.at[1 - self.p.s, self.source(dz)]
        return remote(block, block, self.ss.at[3, dz], self.rs.at[3, dz], self.p.sibling)

    def local(self):
        p = self.p
        return pltpu.make_async_copy(self.src.at[p.h], self.dst.at[p.s, p.h], self.ls)

    def start(self):
        @pl.when(self.p.c == 1)
        def _():
            self.out(0).start()

        @pl.when(self.p.c == 0)
        def _():
            self.cross_own().start()

        for dz in range(1, min(3, self.p.zn)):
            self.out(dz).start()
        self.local().start()

    def arrived(self, dz):
        if 3 <= dz + 2 < self.p.zn:
            self.out(dz + 1).wait_send()
            self.out(dz + 2).start()
        self.out(dz).wait_recv()
        self.cross(dz).start()
        self.aside(dz).start()

    def crossed(self, dz):
        self.cross(dz).wait_recv()
        self.cross_aside(dz).start()

    def first(self):
        @pl.when(self.p.c == 1)
        def _():
            self.arrived(0)

    def steps(self):
        found = [self.first]
        found += [functools.partial(self.arrived, dz) for dz in range(1, self.p.zn)]
        return found + [functools.partial(self.crossed, dz) for dz in range(self.p.zn)]

    def finish(self):
        self.local().wait()

        @pl.when(self.p.c == 0)
        def _():
            self.aside(0).wait_recv()
            self.cross_own().wait_send()

        @pl.when(self.p.c == 1)
        def _():
            self.out(0).wait_send()
            self.aside(0).wait_send()
            self.cross(0).wait_send()

        for dz in range(self.p.zn):
            if dz:
                self.aside(dz).wait_recv()
                self.aside(dz).wait_send()
                if dz == 1 or dz == self.p.zn - 1:
                    self.out(dz).wait_send()
                self.cross(dz).wait_send()
            self.cross_aside(dz).wait_recv()
            self.cross_aside(dz).wait_send()


class RowSwap:
    def __init__(self, p, src, dst, ss, rs, ls):
        self.p, self.src, self.dst, self.ss, self.rs, self.ls = p, src, dst, ss, rs, ls
        self.split = src.shape[0] % 32 == 0

    def piece(self, which):
        count = self.src.shape[0]
        if not self.split:
            return self.src, self.dst.at[which, pl.ds(0, count)]
        half = count // 2
        rows = pl.ds(pl.multiple_of(self.p.c * half, 16), half)
        return self.src.at[rows], self.dst.at[which, rows]

    def cross(self):
        src, dst = self.piece(self.p.s)
        return remote(src, dst, self.ss.at[0], self.rs.at[0], self.p.over)

    def aside(self):
        block = self.piece(1 - self.p.s)[1]
        return remote(block, block, self.ss.at[1], self.rs.at[1], self.p.sibling)

    def local(self):
        rows = pl.ds(0, self.src.shape[0])
        return pltpu.make_async_copy(self.src, self.dst.at[self.p.s, rows], self.ls)

    def start(self):
        self.cross().start()
        self.local().start()

    def step(self):
        self.cross().wait_recv()
        if self.split:
            self.aside().start()

    def finish(self):
        self.local().wait()
        self.cross().wait_send()
        if self.split:
            self.aside().wait_recv()
            self.aside().wait_send()


class Cross:
    def __init__(self, p, src, dst, ss, rs, source):
        self.p, self.source = p, source
        self.copy = remote(src, dst, ss, rs, p.over)

    def start(self):
        @pl.when(self.p.s == self.source)
        def _():
            self.copy.start()

    def finish(self):
        @pl.when(self.p.s == self.source)
        def _():
            self.copy.wait_send()

        @pl.when(self.p.s != self.source)
        def _():
            self.copy.wait_recv()


class Fold:
    def __init__(self, p, src, came, out, ss, rs):
        self.p, self.src, self.came, self.out, self.ss, self.rs = p, src, came, out, ss, rs
        self.count = out.shape[0]
        self.size = out.shape[1]

    def rows(self, item, near):
        p = self.p
        if self.count == 1:
            index = 1 - p.c if near else p.c
        else:
            index = item * 2 + (1 - p.far_y if near else p.far_y)
        return pl.ds(pl.multiple_of(index * self.size, 16), self.size)

    def copy(self, item):
        src = self.src.at[self.rows(item, True)]
        sems = (self.ss.at[item], self.rs.at[item])
        return remote(src, self.came.at[item], *sems, self.p.sibling)

    def start(self):
        for item in range(self.count):
            self.copy(item).start()

    def step(self, item):
        self.copy(item).wait_recv()
        own = self.src[self.rows(item, False)].astype(F32)
        self.out[item] = (own + self.came[item].astype(F32)).astype(BF16)

    def steps(self):
        return [functools.partial(self.step, item) for item in range(self.count)]

    def finish(self):
        for item in range(self.count):
            self.copy(item).wait_send()


def fold_scratch(source, out):
    return [pltpu.VMEM(source, BF16), pltpu.VMEM(out, BF16), DMA((out[0],)), DMA((out[0],))]


def product(a_ref, b_ref, to_ref):
    rows = to_ref.shape[0]

    def step(first, size):
        found = lax.dot_general(
            a_ref[:, first : first + size],
            b_ref[...],
            (((0,), (0,)), ((), ())),
            preferred_element_type=F32,
        )
        to_ref[first : first + size] = found.astype(BF16)

    return [
        functools.partial(step, first, min(256, rows - first)) for first in range(0, rows, 256)
    ]


def home_rows(a_ref, b_ref, to_ref, low, share):
    found = lax.dot_general(
        a_ref[...], b_ref[...], (((0,), (0,)), ((), ())), preferred_element_type=F32
    )
    h = lax.axis_index("shard")
    shift = 0
    for j, first in enumerate(low):
        shift = shift + jnp.where(h == j, (HD * first - j * share) % found.shape[0], 0)
    to_ref[...] = pltpu.roll(found, shift, 0).astype(BF16)


def in_turn(steps, work, each=1):
    for step in steps:
        for _ in range(each):
            run_next(work)
        step()


def by_halves(scatter, gather, rows_step, work, each=1):
    in_turn(scatter.steps(), work, each)
    for half in range(HALVES):
        rows_step(half)
        if gather is not None:
            gather.start([half])
    if gather is not None:
        in_turn(gather.steps(), work, each)


def fetch(src, dst, sem):
    copy = pltpu.make_async_copy(src, dst, sem)
    copy.start()
    return copy


def row_blocks(rows, step):
    size = min(rows, 256)
    count = rows // size
    if count <= 2:
        for b in range(count):
            step(b * size, size)
    else:

        def body(b, carry):
            step(pl.multiple_of(b * size, size), size)
            return carry

        lax.fori_loop(0, count, body, 0)


def gelu_parts(values):
    square = values * values
    return jnp.tanh(GELU_A * (values + GELU_B * values * square)), square


def greet_all(p):
    bar = pltpu.get_barrier_semaphore()
    for a in range(2):
        for b in range(p.n):
            if (a, b) != (0, 0):
                other = (lax.rem(p.s + a, 2), p.c, lax.rem(p.h + b, p.n))
                pl.semaphore_signal(bar, inc=1, device_id=other, device_id_type=MESH)
    pl.semaphore_signal(bar, inc=1, device_id=p.sibling, device_id_type=MESH)
    pl.semaphore_wait(bar, 2 * p.n)


def others(n):
    return [(a, b) for a in range(2) for b in range(n) if (a, b) != (0, 0)]


def start_kernel(n, low, width, tok_ref, pack_ref, qkv_ref, out_ref, mask_ref, *refs):
    normed_to, found_to, qkv_all, out_all, feats_to, qkv_bias, widen_bias = refs[:7]
    tok_all, pack_all, g_ss, g_rs, g_ls, p_ss, p_rs, a_ss, a_rs, o_ss, o_rs, l_sem = refs[7:]
    p = Place(n)
    s, c, h = p.s, p.c, p.h
    greet_all(p)

    def pack_copy(a, b):
        target = (lax.rem(s + a, 2), c, lax.rem(h + b, n))
        return remote(pack_ref, pack_all.at[s, h], p_ss.at[a, b], p_rs.at[a, b], target)

    tokens = Gather(p, tok_ref, tok_all, g_ss, g_rs, g_ls)
    qkv = Spread(p, qkv_ref, qkv_all, a_ss, a_rs, l_sem.at[1])
    out = RowSwap(p, out_ref, out_all, o_ss, o_rs, l_sem.at[2])
    pack_own = pltpu.make_async_copy(pack_ref, pack_all.at[s, h], l_sem.at[0])
    tokens.start()
    qkv.start()
    for a, b in others(n):
        pack_copy(a, b).start()
    pack_own.start()
    out.start()
    qkv_steps = qkv.steps()
    for step in tokens.steps():
        step()
        if qkv_steps:
            qkv_steps.pop(0)()
    tokens.finish()
    pack_own.wait()
    for a, b in others(n):
        pack_copy(a, b).wait_recv()
    sh = qkv_ref.shape[2] // 3
    share = width // n
    padded = qkv_ref.shape[1]
    for layer in range(2):
        pieces = [pack_all[layer, j] for j in range(n)]
        feats_to[layer] = jnp.concatenate([m[:, :padded] for m in pieces], axis=1).astype(F32)
        bias = jnp.concatenate([m[6:7, : 2 * share] for m in pieces], axis=1).astype(F32)
        found = jnp.zeros((1, 2 * sh), F32)
        wide = jnp.zeros((1, widen_bias.shape[2]), F32)
        for j in range(n):
            first = HD * low[j]
            spots = [bias[:, k * width + first : k * width + first + sh] for k in range(2)]
            found = jnp.where(h == j, jnp.concatenate(spots, axis=1), found)
            own = pieces[j][7:8, : wide.shape[1]].astype(F32)
            wide = jnp.where(h == j, own, wide)
        qkv_bias[layer] = jnp.concatenate(
            [found[:, :sh], jnp.zeros((1, sh), F32), found[:, sh:]], axis=1
        )
        widen_bias[layer] = wide
    unit = unit_rows(tok_all[...].astype(F32), mask_ref[...], width)[0]
    normed_to[...] = (unit * feats_to[0, 0:1] + feats_to[0, 1:2]).astype(BF16)
    for step in qkv_steps:
        step()
    out.step()
    qkv.finish()
    weight = qkv_all[0].reshape(n * padded, 3 * sh)
    found_to[...] = (dot_n(normed_to[...], weight) + qkv_bias[0]).astype(BF16)
    for a, b in others(n):
        pack_copy(a, b).wait_send()
    out.finish()


def start_call(n, low, width, hide, tok, pack, qkv, out, mask):
    rows, full = tok.shape
    zn = n // 2
    shapes = [
        jax.ShapeDtypeStruct((n * rows, full), BF16),
        jax.ShapeDtypeStruct((n * rows, qkv.shape[2]), BF16),
        jax.ShapeDtypeStruct((2,) + qkv.shape, BF16),
        jax.ShapeDtypeStruct((2,) + out.shape, BF16),
        jax.ShapeDtypeStruct((2, 16, full), F32),
        jax.ShapeDtypeStruct((2, 1, qkv.shape[2]), F32),
        jax.ShapeDtypeStruct((2, 1, hide), F32),
    ]
    return pl.pallas_call(
        functools.partial(start_kernel, n, low, width),
        out_shape=shapes,
        in_specs=[VMEM_SPEC] * 5,
        out_specs=[VMEM_SPEC] * 7,
        scratch_shapes=[
            pltpu.VMEM((n * rows, full), BF16),
            pltpu.VMEM((2, n) + pack.shape, BF16),
            DMA((4, zn, HALVES)),
            DMA((4, zn, HALVES)),
            DMA((HALVES,)),
            DMA((2, n)),
            DMA((2, n)),
            DMA((4, zn)),
            DMA((4, zn)),
            DMA((2,)),
            DMA((2,)),
            DMA((3,)),
        ],
        compiler_params=params(0),
        name="start",
    )(tok, pack, qkv, out, mask)


def with_gaps(values, n, padded):
    rows, width = values.shape
    share = width // n
    pieces = []
    for j in range(n):
        pieces.append(values[:, j * share : (j + 1) * share])
        if padded > share:
            pieces.append(jnp.zeros((rows, padded - share), values.dtype))
    return jnp.concatenate(pieces, axis=1)


def lay_out_kernel(low, qkv_ref, widen_ref, out_ref, narrow_ref, tok_ref, cot_ref, *refs):
    vectors, outs = refs[:8], refs[8:]
    qkv_to, widen_to, out_to, narrow_to, pack_to, tok_to, x_to, cot_to, grad_to, sums_to = outs
    n, padded, hide_full = widen_to.shape
    share, hidden = widen_ref.shape
    hide = hidden // n
    width = qkv_ref.shape[1] // 3
    sh = qkv_to.shape[2] // 3
    gap = padded - share
    s = lax.axis_index("section")
    h = lax.axis_index("shard")
    for j in range(n):
        for t in range(3):
            first = t * width + HD * low[j]
            qkv_to[j, :share, t * sh : (t + 1) * sh] = qkv_ref[:, first : first + sh]
        widen_to[j, :share, :hide] = widen_ref[:, j * hide : (j + 1) * hide]
        if hide_full > hide:
            widen_to[j, :share, hide:] = jnp.zeros((share, hide_full - hide), BF16)
        if gap:
            qkv_to[j, share:] = jnp.zeros((gap, 3 * sh), BF16)
            widen_to[j, share:] = jnp.zeros((gap, hide_full), BF16)
    narrow_to[:hide] = with_gaps(narrow_ref[...], n, padded)
    extra = narrow_to.shape[0] - hide
    if extra:
        narrow_to[hide:] = jnp.zeros((extra, n * padded), BF16)
    offset = 0
    for j in range(n):
        offset = offset + jnp.where(h == j, j * share - HD * low[j], 0)
    rows = with_gaps(out_ref[...].astype(F32), n, padded)
    rows = jnp.concatenate([rows, jnp.zeros((sh - share, n * padded), F32)], axis=0)
    out_to[...] = pltpu.roll(rows, offset, 0).astype(BF16)
    lanes = pack_to.shape[1]
    members = []
    for ref in vectors:
        member = ref[...].astype(F32)
        members.append(
            jnp.concatenate([member, jnp.zeros((1, lanes - member.shape[1]), F32)], axis=1)
        )
    members.append(jnp.zeros((8, lanes), F32))
    pack_to[...] = jnp.concatenate(members, axis=0).astype(BF16)
    for ref, low_to, full_to in ((tok_ref, tok_to, x_to), (cot_ref, cot_to, grad_to)):
        values = with_gaps(ref[s], n, padded)
        low_to[...] = values
        full_to[...] = values.astype(F32)
    sums_to[...] = jnp.sum(grad_to[...], axis=0, keepdims=True)


def lay_out_call(low, slots, padded, qkv, widen, out, narrow, tokens, cotangent, *vectors):
    n = len(low)
    share, hidden = widen.shape
    sh = slots * HD
    full = n * padded
    rows = tokens.shape[1]
    lanes = max(-(-hidden // n // 128) * 128, -(-2 * share // 128) * 128)
    return pl.pallas_call(
        functools.partial(lay_out_kernel, low),
        out_shape=[
            jax.ShapeDtypeStruct((n, padded, 3 * sh), BF16),
            jax.ShapeDtypeStruct((n, padded, -(-hidden // n // 128) * 128), BF16),
            jax.ShapeDtypeStruct((sh, full), BF16),
            jax.ShapeDtypeStruct((-(-narrow.shape[0] // 16) * 16, full), BF16),
            jax.ShapeDtypeStruct((16, lanes), BF16),
            jax.ShapeDtypeStruct((rows, full), BF16),
            jax.ShapeDtypeStruct((rows, full), F32),
            jax.ShapeDtypeStruct((rows, full), BF16),
            jax.ShapeDtypeStruct((rows, full), F32),
            jax.ShapeDtypeStruct((1, full), F32),
        ],
        in_specs=[VMEM_SPEC] * (6 + len(vectors)),
        out_specs=[VMEM_SPEC] * 10,
        compiler_params=params(),
        name="lay_out",
    )(qkv, widen, out, narrow, tokens, cotangent, *vectors)


def settle_kernel(low, sizes, qkv_ref, widen_ref, out_ref, narrow_ref, vec_ref, came_ref, *refs):
    streams, (qkv_to, widen_to, out_to, narrow_to, *outs) = refs[:4], refs[4:]
    stream_to, vectors = outs[:2], outs[2:]
    n, padded, _ = widen_ref.shape
    share = out_to.shape[0]
    hide = narrow_to.shape[0]
    width = qkv_to.shape[1] // 3
    sh = qkv_ref.shape[2] // 3
    s = lax.axis_index("section")

    def without_gaps(values):
        pieces = [values[:, j * padded : j * padded + share] for j in range(n)]
        return jnp.concatenate(pieces, axis=1)

    qkv_to[...] = jnp.zeros_like(qkv_to)
    for j in range(n):
        for t in range(3):
            first = t * width + HD * low[j]
            qkv_to[:, first : first + sh] += qkv_ref[j, :share, t * sh : (t + 1) * sh].astype(F32)
        widen_to[:, j * hide : (j + 1) * hide] = widen_ref[j, :share, :hide].astype(F32)
    for ref, to in ((out_ref, out_to), (narrow_ref, narrow_to)):
        to[...] = without_gaps(ref[: to.shape[0]].astype(F32))
    for item, to in enumerate(stream_to):
        first, second = (ref[...] for ref in streams[2 * item : 2 * item + 2])
        to[s] = without_gaps(jnp.where(s == 0, first, second))
        to[1 - s] = without_gaps(came_ref[item].astype(F32))
    for row, (size, to) in enumerate(zip(sizes, vectors)):
        to[...] = vec_ref[row : row + 1, :size]


def settle_call(low, share, hide, qkv, widen, out, narrow, vec, came, *streams):
    n = widen.shape[0]
    width = n * share
    rows = came.shape[1]
    sizes = [share] * 6 + [2 * share, hide]
    return pl.pallas_call(
        functools.partial(settle_kernel, low, sizes),
        out_shape=[
            jax.ShapeDtypeStruct((share, 3 * width), F32),
            jax.ShapeDtypeStruct((share, n * hide), F32),
            jax.ShapeDtypeStruct((share, width), F32),
            jax.ShapeDtypeStruct((hide, width), F32),
            jax.ShapeDtypeStruct((2, rows, width), F32),
            jax.ShapeDtypeStruct((2, rows, width), F32),
        ]
        + [jax.ShapeDtypeStruct((1, size), F32) for size in sizes],
        in_specs=[VMEM_SPEC] * 10,
        out_specs=[VMEM_SPEC] * 14,
        compiler_params=params(),
        name="settle",
    )(qkv, widen, out, narrow, vec, came, *streams)


def unit_rows(values, mask, width):
    center = (values - jnp.sum(values, axis=-1, keepdims=True) * (1.0 / width)) * mask
    spread = jnp.sum(center * center, axis=-1, keepdims=True) * (1.0 / width)
    scale = lax.rsqrt(spread + EPSILON)
    return center * scale, scale


def norm_back(grad, unit, scale, gain, width):
    inner = grad * gain
    mean = jnp.sum(inner, axis=-1, keepdims=True) * (1.0 / width)
    along = jnp.sum(inner * unit, axis=-1, keepdims=True) * (1.0 / width)
    return (inner - mean - unit * along) * scale


def forward_kernel(n, width, layer, side, *refs):
    middle = layer is not None
    part, base, bias, gain, shift, mask = refs[:6]
    refs = refs[6:]
    if middle:
        widen_all, narrow_in, widen_bias, refs = refs[0], refs[1], refs[2], refs[3:]
    value_to, low_all, refs = refs[0], refs[1], refs[2:]
    if middle:
        pre_to, hidden_to, part_to, refs = refs[0], refs[1], refs[2], refs[3:]
    if side:
        side_out, refs = refs[0], refs[1:]
    own, g_ss, g_rs, g_ls = refs[5:9]
    p = Place(n)
    greet(p, line=True, over=side, sibling=side)
    scatter = Scatter(p, part, *refs[:5])
    scatter.start()
    loads = []
    if middle:
        widen, load_sems, rest = refs[9], refs[10], refs[11:]
        loads.append(fetch(widen_all.at[layer], widen, load_sems.at[0]))
        if side:
            job = RowSwap(p, narrow_in, side_out, *rest)
            job.start()
            filled = narrow_in.shape[0]
            for member in range(2):
                if side_out.shape[1] > filled:
                    spare = (side_out.shape[1] - filled, side_out.shape[2])
                    side_out[member, filled:] = jnp.zeros(spare, BF16)
            narrow = side_out.at[layer]
        else:
            narrow = rest[0]
            loads.append(fetch(narrow_in.at[layer], narrow, load_sems.at[1]))
    gather = Gather(p, own, low_all, g_ss, g_rs, g_ls)
    hr = own.shape[0] // HALVES

    def rows_step(half):
        rows = slice(half * hr, (half + 1) * hr)
        value = base[rows] + (scatter.result(half) + bias[...])
        value_to[rows] = value
        own[rows] = (unit_rows(value, mask[...], width)[0] * gain[...] + shift[...]).astype(BF16)

    by_halves(scatter, gather, rows_step, [])
    if side:
        job.step()
    gather.finish()
    for load in loads:
        load.wait()
    if side:
        job.finish()
    if middle:

        def block(first, size):
            rows = pl.ds(first, size)
            weight = widen[...].reshape(low_all.shape[1], widen.shape[2])
            pre = dot_n(low_all[rows], weight) + widen_bias[...]
            pre_to[rows] = pre
            hidden = (0.5 * pre * (1.0 + gelu_parts(pre)[0])).astype(BF16)
            hidden_to[rows] = hidden
            part_to[rows] = dot_n(hidden, narrow[...]).astype(BF16)

        row_blocks(low_all.shape[0], block)
    scatter.finish()


def scatter_scratch(n, rows, full):
    zn = n // 2
    piece = (HALVES, rows // HALVES, full)
    return [
        pltpu.VMEM((zn,) + piece, BF16),
        pltpu.VMEM((zn + 1,) + piece, BF16),
        pltpu.VMEM((zn,) + piece, BF16),
        DMA((4, zn, HALVES)),
        DMA((4, zn, HALVES)),
    ]


def gather_scratch(n):
    zn = n // 2
    return [DMA((4, zn, HALVES)), DMA((4, zn, HALVES)), DMA((HALVES,))]


def forward_call(n, collective_id, width, part, *local, layer=None, feed=(), carry=False):
    total_rows, full = part.shape
    rows = total_rows // n
    shapes = [
        jax.ShapeDtypeStruct((rows, full), F32),
        jax.ShapeDtypeStruct((total_rows, full), BF16),
    ]
    scratch = scatter_scratch(n, rows, full)
    scratch += [pltpu.VMEM((rows, full), BF16)] + gather_scratch(n)
    in_specs = [VMEM_SPEC] * (1 + len(local))
    if layer is not None:
        widen, narrow, _ = feed
        hide = widen.shape[3]
        in_specs += [ANY_SPEC, VMEM_SPEC if carry else ANY_SPEC, VMEM_SPEC]
        shapes += [
            jax.ShapeDtypeStruct((total_rows, hide), F32),
            jax.ShapeDtypeStruct((total_rows, hide), BF16),
            jax.ShapeDtypeStruct((total_rows, full), BF16),
        ]
        scratch += [pltpu.VMEM(widen.shape[1:], BF16), DMA((2,))]
        if carry:
            shapes.append(jax.ShapeDtypeStruct((2, hide, full), BF16))
            scratch += [DMA((2,)), DMA((2,)), DMA]
        else:
            scratch.append(pltpu.VMEM((hide, full), BF16))
    return pl.pallas_call(
        functools.partial(forward_kernel, n, width, layer, carry),
        out_shape=shapes,
        in_specs=in_specs,
        out_specs=[VMEM_SPEC] * len(shapes),
        scratch_shapes=scratch,
        compiler_params=params(collective_id),
        name="forward_rows",
    )(part, *local, *feed)


def back_rows(scatter, half, base, grad, gain, mask, width):
    hr = scatter.hr
    rows = slice(half * hr, (half + 1) * hr)
    total = scatter.result(half)
    unit, scale = unit_rows(base[rows], mask[...], width)
    value = grad[rows] + norm_back(total, unit, scale, gain[...], width)
    low = value.astype(BF16)
    terms = (total * unit, total, low.astype(F32))
    return rows, value, low, [jnp.sum(term, axis=0, keepdims=True) for term in terms]


def resid_kernel(n, width, layer, *refs):
    base, grad, gain, mask, normed, hidden_pre, hidden, outs, widen_all, narrow_all = refs[:10]
    value_to, sums_to, low_all, wide_to, wide_came, slim_to, pre_sums = refs[10:17]
    refs = refs[17:]
    own, g_ss, g_rs, g_ls = refs[5:9]
    wide, wide_in, wide_ss, wide_rs, slim, slim_in, slim_ss, slim_rs, x_ss, x_rs = refs[9:19]
    part, pre, widen, narrow, load_sems = refs[19:]
    p = Place(n)
    loads = [
        fetch(narrow_all.at[layer], narrow, load_sems.at[0]),
        fetch(widen_all.at[layer], widen, load_sems.at[1]),
    ]
    greet(p, line=True, over=True, sibling=True)
    for load in loads:
        load.wait()

    def block(first, size):
        rows = pl.ds(first, size)
        values = hidden_pre[rows]
        act, square = gelu_parts(values)
        slope = 0.5 * (1.0 + act) + 0.5 * values * (1.0 - act * act) * GELU_A * (
            1.0 + 3.0 * GELU_B * square
        )
        found = (dot_t(outs[rows], narrow[...]) * slope).astype(BF16)
        pre[rows] = found
        weight = widen[...].reshape(part.shape[1], widen.shape[2])
        part[rows] = dot_t(found, weight).astype(BF16)

    row_blocks(part.shape[0], block)
    scatter = Scatter(p, part, *refs[:5])
    scatter.start()
    gather = Gather(p, own, low_all, g_ss, g_rs, g_ls)
    wide_fold = Fold(p, wide, wide_in, wide_to, wide_ss, wide_rs)
    slim_fold = Fold(p, slim, slim_in, slim_to, slim_ss, slim_rs)
    cross = Cross(p, wide_to, wide_came, x_ss, x_rs, 1 - layer)

    def pre_sum():
        pre_sums[...] = jnp.sum(pre[...].astype(F32), axis=0, keepdims=True)

    for step in product(normed, pre, wide):
        step()
    wide_fold.start()
    work = product(hidden, outs, slim) + wide_fold.steps() + [cross.start, slim_fold.start, pre_sum]
    work += slim_fold.steps()
    sums = []

    def rows_step(half):
        rows, value, low, terms = back_rows(scatter, half, base, grad, gain, mask, width)
        value_to[rows] = value
        own[rows] = low
        sums.append(jnp.concatenate(terms, axis=0))

    by_halves(scatter, gather, rows_step, work, 3)
    sums_to[...] = sum(sums)
    for rest in work:
        rest()
    gather.finish()
    scatter.finish()
    for job in (wide_fold, slim_fold, cross):
        job.finish()


def resid_call(n, collective_id, width, layer, hide, *args):
    base, normed, hidden = args[0], args[4], args[6]
    widen, narrow = args[8:]
    rows = base.shape[0]
    total_rows, full = normed.shape
    zn = n // 2
    wide = (zn, full // n, hidden.shape[1])
    half = -(-hide // 32) * 16
    slim = (1, half, full)
    return pl.pallas_call(
        functools.partial(resid_kernel, n, width, layer),
        out_shape=[
            jax.ShapeDtypeStruct((rows, full), F32),
            jax.ShapeDtypeStruct((3, full), F32),
            jax.ShapeDtypeStruct((total_rows, full), BF16),
            jax.ShapeDtypeStruct(wide, BF16),
            jax.ShapeDtypeStruct(wide, BF16),
            jax.ShapeDtypeStruct(slim, BF16),
            jax.ShapeDtypeStruct((1, hidden.shape[1]), F32),
        ],
        in_specs=[VMEM_SPEC] * 8 + [ANY_SPEC] * 2,
        out_specs=[VMEM_SPEC] * 7,
        scratch_shapes=scatter_scratch(n, rows, full)
        + [pltpu.VMEM((rows, full), BF16)]
        + gather_scratch(n)
        + fold_scratch((full, hidden.shape[1]), wide)
        + fold_scratch((2 * half, full), slim)
        + [DMA, DMA]
        + [
            pltpu.VMEM((total_rows, full), BF16),
            pltpu.VMEM(hidden.shape, BF16),
            pltpu.VMEM(widen.shape[1:], BF16),
            pltpu.VMEM(narrow.shape[1:], BF16),
            DMA((2,)),
        ],
        compiler_params=params(collective_id),
        name="back_resid",
    )(*args)


def input_kernel(n, width, source, low, *refs):
    part, base, grad, gain, mask, normed, triple, att, resid, slim = refs[:10]
    value_to, sums_to, low_all, qkv_to, out_to, slim_came, triple_sums = refs[10:17]
    refs = refs[17:]
    own, g_ss, g_rs, g_ls = refs[5:9]
    qkv, qkv_in, qkv_ss, qkv_rs, out, out_in, out_ss, out_rs, x_ss, x_rs = refs[9:]
    p = Place(n)
    greet(p, line=True, over=True, sibling=True)
    scatter = Scatter(p, part, *refs[:5])
    scatter.start()
    cross = Cross(p, slim, slim_came, x_ss, x_rs, source)
    cross.start()
    gather = Gather(p, own, low_all, g_ss, g_rs, g_ls)
    qkv_fold = Fold(p, qkv, qkv_in, qkv_to, qkv_ss, qkv_rs)
    out_fold = Fold(p, out, out_in, out_to, out_ss, out_rs)

    def triple_sum():
        triple_sums[...] = jnp.sum(triple[...].astype(F32), axis=0, keepdims=True)

    work = product(normed, triple, qkv) + [qkv_fold.start]
    work += [functools.partial(home_rows, att, resid, out, low, width // n), out_fold.start]
    work += qkv_fold.steps() + [triple_sum] + out_fold.steps()
    sums = []

    def rows_step(half):
        rows, value, lower, terms = back_rows(scatter, half, base, grad, gain, mask, width)
        value_to[rows] = value
        own[rows] = lower
        sums.append(jnp.concatenate(terms, axis=0))

    by_halves(scatter, gather, rows_step, work, 2)
    sums_to[...] = sum(sums)
    for rest in work:
        rest()
    gather.finish()
    scatter.finish()
    for job in (qkv_fold, out_fold, cross):
        job.finish()


def input_call(n, collective_id, width, source, low, part, base, grad, gain, mask, *operands):
    normed, triple, att, resid, slim = operands
    total_rows, full = part.shape
    rows = total_rows // n
    zn = n // 2
    qkv = (zn, full // n, triple.shape[1])
    out = (1, att.shape[1] // 2, full)
    return pl.pallas_call(
        functools.partial(input_kernel, n, width, source, low),
        out_shape=[
            jax.ShapeDtypeStruct((rows, full), F32),
            jax.ShapeDtypeStruct((3, full), F32),
            jax.ShapeDtypeStruct((total_rows, full), BF16),
            jax.ShapeDtypeStruct(qkv, BF16),
            jax.ShapeDtypeStruct(out, BF16),
            jax.ShapeDtypeStruct(slim.shape, BF16),
            jax.ShapeDtypeStruct((1, triple.shape[1]), F32),
        ],
        in_specs=[VMEM_SPEC] * 10,
        out_specs=[VMEM_SPEC] * 7,
        scratch_shapes=scatter_scratch(n, rows, full)
        + [pltpu.VMEM((rows, full), BF16)]
        + gather_scratch(n)
        + fold_scratch((full, triple.shape[1]), qkv)
        + fold_scratch((att.shape[1], full), out)
        + [DMA, DMA],
        compiler_params=params(collective_id),
        name="back_input",
    )(part, base, grad, gain, mask, *operands)


def finale_kernel(n, width, low, *refs):
    part, base, grad, gain, mask, normed, triple, att, resid = refs[:9]
    wides, wide_cames, slims, slim_came, qkv_far, out_far, vecs = (
        refs[9:11],
        refs[11:13],
        refs[13:15],
        refs[15],
        refs[16],
        refs[17],
        refs[18:25],
    )
    layer_outs, upper_d_in, refs = refs[25:27], refs[27], refs[28:]
    value_to, wide_to, slim_to, qkv_to, out_to, vec_to, streams_to = refs[:7]
    refs = refs[7:]
    qkv, qkv_fold_in, qkv_ss, qkv_rs, out, out_fold_in, out_ss, out_rs = refs[5:13]
    qkv_own, qkv_in, qkv_sum, out_own, out_in, out_sum = refs[13:19]
    wide_sum, slim_in, slim_sum, vec, vec_in, vec_sum, vec_sib, streams = refs[19:27]
    a_ss, a_rs, x_ss, x_rs, v_ss, v_rs, r_ss, r_rs, ls = refs[27:]
    p = Place(n)
    s, c, h, z, zn = p.s, p.c, p.h, p.z, p.zn
    share = width // n
    greet_all(p)
    scatter = Scatter(p, part, *refs[:5])
    scatter.start()

    @pl.when(s == 0)
    def _():
        wide_sum[...] = (wides[0][...].astype(F32) + wide_cames[0][...].astype(F32)).astype(BF16)

    @pl.when(s == 1)
    def _():
        wide_sum[...] = (wides[1][...].astype(F32) + wide_cames[1][...].astype(F32)).astype(BF16)

    spreads = ((wide_sum, wide_to), (qkv_sum, qkv_to))

    def send(w, k):
        far = p.flip(k)
        src, dst = spreads[w]
        target = (s, c, far * 2 + p.far_y)
        return remote(src.at[far], dst.at[h], a_ss.at[0, w, k], a_rs.at[0, w, k], target)

    def keep(w):
        src, dst = spreads[w]
        return pltpu.make_async_copy(src.at[z], dst.at[h], ls.at[w])

    def aside(w, k):
        block = spreads[w][1].at[p.flip(k) * 2 + p.far_y]
        return remote(block, block, a_ss.at[1, w, k], a_rs.at[1, w, k], p.sibling)

    def start_zero(w):
        @pl.when(c == 1)
        def _():
            send(w, 0).start()

        @pl.when(c == 0)
        def _():
            keep(w).start()

    def x_block(k, src=qkv_far):
        far = p.flip(k)
        return remote(src.at[far], qkv_in.at[far], x_ss.at[k], x_rs.at[k], p.over)

    def out_cross(src=out_far):
        return remote(src, out_in, x_ss.at[zn], x_rs.at[zn], p.over)

    stream_cross = remote(streams, streams_to, x_ss.at[zn + 1], x_rs.at[zn + 1], p.over)
    slim_cross = Cross(p, slims[0], slim_in, x_ss.at[zn + 2], x_rs.at[zn + 2], 1)

    def start_far():
        @pl.when(s == 0)
        def _():
            for k in range(zn):
                x_block(k).start()
            out_cross().start()

    def start_own(k):
        @pl.when(s == 1)
        def _():
            x_block(k, qkv_own).start()

    def start_own_out():
        @pl.when(s == 1)
        def _():
            out_cross(out_own).start()

    qkv_fold = Fold(p, qkv, qkv_fold_in, qkv_own, qkv_ss, qkv_rs)
    out_fold = Fold(p, out, out_fold_in, out_own, out_ss, out_rs)

    start_zero(0)
    for k in range(1, zn):
        send(0, k).start()
    start_far()
    for step in product(normed, triple, qkv):
        step()
    qkv_fold.start()
    work = [functools.partial(home_rows, att, resid, out, low, share), out_fold.start]
    work += qkv_fold.steps()
    work += [functools.partial(start_own, k) for k in list(range(1, zn)) + [0]]
    work += out_fold.steps() + [start_own_out, slim_cross.start]
    sums = []

    def rows_step(half):
        rows, value, lower, terms = back_rows(scatter, half, base, grad, gain, mask, width)
        value_to[rows] = value
        sums.append(jnp.concatenate(terms, axis=0))

    by_halves(scatter, None, rows_step, work, 3)
    for rest in work:
        rest()

    streams[0] = jnp.where(s == 0, layer_outs[1][...], layer_outs[0][...]).astype(BF16)
    streams[1] = jnp.where(s == 0, upper_d_in[...], value_to[...]).astype(BF16)
    stream_cross.start()

    ones = (sum(sums), vecs[0][...])
    twos, triples, pres = vecs[1:3], (None, vecs[3]), vecs[4:6]
    lanes = vec.shape[3]
    padded = base.shape[1] // n
    sh = triple.shape[1] // 3
    for layer in range(2):
        one, two = ones[layer], twos[layer][...]
        outs = vecs[6][...] if layer else ones[1][2:3]
        features = jnp.concatenate([one[0:2], two[2:3], two[0:2], outs], axis=0)
        if layer:
            found = triples[1][...]
        else:
            found = jnp.sum(triple[...].astype(F32), axis=0, keepdims=True)
        bias = jnp.zeros((1, 2 * width), F32)
        for j, first in enumerate(low):
            spots = []
            for begin in (0, 2 * sh):
                spots += [
                    jnp.zeros((1, HD * first), F32),
                    found[:, begin : begin + sh],
                    jnp.zeros((1, width - sh - HD * first), F32),
                ]
            spots = [spot for spot in spots if spot.shape[1]]
            bias = jnp.where(h == j, jnp.concatenate(spots, axis=1), bias)
        for i in range(n):
            pieces = [
                features[:, i * padded : (i + 1) * padded],
                bias[:, i * 2 * share : (i + 1) * 2 * share],
                jnp.where(h == i, pres[layer][...], 0.0),
            ]
            wide_pieces = []
            for piece in pieces:
                rows, size = piece.shape
                if size < lanes:
                    piece = jnp.concatenate([piece, jnp.zeros((rows, lanes - size), F32)], axis=1)
                wide_pieces.append(piece)
            vec[layer, i] = jnp.concatenate(wide_pieces, axis=0)

    def vec_copy(a, b):
        l, i = lax.rem(s + a, 2), lax.rem(h + b, n)
        return remote(vec.at[l, i], vec_in.at[s, h], v_ss.at[a, b], v_rs.at[a, b], (l, c, i))

    for a, b in others(n):
        vec_copy(a, b).start()

    def add(to, index, first, second, came):
        @pl.when(s == 0)
        def _():
            to[index] = (first[index].astype(F32) + came[index].astype(F32)).astype(BF16)

        @pl.when(s == 1)
        def _():
            to[index] = (second[index].astype(F32) + came[index].astype(F32)).astype(BF16)

    for k in list(range(1, zn)) + [0]:
        x_block(k).wait_recv()
        add(qkv_sum, p.flip(k), qkv_own, qkv_far, qkv_in)
        if k:
            send(1, k).start()
        else:
            start_zero(1)
    out_cross().wait_recv()
    add(out_sum, 0, out_own, out_far, out_in)

    @pl.when(s == 0)
    def _():
        slim_cross.copy.wait_recv()
        slim_sum[0] = (slims[0][0].astype(F32) + slim_in[0].astype(F32)).astype(BF16)

    @pl.when(s == 1)
    def _():
        slim_cross.copy.wait_send()
        slim_sum[0] = (slims[1][0].astype(F32) + slim_came[0].astype(F32)).astype(BF16)

    def row_copies(w, src, dst):
        half = src.shape[1]
        piece = dst.at[pl.ds(pl.multiple_of(c * half, 16), half)]
        return (
            pltpu.make_async_copy(src.at[0], piece, ls.at[2 + w]),
            remote(src.at[0], piece, r_ss.at[w], r_rs.at[w], p.sibling),
        )

    copies = row_copies(0, slim_sum, slim_to) + row_copies(1, out_sum, out_to)
    for copy in copies:
        copy.start()
    total = vec[s, h]
    for a, b in others(n):
        vec_copy(a, b).wait_recv()
        total = total + vec_in[lax.rem(s + a, 2), lax.rem(h + n - b, n)]
    vec_sum[...] = total
    vec_share = remote(vec_sum, vec_sib, r_ss.at[2], r_rs.at[2], p.sibling)
    vec_share.start()
    for w in range(2):

        @pl.when(c == 1)
        def _():
            send(w, 0).wait_recv()

        @pl.when(c == 0)
        def _():
            keep(w).wait()

        for k in range(zn):
            if k:
                send(w, k).wait_recv()
            aside(w, k).start()
    vec_share.wait_recv()
    vec_to[...] = total + vec_sib[...]
    vec_share.wait_send()
    for w in range(2):

        @pl.when(c == 1)
        def _():
            send(w, 0).wait_send()

        for k in range(zn):
            if k:
                send(w, k).wait_send()
            aside(w, k).wait_recv()
            aside(w, k).wait_send()
    for w in range(2):
        copies[2 * w].wait()
        copies[2 * w + 1].wait_recv()
        copies[2 * w + 1].wait_send()
    for a, b in others(n):
        vec_copy(a, b).wait_send()
    for k in range(zn):
        x_block(k).wait_send()
    out_cross().wait_send()
    stream_cross.wait_recv()
    stream_cross.wait_send()
    for job in (scatter, qkv_fold, out_fold):
        job.finish()


def finale_call(n, collective_id, width, low, *args):
    part, triple, att = args[0], args[6], args[7]
    wide, slim, lanes = args[9].shape, args[13].shape, args[22].shape[1]
    total_rows, full = part.shape
    rows = total_rows // n
    zn = n // 2
    qkv = (zn, full // n, triple.shape[1])
    out = (1, att.shape[1] // 2, full)
    return pl.pallas_call(
        functools.partial(finale_kernel, n, width, low),
        out_shape=[
            jax.ShapeDtypeStruct((rows, full), F32),
            jax.ShapeDtypeStruct((n,) + wide[1:], BF16),
            jax.ShapeDtypeStruct((2 * slim[1], full), BF16),
            jax.ShapeDtypeStruct((n,) + qkv[1:], BF16),
            jax.ShapeDtypeStruct((2 * out[1], full), BF16),
            jax.ShapeDtypeStruct((8, lanes), F32),
            jax.ShapeDtypeStruct((2, rows, full), BF16),
        ],
        in_specs=[VMEM_SPEC] * len(args),
        out_specs=[VMEM_SPEC] + [ANY_SPEC] * 4 + [VMEM_SPEC] * 2,
        scratch_shapes=scatter_scratch(n, rows, full)
        + fold_scratch((full, triple.shape[1]), qkv)
        + fold_scratch((att.shape[1], full), out)
        + [pltpu.VMEM(qkv, BF16)] * 3
        + [pltpu.VMEM(out, BF16)] * 3
        + [
            pltpu.VMEM(wide, BF16),
            pltpu.VMEM(slim, BF16),
            pltpu.VMEM(slim, BF16),
            pltpu.VMEM((2, n, 8, lanes), F32),
            pltpu.VMEM((2, n, 8, lanes), F32),
            pltpu.VMEM((8, lanes), F32),
            pltpu.VMEM((8, lanes), F32),
            pltpu.VMEM((2, rows, full), BF16),
            DMA((2, 2, zn)),
            DMA((2, 2, zn)),
            DMA((zn + 3,)),
            DMA((zn + 3,)),
            DMA((2, n)),
            DMA((2, n)),
            DMA((3,)),
            DMA((3,)),
            DMA((4,)),
        ],
        compiler_params=params(collective_id),
        name="finale",
    )(*args)


def dot_t(a, b):
    return lax.dot_general(a, b, (((1,), (1,)), ((), ())), preferred_element_type=F32)


def dot_n(a, b):
    return lax.dot_general(a, b, (((1,), (0,)), ((), ())), preferred_element_type=F32)


def in_blocks(rows, step, chunk, between):
    count = rows // step
    if count <= 2:
        for b in range(count):
            chunk(b * step, rows // 2 if (b + 1) * step <= rows // 2 else rows, between)
    else:

        def body(b, carry, keys):
            chunk(pl.multiple_of(b * step, step), keys, [])
            return carry

        middle = count // 2 if count % 2 == 0 else 0
        lax.fori_loop(0, middle, functools.partial(body, keys=rows // 2), 0)
        lax.fori_loop(middle, count, functools.partial(body, keys=rows), 0)


def run_next(between):
    if between:
        between.pop(0)()


def attend_kernel(n, slots, step, layer, side, *refs):
    kpos_ref, qpos_ref, carried, out_all = refs[:4]
    refs = refs[4:]
    if layer:
        normed, qkv_all, qkv_bias = refs[:3]
        refs = refs[3:]
    else:
        own_ref, refs = refs[0], refs[1:]
    att_ref, low_ref, lse_ref, oth_ref, part_to, carried_to = refs[:6]
    refs = refs[6:]
    if layer:
        own_ref, refs = refs[0], refs[1:]
    kv_ss, kv_rs, out_weight, load_sems = refs[:4]
    refs = refs[4:]
    if layer:
        qkv_weight, refs = refs[0], refs[1:]
        qkv_load = fetch(qkv_all.at[layer], qkv_weight, load_sems.at[1])
    out_load = fetch(out_all.at[layer], out_weight, load_sems.at[0])
    p = Place(n)
    rows = own_ref.shape[0]
    sh = slots * HD
    power = HD**-0.5 * LOG2E
    if side == "spread":
        greet(p, spread=True, over=True, sibling=True)
    else:
        greet(p, line=True, sibling=True)
    job = (Spread if side == "spread" else Gather)(p, carried, carried_to, *refs)
    job.start()
    if layer:
        qkv_load.wait()

        def project(first, size):
            some = pl.ds(first, size)
            weight = qkv_weight[...].reshape(normed.shape[1], 3 * sh)
            own_ref[some] = (dot_n(normed[some], weight) + qkv_bias[...]).astype(BF16)

        row_blocks(rows, project)
    swap = remote(own_ref.at[:, pl.ds(sh, 2 * sh)], oth_ref, kv_ss, kv_rs, p.sibling)
    swap.start()
    swap.wait_recv()

    def at(base, slot):
        return slice(base + slot * HD, base + (slot + 1) * HD)

    def chunk(first, seen, between):
        q_rows = pl.ds(first, step)
        qpos = qpos_ref[:, q_rows]
        for slot in range(slots):
            queries = own_ref[q_rows, at(0, slot)]
            keys = (own_ref[:seen, at(sh, slot)], oth_ref[:seen, at(0, slot)])
            values = (own_ref[:seen, at(2 * sh, slot)], oth_ref[:seen, at(sh, slot)])
            scores = []
            for part in range(2):
                allowed = kpos_ref[part * rows : part * rows + seen] <= qpos
                scores.append(jnp.where(allowed, dot_t(keys[part], queries), MASKED))
            top = jnp.maximum(
                jnp.max(scores[0], axis=0, keepdims=True), jnp.max(scores[1], axis=0, keepdims=True)
            )
            total = jnp.zeros_like(top)
            weighted = jnp.zeros((HD, step), F32)
            exps = []
            for part in range(2):
                e = jnp.exp2((scores[part] - top) * power)
                total = total + jnp.sum(e, axis=0, keepdims=True)
                exps.append(e)
            inverse = 1.0 / total
            for part in range(2):
                probs = (exps[part] * inverse).astype(BF16)
                weighted = weighted + dot_n(values[part].T, probs)
            att_ref[at(0, slot), q_rows] = weighted
            low_ref[q_rows, at(0, slot)] = weighted.T.astype(BF16)
            lse_ref[slot : slot + 1, q_rows] = top * power + jnp.log(total) * LOG2E
            run_next(between)

    between = job.steps()
    in_blocks(rows, step, chunk, between)
    out_load.wait()

    def give(first, size):
        some = pl.ds(first, size)
        part_to[some] = dot_n(low_ref[some], out_weight[...]).astype(BF16)

    row_blocks(rows, give)
    for rest in between:
        rest()
    swap.wait_send()
    job.finish()


def attend_call(n, collective_id, slots, layer, side, kpos, qpos, carried, out_all, *source):
    rows = qpos.shape[1]
    zn = n // 2
    sh = slots * HD
    full = out_all.shape[2]
    step = min(rows, 256)
    if side == "spread":
        moved = jax.ShapeDtypeStruct((2,) + carried.shape, BF16)
        scratch = [DMA((4, zn)), DMA((4, zn)), DMA]
    else:
        moved = jax.ShapeDtypeStruct((n * carried.shape[0], carried.shape[1]), BF16)
        scratch = gather_scratch(n)
    shapes = [
        jax.ShapeDtypeStruct((sh, rows), F32),
        jax.ShapeDtypeStruct((rows, sh), BF16),
        jax.ShapeDtypeStruct((slots, rows), F32),
        jax.ShapeDtypeStruct((rows, 2 * sh), BF16),
        jax.ShapeDtypeStruct((rows, full), BF16),
        moved,
    ]
    in_specs = [VMEM_SPEC] * 3 + [ANY_SPEC, VMEM_SPEC]
    kept = [DMA, DMA, pltpu.VMEM((sh, full), BF16), DMA((2,))]
    if layer:
        in_specs += [ANY_SPEC, VMEM_SPEC]
        shapes.append(jax.ShapeDtypeStruct((rows, 3 * sh), BF16))
        kept.append(pltpu.VMEM(source[1].shape[1:], BF16))
    return pl.pallas_call(
        functools.partial(attend_kernel, n, slots, step, layer, side),
        out_shape=shapes,
        in_specs=in_specs,
        out_specs=[VMEM_SPEC] * len(shapes),
        scratch_shapes=kept + scratch,
        compiler_params=params(collective_id),
        name="attend_" + side,
    )(kpos, qpos, carried, out_all, *source)


def attend_back_kernel(n, slots, step, layer, last, *refs):
    own_ref, oth_ref, resid, att_ref, lse_ref, kpos_ref, qpos_ref, out_all, qkv_all = refs[:9]
    refs = refs[9:]
    if last:
        part_ref, base_ref, bias_ref = refs[:3]
        refs = refs[3:]
    triple_ref, part_to, refs = refs[0], refs[1], refs[2:]
    if last:
        value_ref, refs = refs[0], refs[1:]
    dq_t, dkv_own, dkv_oth, came, kv_ss, kv_rs = refs[:6]
    grad_ref, out_weight, qkv_weight, load_sems = refs[6:10]
    out_load = fetch(out_all.at[layer], out_weight, load_sems.at[0])
    qkv_load = fetch(qkv_all.at[layer], qkv_weight, load_sems.at[1])
    p = Place(n)
    rows = own_ref.shape[0]
    sh = slots * HD
    scale = HD**-0.5
    greet(p, line=last, sibling=True)
    between = []
    if last:
        scatter = Scatter(p, part_ref, *refs[10:])
        scatter.start()
        between = scatter.steps()
    out_load.wait()

    def enter(first, size):
        some = pl.ds(first, size)
        grad_ref[some] = dot_t(resid[some], out_weight[...]).astype(BF16)

    row_blocks(rows, enter)

    def at(base, slot):
        return slice(base + slot * HD, base + (slot + 1) * HD)

    dq_t[...] = jnp.zeros_like(dq_t)
    swap = remote(dkv_oth, came, kv_ss, kv_rs, p.sibling)
    for part in (1, 0):
        dkv = (dkv_own, dkv_oth)[part]
        src = (own_ref, oth_ref)[part]
        base = (sh, 0)[part]
        dkv[...] = jnp.zeros_like(dkv)

        def chunk(first, seen, between):
            q_rows = pl.ds(first, step)
            qpos = qpos_ref[:, q_rows]
            for slot in range(slots):
                queries = own_ref[q_rows, at(0, slot)]
                grads = grad_ref[q_rows, at(0, slot)]
                keys, values = src[:seen, at(base, slot)], src[:seen, at(base + sh, slot)]
                lse = lse_ref[slot : slot + 1, q_rows]
                correction = jnp.sum(
                    grads.astype(F32).T * att_ref[at(0, slot), q_rows], axis=0, keepdims=True
                )
                allowed = kpos_ref[part * rows : part * rows + seen] <= qpos
                scores = dot_t(keys, queries)
                probs = jnp.where(allowed, jnp.exp2(scores * (scale * LOG2E) - lse), 0.0)
                prob_grad = dot_t(values, grads)
                score_grad = (probs * (prob_grad - correction)).astype(BF16)
                dkv[:seen, at(0, slot)] += dot_n(score_grad, queries) * scale
                dkv[:seen, at(sh, slot)] += dot_n(probs.astype(BF16), grads)
                dq_t[at(0, slot), q_rows] += dot_n(keys.T, score_grad)
                run_next(between)

        in_blocks(rows, step, chunk, between)
        if part:
            swap.start()
    triple_ref[:, :sh] = (dq_t[...].T * scale).astype(BF16)

    def finish_last():
        for rest in between:
            rest()
        hr = base_ref.shape[0] // HALVES
        for half in range(HALVES):
            part_rows = slice(half * hr, (half + 1) * hr)
            total = scatter.result(half)
            value_ref[part_rows] = base_ref[part_rows] + (total + bias_ref[...])
        scatter.finish()

    swap.wait_recv()
    triple_ref[:, sh:] = (dkv_own[...] + came[...]).astype(BF16)
    qkv_load.wait()

    def leave(first, size):
        some = pl.ds(first, size)
        weight = qkv_weight[...].reshape(part_to.shape[1], 3 * sh)
        part_to[some] = dot_t(triple_ref[some], weight).astype(BF16)

    row_blocks(rows, leave)
    if last:
        finish_last()
    swap.wait_send()


def attend_back_call(n, collective_id, slots, layer, *args, last=()):
    qkv, out_all, qkv_all = args[0], args[7], args[8]
    rows = qkv.shape[0]
    sh = slots * HD
    full = out_all.shape[2]
    step = min(rows, 256)
    shapes = [
        jax.ShapeDtypeStruct((rows, 3 * sh), BF16),
        jax.ShapeDtypeStruct((rows, full), BF16),
    ]
    scratch = [pltpu.VMEM((sh, rows), F32)] + [pltpu.VMEM((rows, 2 * sh), F32)] * 3
    scratch += [DMA, DMA]
    scratch += [
        pltpu.VMEM((rows, sh), BF16),
        pltpu.VMEM((sh, full), BF16),
        pltpu.VMEM(qkv_all.shape[1:], BF16),
        DMA((2,)),
    ]
    if last:
        shapes.append(jax.ShapeDtypeStruct(last[1].shape, F32))
        scratch += scatter_scratch(n, *last[1].shape)
    return pl.pallas_call(
        functools.partial(attend_back_kernel, n, slots, step, layer, bool(last)),
        out_shape=shapes,
        in_specs=[VMEM_SPEC] * 7 + [ANY_SPEC] * 2 + [VMEM_SPEC] * len(last),
        out_specs=[VMEM_SPEC] * len(shapes),
        scratch_shapes=scratch,
        compiler_params=params(collective_id),
        name="attend_back",
    )(*args, *last)


def windows(width, n):
    share = width // n
    low = [j * share // HD for j in range(n)]
    slots = max(((j + 1) * share - 1) // HD - low[j] + 1 for j in range(n))
    return [min(first, HEADS - slots) for first in low], slots


def on_device(n, tokens, block_order, cotangent, *vectors_and_weights):
    (
        first_gain,
        first_shift,
        qkv_weight,
        input_bias,
        out_weight,
        out_bias,
        second_gain,
        second_shift,
        widen_weight,
        widen_bias,
        narrow_weight,
        narrow_bias,
    ) = (member[0] for member in vectors_and_weights)
    c = lax.axis_index("ctx")
    _, rows, width = tokens.shape
    hidden = widen_weight.shape[1]
    share = width // n
    hide = hidden // n
    padded = -(-share // 16) * 16
    full = n * padded
    low, slots = windows(width, n)
    sh = slots * HD
    total_rows = n * rows
    half_rows = rows // HALVES

    mask = jnp.asarray(np.arange(full)[None] % padded < share, F32)
    qkv_send, widen_send, out_send, narrow_send, pack, own_tokens, x, own_cot, out_grad, out_sums = (
        lay_out_call(
            low,
            slots,
            padded,
            qkv_weight,
            widen_weight,
            out_weight,
            narrow_weight,
            tokens,
            cotangent,
            first_gain[None],
            first_shift[None],
            out_bias[None],
            second_gain[None],
            second_shift[None],
            narrow_bias[None],
            input_bias[None],
            widen_bias[None],
        )
    )
    hide_full = widen_send.shape[2]
    normed, qkv, qkv_all, out_all, feats, qkv_bias, widen_biases = start_call(
        n, low, width, widen_send.shape[2], own_tokens, pack, qkv_send, out_send, mask
    )

    order = block_order.reshape(2, n, HALVES).transpose(0, 2, 1)
    places = order[..., None] * half_rows + jnp.arange(half_rows, dtype=jnp.int32)
    places = places.reshape(2, total_rows)
    own_places = jnp.where(c == 0, places[0], places[1])
    oth_places = jnp.where(c == 0, places[1], places[0])
    kpos = jnp.concatenate([own_places, oth_places])[:, None]
    qpos = own_places[None, :]

    layers = [
        dict(
            gain1=feats[layer, 0:1],
            shift1=feats[layer, 1:2],
            out_bias=feats[layer, 2:3],
            gain2=feats[layer, 3:4],
            shift2=feats[layer, 4:5],
            narrow_bias=feats[layer, 5:6],
            qkv_bias=qkv_bias[layer],
            widen_bias=widen_biases[layer],
        )
        for layer in range(2)
    ]

    stored = []
    layer_outs = []
    for layer in range(2):
        w = layers[layer]
        if layer:
            found = attend_call(
                n, 2, slots, 1, "gather", kpos, qpos, own_cot, out_all, normed, qkv_all, w["qkv_bias"]
            )
            out_low_all, qkv = found[5:]
        else:
            found = attend_call(n, 1, slots, 0, "spread", kpos, qpos, widen_send, out_all, qkv)
            widen_all = found[5]
        att, att_low, lse, other, part = found[:5]
        found = forward_call(
            n,
            3 + layer,
            width,
            part,
            x,
            w["out_bias"],
            w["gain2"],
            w["shift2"],
            mask,
            layer=layer,
            feed=(widen_all, narrow_all if layer else narrow_send, w["widen_bias"]),
            carry=not layer,
        )
        residual, normed_two, hidden_pre, hidden_low, part = found[:5]
        stored.append((x, normed, qkv, other, att, att_low, lse, residual, normed_two))
        stored[-1] += (hidden_pre, hidden_low)
        if layer == 0:
            narrow_all = found[5]
            nxt = layers[1]
            x, normed = forward_call(
                n,
                5,
                width,
                part,
                residual,
                w["narrow_bias"],
                nxt["gain1"],
                nxt["shift1"],
                mask,
            )
            layer_outs.append(x)
        else:
            last = (part, residual, w["narrow_bias"])

    found = {}
    for layer in (1, 0):
        w = layers[layer]
        x, normed, qkv, other, att, att_low, lse, residual, normed_two = stored[layer][:9]
        hidden_pre, hidden_low = stored[layer][9:]
        resid_grad, sums_two, resid_low_all, wide, wide_came, slim, pre_sums = resid_call(
            n,
            7 + layer,
            width,
            layer,
            hide,
            residual,
            out_grad,
            w["gain2"],
            mask,
            normed_two,
            hidden_pre,
            hidden_low,
            out_low_all,
            widen_all,
            narrow_all,
        )
        back = attend_back_call(
            n,
            9 + layer,
            slots,
            layer,
            qkv,
            other,
            resid_low_all,
            att,
            lse,
            kpos,
            qpos,
            out_all,
            qkv_all,
            last=last if layer else (),
        )
        triple, part = back[:2]
        local = (part, x, resid_grad, w["gain1"], mask, normed, triple, att_low, resid_low_all)
        found[layer] = (wide, wide_came, slim, sums_two, pre_sums)
        if layer:
            layer_outs.append(back[2])
            upper_d_in, sums_one, out_low_all, qkv_grad, out_rows, slim_came, triple_sums = (
                input_call(n, 11, width, 0, low, *local, slim)
            )
            out_grad = upper_d_in
    lower, upper = found[0], found[1]
    d_in, widen_back, narrow_back, qkv_back, out_back, vec, came = finale_call(
        n,
        12,
        width,
        low,
        *local,
        lower[0],
        upper[0],
        lower[1],
        upper[1],
        lower[2],
        upper[2],
        slim_came,
        qkv_grad,
        out_rows,
        sums_one,
        lower[3],
        upper[3],
        triple_sums,
        lower[4],
        upper[4],
        out_sums,
        *layer_outs,
        upper_d_in,
    )
    settled = settle_call(
        low,
        share,
        hide,
        qkv_back,
        widen_back,
        out_back,
        narrow_back,
        vec,
        came,
        *layer_outs,
        d_in,
        upper_d_in,
    )
    qkv_out, widen_out, out_out, narrow_out, layer_out, d_out = (m[None] for m in settled[:6])
    gain1, shift1, out_b, gain2, shift2, narrow_b, input_b, widen_b = settled[6:]
    return (
        layer_out,
        d_out,
        gain1,
        shift1,
        qkv_out,
        input_b,
        out_out,
        out_b,
        gain2,
        shift2,
        widen_out,
        widen_b,
        narrow_out,
        narrow_b,
    )


def solution(mesh):
    rows = P(None, ("ctx", "shard"), None)
    vector = P("section", "shard")
    matrix = P("section", "shard", None)
    order = (
        vector,
        vector,
        matrix,
        vector,
        matrix,
        vector,
        vector,
        vector,
        matrix,
        vector,
        matrix,
        vector,
    )
    streams = P("section", None, ("ctx", "shard"), None)
    return jax.shard_map(
        functools.partial(on_device, mesh.shape["shard"]),
        mesh=mesh,
        in_specs=(rows, P(), rows) + order,
        out_specs=(streams, streams) + order,
        check_vma=False,
    )
```

time: 841 us -> 631 us (0.75)
  matrix products: 84.8 us -> 0 us
  local copies, waits for them, and re-layouts: 55.2 us -> 6.44 us
  Pallas kernels: 658 us -> 617 us
  other arithmetic: 28.2 us -> 0.77 us
    dot_general x24 -> x0, matrix products: 84.8 us -> none  [the longest x8 30.4 us: dot_t(): lax.dot_general(a, b, (((1,), (1,)), ((), ())), preferred_element_type=F32)]
    pallas_call x19 -> x14, Pallas kernels: 658 us -> 617 us  [the longest x3 144 us: forward_call(): pl.pallas_call(functools.partial(forward_kernel, n, width, layer, carry),...]
    slice x22 -> x0, local copies, waits for them, and re-layouts: 13.6 us -> none  [the longest x1 4.3 us: on_device(): qkv_all[layer].reshape(full, 3 * sh)]
    convert_element_type x2 -> x0, local copies, waits for them, and re-layouts: 10.8 us -> none  [over_rows(): return found.astype(BF16)]
    reshape x18 -> x0, local copies, waits for them, and re-layouts: 9.81 us -> none  [the longest x11 7.56 us: feature(): jnp.pad(vec[:, row, :share], [(0, 0), (0, padded - share)]).reshape(1, full)]
where the time goes in v2:
time: 631 us; the launch traced here: 625 us
  Pallas kernels  617 us (98%)
  local copies, waits for them, and re-layouts  6.44 us (1%)
    pallas_call x3, Pallas kernels, forward_call(): pl.pallas_call(functools.partial(forward_kernel, n, width, layer, carry),...  144 us
    pallas_call x2, Pallas kernels, resid_call(): pl.pallas_call(functools.partial(resid_kernel, n, width, layer), out_shap...  107 us
    pallas_call x1, Pallas kernels, finale_call(): pl.pallas_call(functools.partial(finale_kernel, n, width, low), out_shape...  105 us
    pallas_call x2, Pallas kernels, attend_call(): pl.pallas_call(functools.partial(attend_kernel, n, slots, step, layer, si...  83.5 us
    pallas_call x1, Pallas kernels, start_call(): pl.pallas_call(functools.partial(start_kernel, n, low, width), out_shape=...  66.8 us
    pallas_call x1, Pallas kernels, input_call(): pl.pallas_call(functools.partial(input_kernel, n, width, source, low), ou...  46.5 us
    pallas_call x2, Pallas kernels, attend_back_call(): pl.pallas_call(functools.partial(attend_back_kernel, n, slots, step, laye...  39.8 us
    pallas_call x1, Pallas kernels, settle_call(): pl.pallas_call(functools.partial(settle_kernel, low, sizes), out_shape=[j...  13.2 us

profile of v2, /device:TPU:0, one launch (start us, length us, event | category | flops | bytes accessed | tf_op | source)
XLA Modules:
  0.0 625.0 jit_solution(6204622151774631196)
XLA Ops:
  0.7 0.7 broadcast_multiply_fusion
  1.3 0.1 mul.15
  1.4 0.1 iota_add_fusion
  1.5 0.1 select_n.32
  1.6 0.7 select_n.33.refs_1_.refs_6_
  2.2 0.1 select_n.30
  2.3 1.0 copy.32.refs_0_.refs_5_
  3.4 10.5 %lay_out.1 = (bf16[8,208,768]{2,1,0:T(8,128)(2,1)}, bf16[8,208,896]{2,1,0:T(8,128)(2,1)}, bf16[256,1664]{1,0:T(8,128)(2,1)}, bf16[800,1664]{1,0:T(8,128)(2,1)}, ...) custom-call(bf16[200,4800]{1,0:T(8,128)(2,1)} %bitcast.50, ...), custom_call_target="tpu_custom_call" | custom-call | tf_op jit(solution)/shard_map/lay_out/pallas_call | solution.py:799
  13.8 66.8 %start.1 = (bf16[512,1664]{1,0:T(8,128)(2,1)}, bf16[512,768]{1,0:T(8,128)(2,1)}, bf16[2,8,208,768]{3,2,1,0:T(8,128)(2,1)}, bf16[2,256,1664]{2,1,0:T(8,128)(2,1)}...) custom-call(bf16[64,1664]{1,0:T(8,128)(2,1)} %get-tuple-element.104.tok_ref, ...), custom_call_target="tpu_custom_call" | custom-call | tf_op jit(solution)/shard_map/start/pallas_call | solution.py:710
  80.6 1.9 slice_bitcast_fusion
  82.5 1.3 slice_bitcast_fusion.13.refs_6_
  83.8 1.3 slice_bitcast_fusion.11
  85.1 57.0 %attend_spread.1 = (f32[256,512]{1,0:T(8,128)}, bf16[512,256]{1,0:T(8,128)(2,1)}, f32[4,512]{1,0:T(4,128)}, bf16[512,512]{1,0:T(8,128)(2,1)}, bf16[512,1664]{1,0...) custom-call(s32[1024,1]{1,0:T(8,128)} %copy.32.refs_0_.refs_5_, s32[1,512]{1,0:T(1,128)} %select_n.33.refs_1_.refs_6_, ...), custom_call_target="tpu_custom_call" | custom-call | tf_op jit(solution)/shard_map/attend_spread/pallas_call | solution.py:1631
  142.1 53.0 %forward_rows.3 = (f32[64,1664]{1,0:T(8,128)}, bf16[512,1664]{1,0:T(8,128)(2,1)}, f32[512,896]{1,0:T(8,128)}, bf16[512,896]{1,0:T(8,128)(2,1)}, bf16[512,1664]{1...) custom-call(bf16[512,1664]{1,0:T(8,128)(2,1)} %get-tuple-element.112.refs_0_, f32[64,1664]{1,0:T(8,128)} %get-tuple-element.113.refs_1_, ...), custom_call_target="tpu_custom_call" | custom-call | tf_op jit(solution)/shard_map/forward_rows/pallas_call | solution.py:993
  195.1 42.5 %forward_rows.4 = (f32[64,1664]{1,0:T(8,128)}, bf16[512,1664]{1,0:T(8,128)(2,1)}) custom-call(bf16[512,1664]{1,0:T(8,128)(2,1)} %get-tuple-element.120.refs_0_, f32[64,1664]{1,0:T(8,128)} %get-tuple-element.118.refs_1_.refs_0_, f32[1,1664]{1,0:T(1,128)} %get-tuple-element.201.refs_2_, f32[1,1664]{1,0:T(1,128)} %get-tuple-element.200.refs_3_, ...), custom_call_target="tpu_custom_call" | custom-call | tf_op jit(solution)/shard_map/forward_rows/pallas_call | solution.py:993
  237.6 26.5 %attend_gather.1 = (f32[256,512]{1,0:T(8,128)}, bf16[512,256]{1,0:T(8,128)(2,1)}, f32[4,512]{1,0:T(4,128)}, bf16[512,512]{1,0:T(8,128)(2,1)}, bf16[512,1664]{1,0...) custom-call(s32[1024,1]{1,0:T(8,128)} %copy.32.refs_0_.refs_5_, s32[1,512]{1,0:T(1,128)} %select_n.33.refs_1_.refs_6_, ...), custom_call_target="tpu_custom_call" | custom-call | tf_op jit(solution)/shard_map/attend_gather/pallas_call | solution.py:1631
  264.0 48.6 %forward_rows.5 = (f32[64,1664]{1,0:T(8,128)}, bf16[512,1664]{1,0:T(8,128)(2,1)}, f32[512,896]{1,0:T(8,128)}, bf16[512,896]{1,0:T(8,128)(2,1)}, bf16[512,1664]{1,0:T(8,128)(2,1)}) custom-call(bf16[512,1664]{1,0:T(8,128)(2,1)} %get-tuple-element.126.refs_0_, f32[64,1664]{1,0:T(8,128)} %get-tuple-element.127.refs_1_.refs_25_.refs_0_, ...), custom_call_target="tpu_custom_call" | custom-call | tf_op jit(solution)/shard_map/forward_rows/pallas_call | solution.py:993
  312.6 54.0 %back_resid.2 = (f32[64,1664]{1,0:T(8,128)}, f32[3,1664]{1,0:T(4,128)}, bf16[512,1664]{1,0:T(8,128)(2,1)}, bf16[4,208,896]{2,1,0:T(8,128)(2,1)}, bf16[4,208,896]...) custom-call(f32[64,1664]{1,0:T(8,128)} %get-tuple-element.129.refs_0_.refs_10_, ...), custom_call_target="tpu_custom_call" | custom-call | tf_op jit(solution)/shard_map/back_resid/pallas_call | solution.py:1086
  366.6 27.2 %attend_back.2 = (bf16[512,768]{1,0:T(8,128)(2,1)}, bf16[512,1664]{1,0:T(8,128)(2,1)}, f32[64,1664]{1,0:T(8,128)}) custom-call(bf16[512,768]{1,0:T(8,128)(2,1)} %get-tuple-element.124.refs_0_, bf16[512,512]{1,0:T(8,128)(2,1)} %get-tuple-element.125.refs_1_, bf16[512,1664]{1,0:T(8,128)(2,1)} %get-tuple-element.135.refs_2_.refs_8_, ...), custom_call_target="tpu_custom_call" | custom-call | tf_op jit(solution)/shard_map/attend_back/pallas_call | solution.py:1756
  393.8 46.5 %back_input.1 = (f32[64,1664]{1,0:T(8,128)}, f32[3,1664]{1,0:T(4,128)}, bf16[512,1664]{1,0:T(8,128)(2,1)}, bf16[4,208,768]{2,1,0:T(8,128)(2,1)}, bf16[1,128,1664...) custom-call(bf16[512,1664]{1,0:T(8,128)(2,1)} %get-tuple-element.139.refs_0_, ...), custom_call_target="tpu_custom_call" | custom-call | tf_op jit(solution)/shard_map/back_input/pallas_call | solution.py:1164
  440.2 53.4 %back_resid.3 = (f32[64,1664]{1,0:T(8,128)}, f32[3,1664]{1,0:T(4,128)}, bf16[512,1664]{1,0:T(8,128)(2,1)}, bf16[4,208,896]{2,1,0:T(8,128)(2,1)}, bf16[4,208,896]...) custom-call(f32[64,1664]{1,0:T(8,128)} %get-tuple-element.118.refs_1_.refs_0_, ...), custom_call_target="tpu_custom_call" | custom-call | tf_op jit(solution)/shard_map/back_resid/pallas_call | solution.py:1086
  493.7 12.6 %attend_back.3 = (bf16[512,768]{1,0:T(8,128)(2,1)}, bf16[512,1664]{1,0:T(8,128)(2,1)}) custom-call(bf16[512,768]{1,0:T(8,128)(2,1)} %get-tuple-element.108.refs_4_.refs_0_, bf16[512,512]{1,0:T(8,128)(2,1)} %get-tuple-element.111.refs_1_, bf16[512,1664]{1,0:T(8,128)(2,1)} %get-tuple-element.149.refs_2_.refs_8_, f32[256,512]{1,0:T(8,128)} %get-tuple-element.150.refs_3_, ...), custom_call_target="tpu_custom_call" | custom-call | tf_op jit(solution)/shard_map/attend_back/pallas_call | solution.py:1756
  506.3 105.1 %finale.1 = (f32[64,1664]{1,0:T(8,128)}, bf16[8,208,896]{2,1,0:T(8,128)(2,1)}, bf16[800,1664]{1,0:T(8,128)(2,1)}, bf16[8,208,768]{2,1,0:T(8,128)(2,1)}, bf16[256...) custom-call(bf16[512,1664]{1,0:T(8,128)(2,1)} %get-tuple-element.152.refs_0_, ...), custom_call_target="tpu_custom_call" | custom-call | tf_op jit(solution)/shard_map/finale/pallas_call | solution.py:1445
  611.4 13.2 %settle.1 = (f32[200,4800]{1,0:T(8,128)}, f32[200,6400]{1,0:T(8,128)}, f32[200,1600]{1,0:T(8,128)}, f32[800,1600]{1,0:T(8,128)}, f32[2,64,1600]{2,1,0:T(8,128)},...) custom-call(bf16[8,208,768]{2,1,0:T(8,128)(2,1)} %get-tuple-element., ...), custom_call_target="tpu_custom_call" | custom-call | tf_op jit(solution)/shard_map/settle/pallas_call | solution.py:855
  (3 shorter events, 0.0 us)

commit v3 on v2

--- a/solution.py
+++ b/solution.py
@@ -507,6 +507,76 @@
             self.copy.wait_recv()
 
 
+class Home:
+    def __init__(self, p, src, dst, ss, rs, ls):
+        self.p, self.src, self.dst, self.ss, self.rs, self.ls = p, src, dst, ss, rs, ls
+
+    def send(self, k):
+        p = self.p
+        far = p.flip(k)
+        target = (p.s, p.c, far * 2 + p.far_y)
+        sems = (self.ss.at[0, k], self.rs.at[0, k])
+        return remote(self.src.at[far], self.dst.at[p.h], *sems, target)
+
+    def keep(self):
+        return pltpu.make_async_copy(self.src.at[self.p.z], self.dst.at[self.p.h], self.ls)
+
+    def aside(self, k):
+        block = self.dst.at[self.p.flip(k) * 2 + self.p.far_y]
+        return remote(block, block, self.ss.at[1, k], self.rs.at[1, k], self.p.sibling)
+
+    def start(self, k):
+        if k:
+            self.send(k).start()
+            return
+
+        @pl.when(self.p.c == 1)
+        def _():
+            self.send(0).start()
+
+        @pl.when(self.p.c == 0)
+        def _():
+            self.keep().start()
+
+    def arrived(self, k):
+        if k:
+            self.send(k).wait_recv()
+        else:
+
+            @pl.when(self.p.c == 1)
+            def _():
+                self.send(0).wait_recv()
+
+            @pl.when(self.p.c == 0)
+            def _():
+                self.keep().wait()
+
+        self.aside(k).start()
+
+    def steps(self):
+        return [functools.partial(self.arrived, k) for k in range(self.p.zn)]
+
+    def finish(self):
+        @pl.when(self.p.c == 1)
+        def _():
+            self.send(0).wait_send()
+
+        for k in range(self.p.zn):
+            if k:
+                self.send(k).wait_send()
+            self.aside(k).wait_recv()
+            self.aside(k).wait_send()
+
+
+def add_home(p, to, index, first, first_came, second, second_came):
+    pairs = ((first, first_came), (second, second_came))
+    for section, (own, came) in enumerate(pairs):
+
+        @pl.when(p.s == section)
+        def _():
+            to[index] = (own[index].astype(F32) + came[index].astype(F32)).astype(BF16)
+
+
 class Fold:
     def __init__(self, p, src, came, out, ss, rs):
         self.p, self.src, self.came, self.out, self.ss, self.rs = p, src, came, out, ss, rs
@@ -598,6 +668,58 @@
     return copy
 
 
+class Staging:
+    def __init__(self):
+        self.loads, self.stores, self.running = {}, {}, []
+
+    def need(self, *items):
+        for item in items:
+            self.loads.pop(item).wait()
+
+    def done(self, *items):
+        for item in items:
+            self.running.append(fetch(*self.stores.pop(item)))
+
+    def end(self):
+        self.done(*list(self.stores))
+        for copy in self.running:
+            copy.wait()
+
+
+def staged_call(body, name, collective_id, args, shapes, scratch, late=(), plain=(), early=(), raw=()):
+    late, early = tuple(late), tuple(early)
+    n_in, n_out, n_scratch = len(args), len(shapes), len(scratch)
+
+    def run(*refs):
+        ins, outs = list(refs[:n_in]), list(refs[n_in : n_in + n_out])
+        rest = refs[n_in + n_out :]
+        own, rest = rest[:n_scratch], rest[n_scratch:]
+        staged_in, rest = rest[: len(late)], rest[len(late) :]
+        staged_out, sems = rest[: len(early)], rest[len(early) :]
+        io = Staging()
+        for x, item in enumerate(late):
+            io.loads[item] = fetch(ins[item], staged_in[x], sems[0].at[x])
+            ins[item] = staged_in[x]
+        for x, item in enumerate(early):
+            io.stores[item] = (staged_out[x], outs[item], sems[1].at[x])
+            outs[item] = staged_out[x]
+        body(io, *ins, *outs, *own)
+        io.end()
+
+    stages = [pltpu.VMEM(args[item].shape, args[item].dtype) for item in late]
+    stages += [pltpu.VMEM(shapes[item].shape, shapes[item].dtype) for item in early]
+    stages += [DMA((max(len(late), 1),)), DMA((max(len(early), 1),))]
+    return pl.pallas_call(
+        run,
+        out_shape=shapes,
+        in_specs=[ANY_SPEC if i in late + tuple(plain) else VMEM_SPEC for i in range(n_in)],
+        out_specs=[ANY_SPEC if i in early + tuple(raw) else VMEM_SPEC for i in range(n_out)],
+        scratch_shapes=list(scratch) + stages,
+        compiler_params=params(collective_id),
+        name=name,
+    )(*args)
+
+
 def row_blocks(rows, step):
     size = min(rows, 256)
     count = rows // size
@@ -633,39 +755,76 @@
     return [(a, b) for a in range(2) for b in range(n) if (a, b) != (0, 0)]
 
 
-def start_kernel(n, low, width, tok_ref, pack_ref, qkv_ref, out_ref, mask_ref, *refs):
-    normed_to, found_to, qkv_all, out_all, feats_to, qkv_bias, widen_bias = refs[:7]
-    tok_all, pack_all, g_ss, g_rs, g_ls, p_ss, p_rs, a_ss, a_rs, o_ss, o_rs, l_sem = refs[7:]
-    p = Place(n)
-    s, c, h = p.s, p.c, p.h
-    greet_all(p)
-
-    def pack_copy(a, b):
-        target = (lax.rem(s + a, 2), c, lax.rem(h + b, n))
-        return remote(pack_ref, pack_all.at[s, h], p_ss.at[a, b], p_rs.at[a, b], target)
-
-    tokens = Gather(p, tok_ref, tok_all, g_ss, g_rs, g_ls)
-    qkv = Spread(p, qkv_ref, qkv_all, a_ss, a_rs, l_sem.at[1])
-    out = RowSwap(p, out_ref, out_all, o_ss, o_rs, l_sem.at[2])
-    pack_own = pltpu.make_async_copy(pack_ref, pack_all.at[s, h], l_sem.at[0])
-    tokens.start()
-    qkv.start()
-    for a, b in others(n):
-        pack_copy(a, b).start()
-    pack_own.start()
-    out.start()
-    qkv_steps = qkv.steps()
-    for step in tokens.steps():
-        step()
-        if qkv_steps:
-            qkv_steps.pop(0)()
-    tokens.finish()
-    pack_own.wait()
-    for a, b in others(n):
-        pack_copy(a, b).wait_recv()
-    sh = qkv_ref.shape[2] // 3
+def with_gaps(values, n, padded):
+    rows, width = values.shape
     share = width // n
-    padded = qkv_ref.shape[1]
+    pieces = []
+    for j in range(n):
+        pieces.append(values[:, j * share : (j + 1) * share])
+        if padded > share:
+            pieces.append(jnp.zeros((rows, padded - share), values.dtype))
+    return jnp.concatenate(pieces, axis=1)
+
+
+def lay_vectors(vectors, pack_to):
+    lanes = pack_to.shape[1]
+    members = []
+    for ref in vectors:
+        member = ref[...].astype(F32)
+        members.append(
+            jnp.concatenate([member, jnp.zeros((1, lanes - member.shape[1]), F32)], axis=1)
+        )
+    members.append(jnp.zeros((8, lanes), F32))
+    pack_to[...] = jnp.concatenate(members, axis=0).astype(BF16)
+
+
+def lay_first(low, qkv_ref, qkv_to):
+    n, padded, triple = qkv_to.shape
+    share = qkv_ref.shape[0]
+    width = qkv_ref.shape[1] // 3
+    sh = triple // 3
+    for j in range(n):
+        for t in range(3):
+            first = t * width + HD * low[j]
+            qkv_to[j, :share, t * sh : (t + 1) * sh] = qkv_ref[:, first : first + sh]
+        if padded > share:
+            qkv_to[j, share:] = jnp.zeros((padded - share, triple), BF16)
+
+
+def lay_rows(low, out_ref, out_to):
+    share = out_ref.shape[0]
+    sh, full = out_to.shape
+    n = len(low)
+    h = lax.axis_index("shard")
+    offset = 0
+    for j in range(n):
+        offset = offset + jnp.where(h == j, j * share - HD * low[j], 0)
+    rows = with_gaps(out_ref[...].astype(F32), n, full // n)
+    rows = jnp.concatenate([rows, jnp.zeros((sh - share, full), F32)], axis=0)
+    out_to[...] = pltpu.roll(rows, offset, 0).astype(BF16)
+
+
+def lay_widen(j, widen_ref, widen_to):
+    n, padded, hide_full = widen_to.shape
+    share, hidden = widen_ref.shape
+    hide = hidden // n
+    widen_to[j, :share, :hide] = widen_ref[:, j * hide : (j + 1) * hide]
+    if hide_full > hide:
+        widen_to[j, :share, hide:] = jnp.zeros((share, hide_full - hide), BF16)
+    if padded > share:
+        widen_to[j, share:] = jnp.zeros((padded - share, hide_full), BF16)
+
+
+def lay_narrow(first, size, n, narrow_ref, narrow_to):
+    rows = slice(first, first + size)
+    narrow_to[rows] = with_gaps(narrow_ref[rows], n, narrow_to.shape[1] // n)
+
+
+def spread_vectors(n, low, width, pack_all, feats_to, qkv_bias, widen_bias):
+    h = lax.axis_index("shard")
+    sh = qkv_bias.shape[2] // 3
+    share = width // n
+    padded = feats_to.shape[2] // n
     for layer in range(2):
         pieces = [pack_all[layer, j] for j in range(n)]
         feats_to[layer] = jnp.concatenate([m[:, :padded] for m in pieces], axis=1).astype(F32)
@@ -682,144 +841,205 @@
             [found[:, :sh], jnp.zeros((1, sh), F32), found[:, sh:]], axis=1
         )
         widen_bias[layer] = wide
-    unit = unit_rows(tok_all[...].astype(F32), mask_ref[...], width)[0]
-    normed_to[...] = (unit * feats_to[0, 0:1] + feats_to[0, 1:2]).astype(BF16)
-    for step in qkv_steps:
-        step()
-    out.step()
-    qkv.finish()
-    weight = qkv_all[0].reshape(n * padded, 3 * sh)
-    found_to[...] = (dot_n(normed_to[...], weight) + qkv_bias[0]).astype(BF16)
+
+
+def open_kernel(n, low, width, slots, step, io, *refs):
+    tok_ref, cot_ref, vectors, refs = refs[0], refs[1], refs[2:10], refs[10:]
+    qkv_ref, out_ref, widen_ref, narrow_ref, mask, kpos_ref, qpos_ref = refs[:7]
+    refs = refs[7:]
+    narrow_to, x_to, cot_to, grad_to, sums_to, normed_to, own_ref, qkv_all, out_all = refs[:9]
+    feats_to, qkv_bias, widen_bias, att_ref, low_ref, lse_ref, oth_ref, part_to = refs[9:17]
+    widen_all, refs = refs[17], refs[18:]
+    tok_own, pack, qkv_send, out_rows, widen_raw, narrow_raw, widen_send = refs[:7]
+    tok_all, pack_all, refs = refs[7], refs[8], refs[9:]
+    g_ss, g_rs, g_ls, p_ss, p_rs, a_ss, a_rs, w_ss, w_rs, o_ss, o_rs, l_sem = refs[:12]
+    kv_ss, kv_rs = refs[12:]
+    p = Place(n)
+    s, c, h = p.s, p.c, p.h
+    widen_load = fetch(widen_ref, widen_raw, l_sem.at[4])
+    narrow_load = fetch(narrow_ref, narrow_raw, l_sem.at[5])
+    padded = qkv_send.shape[1]
+    tok_own[...] = with_gaps(tok_ref[s], n, padded)
+    greet_all(p)
+
+    def pack_copy(a, b):
+        target = (lax.rem(s + a, 2), c, lax.rem(h + b, n))
+        return remote(pack, pack_all.at[s, h], p_ss.at[a, b], p_rs.at[a, b], target)
+
+    tokens = Gather(p, tok_own, tok_all, g_ss, g_rs, g_ls)
+    qkv = Spread(p, qkv_send, qkv_all, a_ss, a_rs, l_sem.at[1])
+    widen = Spread(p, widen_send, widen_all, w_ss, w_rs, l_sem.at[3])
+    out = RowSwap(p, out_rows, out_all, o_ss, o_rs, l_sem.at[2])
+    pack_own = pltpu.make_async_copy(pack, pack_all.at[s, h], l_sem.at[0])
+    tokens.start()
+    io.need(10)
+    lay_first(low, qkv_ref, qkv_send)
+    qkv.start()
+    lay_vectors(vectors, pack)
     for a, b in others(n):
-        pack_copy(a, b).wait_send()
-    out.finish()
-
-
-def start_call(n, low, width, hide, tok, pack, qkv, out, mask):
-    rows, full = tok.shape
-    zn = n // 2
-    shapes = [
-        jax.ShapeDtypeStruct((n * rows, full), BF16),
-        jax.ShapeDtypeStruct((n * rows, qkv.shape[2]), BF16),
-        jax.ShapeDtypeStruct((2,) + qkv.shape, BF16),
-        jax.ShapeDtypeStruct((2,) + out.shape, BF16),
-        jax.ShapeDtypeStruct((2, 16, full), F32),
-        jax.ShapeDtypeStruct((2, 1, qkv.shape[2]), F32),
-        jax.ShapeDtypeStruct((2, 1, hide), F32),
+        pack_copy(a, b).start()
+    pack_own.start()
+
+    def start_out():
+        io.need(1, 11)
+        lay_rows(low, out_ref, out_rows)
+        out.start()
+
+    def lay_cot():
+        values = with_gaps(cot_ref[s], n, padded)
+        cot_to[...] = values
+        grad_to[...] = values.astype(F32)
+        sums_to[...] = jnp.sum(grad_to[...], axis=0, keepdims=True)
+        x_to[...] = tok_own[...].astype(F32)
+
+    hide = narrow_ref.shape[0]
+    work = [start_out, widen_load.wait]
+    work += [functools.partial(lay_widen, j, widen_raw, widen_send) for j in range(n)]
+    work += [lay_cot, narrow_load.wait]
+    work += [
+        functools.partial(lay_narrow, first, min(208, hide - first), n, narrow_raw, narrow_to)
+        for first in range(0, hide, 208)
     ]
-    return pl.pallas_call(
-        functools.partial(start_kernel, n, low, width),
-        out_shape=shapes,
-        in_specs=[VMEM_SPEC] * 5,
-        out_specs=[VMEM_SPEC] * 7,
-        scratch_shapes=[
-            pltpu.VMEM((n * rows, full), BF16),
-            pltpu.VMEM((2, n) + pack.shape, BF16),
-            DMA((4, zn, HALVES)),
-            DMA((4, zn, HALVES)),
-            DMA((HALVES,)),
-            DMA((2, n)),
-            DMA((2, n)),
-            DMA((4, zn)),
-            DMA((4, zn)),
-            DMA((2,)),
-            DMA((2,)),
-            DMA((3,)),
-        ],
-        compiler_params=params(0),
-        name="start",
-    )(tok, pack, qkv, out, mask)
-
-
-def with_gaps(values, n, padded):
-    rows, width = values.shape
-    share = width // n
-    pieces = []
-    for j in range(n):
-        pieces.append(values[:, j * share : (j + 1) * share])
-        if padded > share:
-            pieces.append(jnp.zeros((rows, padded - share), values.dtype))
-    return jnp.concatenate(pieces, axis=1)
-
-
-def lay_out_kernel(low, qkv_ref, widen_ref, out_ref, narrow_ref, tok_ref, cot_ref, *refs):
-    vectors, outs = refs[:8], refs[8:]
-    qkv_to, widen_to, out_to, narrow_to, pack_to, tok_to, x_to, cot_to, grad_to, sums_to = outs
-    n, padded, hide_full = widen_to.shape
-    share, hidden = widen_ref.shape
-    hide = hidden // n
-    width = qkv_ref.shape[1] // 3
-    sh = qkv_to.shape[2] // 3
-    gap = padded - share
-    s = lax.axis_index("section")
-    h = lax.axis_index("shard")
-    for j in range(n):
-        for t in range(3):
-            first = t * width + HD * low[j]
-            qkv_to[j, :share, t * sh : (t + 1) * sh] = qkv_ref[:, first : first + sh]
-        widen_to[j, :share, :hide] = widen_ref[:, j * hide : (j + 1) * hide]
-        if hide_full > hide:
-            widen_to[j, :share, hide:] = jnp.zeros((share, hide_full - hide), BF16)
-        if gap:
-            qkv_to[j, share:] = jnp.zeros((gap, 3 * sh), BF16)
-            widen_to[j, share:] = jnp.zeros((gap, hide_full), BF16)
-    narrow_to[:hide] = with_gaps(narrow_ref[...], n, padded)
+    qkv_steps = qkv.steps()
+    for token_step in tokens.steps():
+        run_next(work)
+        run_next(work)
+        token_step()
+        run_next(qkv_steps)
+    for rest in work:
+        rest()
     extra = narrow_to.shape[0] - hide
     if extra:
         narrow_to[hide:] = jnp.zeros((extra, n * padded), BF16)
-    offset = 0
-    for j in range(n):
-        offset = offset + jnp.where(h == j, j * share - HD * low[j], 0)
-    rows = with_gaps(out_ref[...].astype(F32), n, padded)
-    rows = jnp.concatenate([rows, jnp.zeros((sh - share, n * padded), F32)], axis=0)
-    out_to[...] = pltpu.roll(rows, offset, 0).astype(BF16)
-    lanes = pack_to.shape[1]
-    members = []
-    for ref in vectors:
-        member = ref[...].astype(F32)
-        members.append(
-            jnp.concatenate([member, jnp.zeros((1, lanes - member.shape[1]), F32)], axis=1)
-        )
-    members.append(jnp.zeros((8, lanes), F32))
-    pack_to[...] = jnp.concatenate(members, axis=0).astype(BF16)
-    for ref, low_to, full_to in ((tok_ref, tok_to, x_to), (cot_ref, cot_to, grad_to)):
-        values = with_gaps(ref[s], n, padded)
-        low_to[...] = values
-        full_to[...] = values.astype(F32)
-    sums_to[...] = jnp.sum(grad_to[...], axis=0, keepdims=True)
-
-
-def lay_out_call(low, slots, padded, qkv, widen, out, narrow, tokens, cotangent, *vectors):
-    n = len(low)
+    io.done(0)
+    tokens.finish()
+    widen.start()
+    pack_own.wait()
+    for a, b in others(n):
+        pack_copy(a, b).wait_recv()
+    spread_vectors(n, low, width, pack_all, feats_to, qkv_bias, widen_bias)
+
+    def first_norm(first, size):
+        some = pl.ds(first, size)
+        unit = unit_rows(tok_all[some].astype(F32), mask[...], width)[0]
+        normed_to[some] = (unit * feats_to[0, 0:1] + feats_to[0, 1:2]).astype(BF16)
+
+    rows = tok_all.shape[0]
+    row_blocks(rows, first_norm)
+    io.done(5)
+    for rest in qkv_steps:
+        rest()
+    qkv.finish()
+    io.done(7)
+    sh = slots * HD
+
+    def project(first, size):
+        some = pl.ds(first, size)
+        weight = qkv_all[0].reshape(n * padded, 3 * sh)
+        own_ref[some] = (dot_n(normed_to[some], weight) + qkv_bias[0]).astype(BF16)
+
+    row_blocks(rows, project)
+    swap = remote(own_ref.at[:, pl.ds(sh, 2 * sh)], oth_ref, kv_ss, kv_rs, p.sibling)
+    swap.start()
+    swap.wait_recv()
+    out.step()
+    between = widen.steps()
+    chunk = attention(slots, step, own_ref, oth_ref, kpos_ref, qpos_ref, att_ref, low_ref, lse_ref)
+    in_blocks(rows, step, chunk, between)
+    out.finish()
+    io.done(6, 8, 12, 13, 15)
+
+    def give(first, size):
+        some = pl.ds(first, size)
+        part_to[some] = dot_n(low_ref[some], out_all[0]).astype(BF16)
+
+    row_blocks(rows, give)
+    io.done(16)
+    for rest in between:
+        rest()
+    for a, b in others(n):
+        pack_copy(a, b).wait_send()
+    swap.wait_send()
+    widen.finish()
+
+
+def open_call(n, low, slots, padded, tokens, cotangent, vectors, weights, mask, kpos, qpos):
+    qkv, out, widen, narrow = weights
     share, hidden = widen.shape
+    width = n * share
+    hide = hidden // n
+    hide_full = -(-hide // 128) * 128
     sh = slots * HD
     full = n * padded
     rows = tokens.shape[1]
-    lanes = max(-(-hidden // n // 128) * 128, -(-2 * share // 128) * 128)
-    return pl.pallas_call(
-        functools.partial(lay_out_kernel, low),
-        out_shape=[
-            jax.ShapeDtypeStruct((n, padded, 3 * sh), BF16),
-            jax.ShapeDtypeStruct((n, padded, -(-hidden // n // 128) * 128), BF16),
-            jax.ShapeDtypeStruct((sh, full), BF16),
-            jax.ShapeDtypeStruct((-(-narrow.shape[0] // 16) * 16, full), BF16),
-            jax.ShapeDtypeStruct((16, lanes), BF16),
-            jax.ShapeDtypeStruct((rows, full), BF16),
-            jax.ShapeDtypeStruct((rows, full), F32),
-            jax.ShapeDtypeStruct((rows, full), BF16),
-            jax.ShapeDtypeStruct((rows, full), F32),
-            jax.ShapeDtypeStruct((1, full), F32),
+    total = n * rows
+    zn = n // 2
+    lanes = max(hide_full, -(-2 * share // 128) * 128)
+    blocks = (n, padded, 3 * sh)
+    wide = (n, padded, hide_full)
+
+    def low_type(*shape):
+        return jax.ShapeDtypeStruct(shape, BF16)
+
+    def full_type(*shape):
+        return jax.ShapeDtypeStruct(shape, F32)
+
+    return staged_call(
+        functools.partial(open_kernel, n, low, width, slots, min(total, 256)),
+        "open",
+        0,
+        (tokens, cotangent, *vectors, qkv, out, widen, narrow, mask, kpos, qpos),
+        [
+            low_type(-(-hide // 16) * 16, full),
+            full_type(rows, full),
+            low_type(rows, full),
+            full_type(rows, full),
+            full_type(1, full),
+            low_type(total, full),
+            low_type(total, 3 * sh),
+            low_type(2, *blocks),
+            low_type(2, sh, full),
+            full_type(2, 16, full),
+            full_type(2, 1, 3 * sh),
+            full_type(2, 1, hide_full),
+            full_type(sh, total),
+            low_type(total, sh),
+            full_type(slots, total),
+            low_type(total, 2 * sh),
+            low_type(total, full),
+            low_type(2, *wide),
         ],
-        in_specs=[VMEM_SPEC] * (6 + len(vectors)),
-        out_specs=[VMEM_SPEC] * 10,
-        compiler_params=params(),
-        name="lay_out",
-    )(qkv, widen, out, narrow, tokens, cotangent, *vectors)
-
-
-def settle_kernel(low, sizes, qkv_ref, widen_ref, out_ref, narrow_ref, vec_ref, came_ref, *refs):
-    streams, (qkv_to, widen_to, out_to, narrow_to, *outs) = refs[:4], refs[4:]
-    stream_to, vectors = outs[:2], outs[2:]
+        [
+            pltpu.VMEM((rows, full), BF16),
+            pltpu.VMEM((16, lanes), BF16),
+            pltpu.VMEM(blocks, BF16),
+            pltpu.VMEM((sh, full), BF16),
+            pltpu.VMEM(widen.shape, BF16),
+            pltpu.VMEM(narrow.shape, BF16),
+            pltpu.VMEM(wide, BF16),
+            pltpu.VMEM((total, full), BF16),
+            pltpu.VMEM((2, n, 16, lanes), BF16),
+        ]
+        + gather_scratch(n)
+        + [DMA((2, n))] * 2
+        + [DMA((4, zn))] * 4
+        + [DMA((2,))] * 2
+        + [DMA((6,)), DMA, DMA],
+        late=(1, 10, 11),
+        plain=(12, 13),
+        early=(0, 5, 6, 7, 8, 12, 13, 15, 16),
+        raw=(17,),
+    )
+
+
+def settle_kernel(low, sizes, *refs):
+    sources, vec_ref, came_ref, streams, refs = refs[:4], refs[4], refs[5], refs[6:10], refs[10:]
+    outs, stream_to, vectors, refs = refs[:4], refs[4:6], refs[6:14], refs[14:]
+    loaded, made, in_sem, out_sem = refs[:4], refs[4:8], refs[8], refs[9]
+    qkv_ref, widen_ref, out_ref, narrow_ref = loaded
+    qkv_to, widen_to, out_to, narrow_to = made
+    order = (3, 1, 0, 2)
+    loads = {i: fetch(sources[i], loaded[i], in_sem.at[i]) for i in order}
     n, padded, _ = widen_ref.shape
     share = out_to.shape[0]
     hide = narrow_to.shape[0]
@@ -831,20 +1051,40 @@
         pieces = [values[:, j * padded : j * padded + share] for j in range(n)]
         return jnp.concatenate(pieces, axis=1)
 
-    qkv_to[...] = jnp.zeros_like(qkv_to)
-    for j in range(n):
-        for t in range(3):
-            first = t * width + HD * low[j]
-            qkv_to[:, first : first + sh] += qkv_ref[j, :share, t * sh : (t + 1) * sh].astype(F32)
-        widen_to[:, j * hide : (j + 1) * hide] = widen_ref[j, :share, :hide].astype(F32)
-    for ref, to in ((out_ref, out_to), (narrow_ref, narrow_to)):
+    def lay_rows_back(ref, to):
         to[...] = without_gaps(ref[: to.shape[0]].astype(F32))
+
+    def lay_qkv_back():
+        qkv_to[...] = jnp.zeros_like(qkv_to)
+        for j in range(n):
+            for t in range(3):
+                first = t * width + HD * low[j]
+                block = qkv_ref[j, :share, t * sh : (t + 1) * sh]
+                qkv_to[:, first : first + sh] += block.astype(F32)
+
+    def lay_widen_back():
+        for j in range(n):
+            widen_to[:, j * hide : (j + 1) * hide] = widen_ref[j, :share, :hide].astype(F32)
+
+    makers = (
+        lay_qkv_back,
+        lay_widen_back,
+        functools.partial(lay_rows_back, out_ref, out_to),
+        functools.partial(lay_rows_back, narrow_ref, narrow_to),
+    )
     for item, to in enumerate(stream_to):
         first, second = (ref[...] for ref in streams[2 * item : 2 * item + 2])
         to[s] = without_gaps(jnp.where(s == 0, first, second))
         to[1 - s] = without_gaps(came_ref[item].astype(F32))
     for row, (size, to) in enumerate(zip(sizes, vectors)):
         to[...] = vec_ref[row : row + 1, :size]
+    stores = []
+    for i in order:
+        loads[i].wait()
+        makers[i]()
+        stores.append(fetch(made[i], outs[i], out_sem.at[i]))
+    for store in stores:
+        store.wait()
 
 
 def settle_call(low, share, hide, qkv, widen, out, narrow, vec, came, *streams):
@@ -852,19 +1092,20 @@
     width = n * share
     rows = came.shape[1]
     sizes = [share] * 6 + [2 * share, hide]
+    big = [(share, 3 * width), (share, n * hide), (share, width), (hide, width)]
     return pl.pallas_call(
         functools.partial(settle_kernel, low, sizes),
-        out_shape=[
-            jax.ShapeDtypeStruct((share, 3 * width), F32),
-            jax.ShapeDtypeStruct((share, n * hide), F32),
-            jax.ShapeDtypeStruct((share, width), F32),
-            jax.ShapeDtypeStruct((hide, width), F32),
+        out_shape=[jax.ShapeDtypeStruct(shape, F32) for shape in big]
+        + [
             jax.ShapeDtypeStruct((2, rows, width), F32),
             jax.ShapeDtypeStruct((2, rows, width), F32),
         ]
         + [jax.ShapeDtypeStruct((1, size), F32) for size in sizes],
-        in_specs=[VMEM_SPEC] * 10,
-        out_specs=[VMEM_SPEC] * 14,
+        in_specs=[ANY_SPEC] * 4 + [VMEM_SPEC] * 6,
+        out_specs=[ANY_SPEC] * 4 + [VMEM_SPEC] * 10,
+        scratch_shapes=[pltpu.VMEM(m.shape, BF16) for m in (qkv, widen, out, narrow)]
+        + [pltpu.VMEM(shape, F32) for shape in big]
+        + [DMA((4,)), DMA((4,))],
         compiler_params=params(),
         name="settle",
     )(qkv, widen, out, narrow, vec, came, *streams)
@@ -884,12 +1125,15 @@
     return (inner - mean - unit * along) * scale
 
 
-def forward_kernel(n, width, layer, side, *refs):
+def forward_kernel(n, width, layer, side, io, *refs):
     middle = layer is not None
-    part, base, bias, gain, shift, mask = refs[:6]
-    refs = refs[6:]
+    part, base, feats, mask = refs[:4]
+    refs = refs[4:]
     if middle:
+        bias, gain, shift = (feats[layer, row : row + 1] for row in (2, 3, 4))
         widen_all, narrow_in, widen_bias, refs = refs[0], refs[1], refs[2], refs[3:]
+    else:
+        bias, gain, shift = feats[0, 5:6], feats[1, 0:1], feats[1, 1:2]
     value_to, low_all, refs = refs[0], refs[1], refs[2:]
     if middle:
         pre_to, hidden_to, part_to, refs = refs[0], refs[1], refs[2], refs[3:]
@@ -905,6 +1149,7 @@
         widen, load_sems, rest = refs[9], refs[10], refs[11:]
         loads.append(fetch(widen_all.at[layer], widen, load_sems.at[0]))
         if side:
+            io.need(5)
             job = RowSwap(p, narrow_in, side_out, *rest)
             job.start()
             filled = narrow_in.shape[0]
@@ -921,9 +1166,9 @@
 
     def rows_step(half):
         rows = slice(half * hr, (half + 1) * hr)
-        value = base[rows] + (scatter.result(half) + bias[...])
+        value = base[rows] + (scatter.result(half) + bias)
         value_to[rows] = value
-        own[rows] = (unit_rows(value, mask[...], width)[0] * gain[...] + shift[...]).astype(BF16)
+        own[rows] = (unit_rows(value, mask[...], width)[0] * gain + shift).astype(BF16)
 
     by_halves(scatter, gather, rows_step, [])
     if side:
@@ -933,12 +1178,14 @@
         load.wait()
     if side:
         job.finish()
+        io.done(5)
     if middle:
+        io.done(1)
 
         def block(first, size):
             rows = pl.ds(first, size)
             weight = widen[...].reshape(low_all.shape[1], widen.shape[2])
-            pre = dot_n(low_all[rows], weight) + widen_bias[...]
+            pre = dot_n(low_all[rows], weight) + widen_bias[layer]
             pre_to[rows] = pre
             hidden = (0.5 * pre * (1.0 + gelu_parts(pre)[0])).astype(BF16)
             hidden_to[rows] = hidden
@@ -974,11 +1221,9 @@
     ]
     scratch = scatter_scratch(n, rows, full)
     scratch += [pltpu.VMEM((rows, full), BF16)] + gather_scratch(n)
-    in_specs = [VMEM_SPEC] * (1 + len(local))
     if layer is not None:
         widen, narrow, _ = feed
         hide = widen.shape[3]
-        in_specs += [ANY_SPEC, VMEM_SPEC if carry else ANY_SPEC, VMEM_SPEC]
         shapes += [
             jax.ShapeDtypeStruct((total_rows, hide), F32),
             jax.ShapeDtypeStruct((total_rows, hide), BF16),
@@ -990,15 +1235,19 @@
             scratch += [DMA((2,)), DMA((2,)), DMA]
         else:
             scratch.append(pltpu.VMEM((hide, full), BF16))
-    return pl.pallas_call(
+    middle = layer is not None
+    return staged_call(
         functools.partial(forward_kernel, n, width, layer, carry),
-        out_shape=shapes,
-        in_specs=in_specs,
-        out_specs=[VMEM_SPEC] * len(shapes),
-        scratch_shapes=scratch,
-        compiler_params=params(collective_id),
-        name="forward_rows",
-    )(part, *local, *feed)
+        "forward_rows",
+        collective_id,
+        (part, *local, *feed),
+        shapes,
+        scratch,
+        late=(5,) if carry else (),
+        plain=((4,) if carry else (4, 5)) if middle else (),
+        early=((1, 2, 3, 4, 5) if carry else (1, 2, 3, 4)) if middle else (),
+        raw=() if middle else (1,),
+    )
 
 
 def back_rows(scatter, half, base, grad, gain, mask, width):
@@ -1006,14 +1255,15 @@
     rows = slice(half * hr, (half + 1) * hr)
     total = scatter.result(half)
     unit, scale = unit_rows(base[rows], mask[...], width)
-    value = grad[rows] + norm_back(total, unit, scale, gain[...], width)
+    value = grad[rows] + norm_back(total, unit, scale, gain, width)
     low = value.astype(BF16)
     terms = (total * unit, total, low.astype(F32))
     return rows, value, low, [jnp.sum(term, axis=0, keepdims=True) for term in terms]
 
 
-def resid_kernel(n, width, layer, *refs):
-    base, grad, gain, mask, normed, hidden_pre, hidden, outs, widen_all, narrow_all = refs[:10]
+def resid_kernel(n, width, layer, io, *refs):
+    base, grad, feats, mask, normed, hidden_pre, hidden, outs, widen_all, narrow_all = refs[:10]
+    gain = feats[layer, 3:4]
     value_to, sums_to, low_all, wide_to, wide_came, slim_to, pre_sums = refs[10:17]
     refs = refs[17:]
     own, g_ss, g_rs, g_ls = refs[5:9]
@@ -1027,6 +1277,7 @@
     greet(p, line=True, over=True, sibling=True)
     for load in loads:
         load.wait()
+    io.need(5, 7)
 
     def block(first, size):
         rows = pl.ds(first, size)
@@ -1051,11 +1302,17 @@
     def pre_sum():
         pre_sums[...] = jnp.sum(pre[...].astype(F32), axis=0, keepdims=True)
 
+    io.need(4, 6)
     for step in product(normed, pre, wide):
         step()
     wide_fold.start()
-    work = product(hidden, outs, slim) + wide_fold.steps() + [cross.start, slim_fold.start, pre_sum]
-    work += slim_fold.steps()
+
+    def wide_done():
+        cross.start()
+        io.done(3)
+
+    work = product(hidden, outs, slim) + wide_fold.steps() + [wide_done, slim_fold.start, pre_sum]
+    work += slim_fold.steps() + [functools.partial(io.done, 5)]
     sums = []
 
     def rows_step(half):
@@ -1083,9 +1340,12 @@
     wide = (zn, full // n, hidden.shape[1])
     half = -(-hide // 32) * 16
     slim = (1, half, full)
-    return pl.pallas_call(
+    return staged_call(
         functools.partial(resid_kernel, n, width, layer),
-        out_shape=[
+        "back_resid",
+        collective_id,
+        args,
+        [
             jax.ShapeDtypeStruct((rows, full), F32),
             jax.ShapeDtypeStruct((3, full), F32),
             jax.ShapeDtypeStruct((total_rows, full), BF16),
@@ -1094,9 +1354,7 @@
             jax.ShapeDtypeStruct(slim, BF16),
             jax.ShapeDtypeStruct((1, hidden.shape[1]), F32),
         ],
-        in_specs=[VMEM_SPEC] * 8 + [ANY_SPEC] * 2,
-        out_specs=[VMEM_SPEC] * 7,
-        scratch_shapes=scatter_scratch(n, rows, full)
+        scatter_scratch(n, rows, full)
         + [pltpu.VMEM((rows, full), BF16)]
         + gather_scratch(n)
         + fold_scratch((full, hidden.shape[1]), wide)
@@ -1109,13 +1367,16 @@
             pltpu.VMEM(narrow.shape[1:], BF16),
             DMA((2,)),
         ],
-        compiler_params=params(collective_id),
-        name="back_resid",
-    )(*args)
-
-
-def input_kernel(n, width, source, low, *refs):
-    part, base, grad, gain, mask, normed, triple, att, resid, slim = refs[:10]
+        late=(4, 5, 6, 7),
+        plain=(8, 9),
+        early=(3, 5),
+        raw=(2, 4),
+    )
+
+
+def input_kernel(n, width, source, low, io, *refs):
+    part, base, grad, feats, mask, normed, triple, att, resid, slim = refs[:10]
+    gain = feats[1, 0:1]
     value_to, sums_to, low_all, qkv_to, out_to, slim_came, triple_sums = refs[10:17]
     refs = refs[17:]
     own, g_ss, g_rs, g_ls = refs[5:9]
@@ -1133,9 +1394,11 @@
     def triple_sum():
         triple_sums[...] = jnp.sum(triple[...].astype(F32), axis=0, keepdims=True)
 
-    work = product(normed, triple, qkv) + [qkv_fold.start]
+    work = [functools.partial(io.need, 5, 6)] + product(normed, triple, qkv)
+    work += [qkv_fold.start, functools.partial(io.need, 7, 8)]
     work += [functools.partial(home_rows, att, resid, out, low, width // n), out_fold.start]
-    work += qkv_fold.steps() + [triple_sum] + out_fold.steps()
+    work += qkv_fold.steps() + [functools.partial(io.done, 3), triple_sum]
+    work += out_fold.steps() + [functools.partial(io.done, 4)]
     sums = []
 
     def rows_step(half):
@@ -1154,16 +1417,19 @@
         job.finish()
 
 
-def input_call(n, collective_id, width, source, low, part, base, grad, gain, mask, *operands):
+def input_call(n, collective_id, width, source, low, part, base, grad, feats, mask, *operands):
     normed, triple, att, resid, slim = operands
     total_rows, full = part.shape
     rows = total_rows // n
     zn = n // 2
     qkv = (zn, full // n, triple.shape[1])
     out = (1, att.shape[1] // 2, full)
-    return pl.pallas_call(
+    return staged_call(
         functools.partial(input_kernel, n, width, source, low),
-        out_shape=[
+        "back_input",
+        collective_id,
+        (part, base, grad, feats, mask) + operands,
+        [
             jax.ShapeDtypeStruct((rows, full), F32),
             jax.ShapeDtypeStruct((3, full), F32),
             jax.ShapeDtypeStruct((total_rows, full), BF16),
@@ -1172,37 +1438,29 @@
             jax.ShapeDtypeStruct(slim.shape, BF16),
             jax.ShapeDtypeStruct((1, triple.shape[1]), F32),
         ],
-        in_specs=[VMEM_SPEC] * 10,
-        out_specs=[VMEM_SPEC] * 7,
-        scratch_shapes=scatter_scratch(n, rows, full)
+        scatter_scratch(n, rows, full)
         + [pltpu.VMEM((rows, full), BF16)]
         + gather_scratch(n)
         + fold_scratch((full, triple.shape[1]), qkv)
         + fold_scratch((att.shape[1], full), out)
         + [DMA, DMA],
-        compiler_params=params(collective_id),
-        name="back_input",
-    )(part, base, grad, gain, mask, *operands)
-
-
-def finale_kernel(n, width, low, *refs):
-    part, base, grad, gain, mask, normed, triple, att, resid = refs[:9]
-    wides, wide_cames, slims, slim_came, qkv_far, out_far, vecs = (
-        refs[9:11],
-        refs[11:13],
-        refs[13:15],
-        refs[15],
-        refs[16],
-        refs[17],
-        refs[18:25],
+        late=(5, 6, 7, 8),
+        plain=(9,),
+        early=(3, 4),
+        raw=(2, 5),
     )
-    layer_outs, upper_d_in, refs = refs[25:27], refs[27], refs[28:]
-    value_to, wide_to, slim_to, qkv_to, out_to, vec_to, streams_to = refs[:7]
-    refs = refs[7:]
+
+
+def finale_kernel(n, width, low, io, *refs):
+    part, base, grad, feats, mask, normed, triple, att, resid = refs[:9]
+    slims, slim_cames, qkv_far, out_far, vecs = refs[9:11], refs[11:13], refs[13], refs[14], refs[15:22]
+    layer_outs, upper_d_in, refs = refs[22:24], refs[24], refs[25:]
+    value_to, slim_to, qkv_to, out_to, vec_to, streams_to = refs[:6]
+    refs = refs[6:]
     qkv, qkv_fold_in, qkv_ss, qkv_rs, out, out_fold_in, out_ss, out_rs = refs[5:13]
     qkv_own, qkv_in, qkv_sum, out_own, out_in, out_sum = refs[13:19]
-    wide_sum, slim_in, slim_sum, vec, vec_in, vec_sum, vec_sib, streams = refs[19:27]
-    a_ss, a_rs, x_ss, x_rs, v_ss, v_rs, r_ss, r_rs, ls = refs[27:]
+    slim_sum, slim_pair, vec, vec_in, vec_sum, vec_sib, streams = refs[19:26]
+    a_ss, a_rs, x_ss, x_rs, v_ss, v_rs, r_ss, r_rs, ls = refs[26:]
     p = Place(n)
     s, c, h, z, zn = p.s, p.c, p.h, p.z, p.zn
     share = width // n
@@ -1210,38 +1468,21 @@
     scatter = Scatter(p, part, *refs[:5])
     scatter.start()
 
-    @pl.when(s == 0)
-    def _():
-        wide_sum[...] = (wides[0][...].astype(F32) + wide_cames[0][...].astype(F32)).astype(BF16)
-
-    @pl.when(s == 1)
-    def _():
-        wide_sum[...] = (wides[1][...].astype(F32) + wide_cames[1][...].astype(F32)).astype(BF16)
-
-    spreads = ((wide_sum, wide_to), (qkv_sum, qkv_to))
-
-    def send(w, k):
-        far = p.flip(k)
-        src, dst = spreads[w]
-        target = (s, c, far * 2 + p.far_y)
-        return remote(src.at[far], dst.at[h], a_ss.at[0, w, k], a_rs.at[0, w, k], target)
-
-    def keep(w):
-        src, dst = spreads[w]
-        return pltpu.make_async_copy(src.at[z], dst.at[h], ls.at[w])
-
-    def aside(w, k):
-        block = spreads[w][1].at[p.flip(k) * 2 + p.far_y]
-        return remote(block, block, a_ss.at[1, w, k], a_rs.at[1, w, k], p.sibling)
-
-    def start_zero(w):
-        @pl.when(c == 1)
+    slim_loads = [
+        (
+            pltpu.make_async_copy(slims[layer], slim_pair.at[0], ls.at[1]),
+            pltpu.make_async_copy(slim_cames[layer], slim_pair.at[1], ls.at[4]),
+        )
+        for layer in range(2)
+    ]
+    for section, loads in enumerate(slim_loads):
+
+        @pl.when(s == section)
         def _():
-            send(w, 0).start()
-
-        @pl.when(c == 0)
-        def _():
-            keep(w).start()
+            for load in loads:
+                load.start()
+
+    back = Home(p, qkv_sum, qkv_to, a_ss, a_rs, ls.at[0])
 
     def x_block(k, src=qkv_far):
         far = p.flip(k)
@@ -1251,7 +1492,6 @@
         return remote(src, out_in, x_ss.at[zn], x_rs.at[zn], p.over)
 
     stream_cross = remote(streams, streams_to, x_ss.at[zn + 1], x_rs.at[zn + 1], p.over)
-    slim_cross = Cross(p, slims[0], slim_in, x_ss.at[zn + 2], x_rs.at[zn + 2], 1)
 
     def start_far():
         @pl.when(s == 0)
@@ -1273,21 +1513,21 @@
     qkv_fold = Fold(p, qkv, qkv_fold_in, qkv_own, qkv_ss, qkv_rs)
     out_fold = Fold(p, out, out_fold_in, out_own, out_ss, out_rs)
 
-    start_zero(0)
-    for k in range(1, zn):
-        send(0, k).start()
+    io.need(13, 14)
     start_far()
+    io.need(5, 6)
     for step in product(normed, triple, qkv):
         step()
     qkv_fold.start()
+    io.need(7, 8)
     work = [functools.partial(home_rows, att, resid, out, low, share), out_fold.start]
     work += qkv_fold.steps()
     work += [functools.partial(start_own, k) for k in list(range(1, zn)) + [0]]
-    work += out_fold.steps() + [start_own_out, slim_cross.start]
+    work += out_fold.steps() + [start_own_out]
     sums = []
 
     def rows_step(half):
-        rows, value, lower, terms = back_rows(scatter, half, base, grad, gain, mask, width)
+        rows, value, lower, terms = back_rows(scatter, half, base, grad, feats[0, 0:1], mask, width)
         value_to[rows] = value
         sums.append(jnp.concatenate(terms, axis=0))
 
@@ -1295,8 +1535,10 @@
     for rest in work:
         rest()
 
+    io.need(22, 23, 24)
     streams[0] = jnp.where(s == 0, layer_outs[1][...], layer_outs[0][...]).astype(BF16)
     streams[1] = jnp.where(s == 0, upper_d_in[...], value_to[...]).astype(BF16)
+    io.done(0)
     stream_cross.start()
 
     ones = (sum(sums), vecs[0][...])
@@ -1344,34 +1586,15 @@
     for a, b in others(n):
         vec_copy(a, b).start()
 
-    def add(to, index, first, second, came):
-        @pl.when(s == 0)
-        def _():
-            to[index] = (first[index].astype(F32) + came[index].astype(F32)).astype(BF16)
-
-        @pl.when(s == 1)
-        def _():
-            to[index] = (second[index].astype(F32) + came[index].astype(F32)).astype(BF16)
-
     for k in list(range(1, zn)) + [0]:
         x_block(k).wait_recv()
-        add(qkv_sum, p.flip(k), qkv_own, qkv_far, qkv_in)
-        if k:
-            send(1, k).start()
-        else:
-            start_zero(1)
+        add_home(p, qkv_sum, p.flip(k), qkv_own, qkv_in, qkv_far, qkv_in)
+        back.start(k)
     out_cross().wait_recv()
-    add(out_sum, 0, out_own, out_far, out_in)
-
-    @pl.when(s == 0)
-    def _():
-        slim_cross.copy.wait_recv()
-        slim_sum[0] = (slims[0][0].astype(F32) + slim_in[0].astype(F32)).astype(BF16)
-
-    @pl.when(s == 1)
-    def _():
-        slim_cross.copy.wait_send()
-        slim_sum[0] = (slims[1][0].astype(F32) + slim_came[0].astype(F32)).astype(BF16)
+    add_home(p, out_sum, 0, out_own, out_in, out_far, out_in)
+    for load in slim_loads[0]:
+        load.wait()
+    slim_sum[0] = (slim_pair[0, 0].astype(F32) + slim_pair[1, 0].astype(F32)).astype(BF16)
 
     def row_copies(w, src, dst):
         half = src.shape[1]
@@ -1391,34 +1614,12 @@
     vec_sum[...] = total
     vec_share = remote(vec_sum, vec_sib, r_ss.at[2], r_rs.at[2], p.sibling)
     vec_share.start()
-    for w in range(2):
-
-        @pl.when(c == 1)
-        def _():
-            send(w, 0).wait_recv()
-
-        @pl.when(c == 0)
-        def _():
-            keep(w).wait()
-
-        for k in range(zn):
-            if k:
-                send(w, k).wait_recv()
-            aside(w, k).start()
+    for step in back.steps():
+        step()
     vec_share.wait_recv()
     vec_to[...] = total + vec_sib[...]
     vec_share.wait_send()
-    for w in range(2):
-
-        @pl.when(c == 1)
-        def _():
-            send(w, 0).wait_send()
-
-        for k in range(zn):
-            if k:
-                send(w, k).wait_send()
-            aside(w, k).wait_recv()
-            aside(w, k).wait_send()
+    back.finish()
     for w in range(2):
         copies[2 * w].wait()
         copies[2 * w + 1].wait_recv()
@@ -1436,52 +1637,53 @@
 
 def finale_call(n, collective_id, width, low, *args):
     part, triple, att = args[0], args[6], args[7]
-    wide, slim, lanes = args[9].shape, args[13].shape, args[22].shape[1]
+    slim, lanes = args[9].shape, args[19].shape[1]
     total_rows, full = part.shape
     rows = total_rows // n
     zn = n // 2
     qkv = (zn, full // n, triple.shape[1])
     out = (1, att.shape[1] // 2, full)
-    return pl.pallas_call(
+    return staged_call(
         functools.partial(finale_kernel, n, width, low),
-        out_shape=[
+        "finale",
+        collective_id,
+        args,
+        [
             jax.ShapeDtypeStruct((rows, full), F32),
-            jax.ShapeDtypeStruct((n,) + wide[1:], BF16),
             jax.ShapeDtypeStruct((2 * slim[1], full), BF16),
             jax.ShapeDtypeStruct((n,) + qkv[1:], BF16),
             jax.ShapeDtypeStruct((2 * out[1], full), BF16),
             jax.ShapeDtypeStruct((8, lanes), F32),
             jax.ShapeDtypeStruct((2, rows, full), BF16),
         ],
-        in_specs=[VMEM_SPEC] * len(args),
-        out_specs=[VMEM_SPEC] + [ANY_SPEC] * 4 + [VMEM_SPEC] * 2,
-        scratch_shapes=scatter_scratch(n, rows, full)
+        scatter_scratch(n, rows, full)
         + fold_scratch((full, triple.shape[1]), qkv)
         + fold_scratch((att.shape[1], full), out)
         + [pltpu.VMEM(qkv, BF16)] * 3
         + [pltpu.VMEM(out, BF16)] * 3
         + [
-            pltpu.VMEM(wide, BF16),
             pltpu.VMEM(slim, BF16),
-            pltpu.VMEM(slim, BF16),
+            pltpu.VMEM((2,) + slim, BF16),
             pltpu.VMEM((2, n, 8, lanes), F32),
             pltpu.VMEM((2, n, 8, lanes), F32),
             pltpu.VMEM((8, lanes), F32),
             pltpu.VMEM((8, lanes), F32),
             pltpu.VMEM((2, rows, full), BF16),
-            DMA((2, 2, zn)),
-            DMA((2, 2, zn)),
-            DMA((zn + 3,)),
-            DMA((zn + 3,)),
+            DMA((2, zn)),
+            DMA((2, zn)),
+            DMA((zn + 2,)),
+            DMA((zn + 2,)),
             DMA((2, n)),
             DMA((2, n)),
             DMA((3,)),
             DMA((3,)),
-            DMA((4,)),
+            DMA((5,)),
         ],
-        compiler_params=params(collective_id),
-        name="finale",
-    )(*args)
+        late=(5, 6, 7, 8, 13, 14, 22, 23, 24),
+        plain=(9, 10, 11, 12),
+        early=(0,),
+        raw=(1, 2, 3, 5),
+    )
 
 
 def dot_t(a, b):
@@ -1513,46 +1715,10 @@
         between.pop(0)()
 
 
-def attend_kernel(n, slots, step, layer, side, *refs):
-    kpos_ref, qpos_ref, carried, out_all = refs[:4]
-    refs = refs[4:]
-    if layer:
-        normed, qkv_all, qkv_bias = refs[:3]
-        refs = refs[3:]
-    else:
-        own_ref, refs = refs[0], refs[1:]
-    att_ref, low_ref, lse_ref, oth_ref, part_to, carried_to = refs[:6]
-    refs = refs[6:]
-    if layer:
-        own_ref, refs = refs[0], refs[1:]
-    kv_ss, kv_rs, out_weight, load_sems = refs[:4]
-    refs = refs[4:]
-    if layer:
-        qkv_weight, refs = refs[0], refs[1:]
-        qkv_load = fetch(qkv_all.at[layer], qkv_weight, load_sems.at[1])
-    out_load = fetch(out_all.at[layer], out_weight, load_sems.at[0])
-    p = Place(n)
+def attention(slots, step, own_ref, oth_ref, kpos_ref, qpos_ref, att_ref, low_ref, lse_ref):
     rows = own_ref.shape[0]
     sh = slots * HD
     power = HD**-0.5 * LOG2E
-    if side == "spread":
-        greet(p, spread=True, over=True, sibling=True)
-    else:
-        greet(p, line=True, sibling=True)
-    job = (Spread if side == "spread" else Gather)(p, carried, carried_to, *refs)
-    job.start()
-    if layer:
-        qkv_load.wait()
-
-        def project(first, size):
-            some = pl.ds(first, size)
-            weight = qkv_weight[...].reshape(normed.shape[1], 3 * sh)
-            own_ref[some] = (dot_n(normed[some], weight) + qkv_bias[...]).astype(BF16)
-
-        row_blocks(rows, project)
-    swap = remote(own_ref.at[:, pl.ds(sh, 2 * sh)], oth_ref, kv_ss, kv_rs, p.sibling)
-    swap.start()
-    swap.wait_recv()
 
     def at(base, slot):
         return slice(base + slot * HD, base + (slot + 1) * HD)
@@ -1587,7 +1753,37 @@
             lse_ref[slot : slot + 1, q_rows] = top * power + jnp.log(total) * LOG2E
             run_next(between)
 
+    return chunk
+
+
+def attend_kernel(n, slots, step, layer, io, *refs):
+    kpos_ref, qpos_ref, carried, out_all, normed, qkv_all, qkv_bias = refs[:7]
+    att_ref, low_ref, lse_ref, oth_ref, part_to, carried_to, own_ref = refs[7:14]
+    kv_ss, kv_rs, out_weight, qkv_weight, load_sems = refs[14:19]
+    qkv_load = fetch(qkv_all.at[layer], qkv_weight, load_sems.at[1])
+    out_load = fetch(out_all.at[layer], out_weight, load_sems.at[0])
+    p = Place(n)
+    rows = own_ref.shape[0]
+    sh = slots * HD
+    greet(p, line=True, sibling=True)
+    job = Gather(p, carried, carried_to, *refs[19:])
+    job.start()
+    qkv_load.wait()
+    io.need(4)
     between = job.steps()
+
+    def project(first, size):
+        some = pl.ds(first, size)
+        weight = qkv_weight[...].reshape(normed.shape[1], 3 * sh)
+        own_ref[some] = (dot_n(normed[some], weight) + qkv_bias[layer]).astype(BF16)
+
+    row_blocks(rows, project)
+    swap = remote(own_ref.at[:, pl.ds(sh, 2 * sh)], oth_ref, kv_ss, kv_rs, p.sibling)
+    swap.start()
+    run_next(between)
+    run_next(between)
+    swap.wait_recv()
+    chunk = attention(slots, step, own_ref, oth_ref, kpos_ref, qpos_ref, att_ref, low_ref, lse_ref)
     in_blocks(rows, step, chunk, between)
     out_load.wait()
 
@@ -1596,58 +1792,59 @@
         part_to[some] = dot_n(low_ref[some], out_weight[...]).astype(BF16)
 
     row_blocks(rows, give)
+    io.done(0, 1, 4, 6)
     for rest in between:
         rest()
     swap.wait_send()
     job.finish()
 
 
-def attend_call(n, collective_id, slots, layer, side, kpos, qpos, carried, out_all, *source):
+def attend_call(n, collective_id, slots, layer, kpos, qpos, carried, out_all, *source):
     rows = qpos.shape[1]
-    zn = n // 2
     sh = slots * HD
     full = out_all.shape[2]
-    step = min(rows, 256)
-    if side == "spread":
-        moved = jax.ShapeDtypeStruct((2,) + carried.shape, BF16)
-        scratch = [DMA((4, zn)), DMA((4, zn)), DMA]
-    else:
-        moved = jax.ShapeDtypeStruct((n * carried.shape[0], carried.shape[1]), BF16)
-        scratch = gather_scratch(n)
-    shapes = [
-        jax.ShapeDtypeStruct((sh, rows), F32),
-        jax.ShapeDtypeStruct((rows, sh), BF16),
-        jax.ShapeDtypeStruct((slots, rows), F32),
-        jax.ShapeDtypeStruct((rows, 2 * sh), BF16),
-        jax.ShapeDtypeStruct((rows, full), BF16),
-        moved,
-    ]
-    in_specs = [VMEM_SPEC] * 3 + [ANY_SPEC, VMEM_SPEC]
-    kept = [DMA, DMA, pltpu.VMEM((sh, full), BF16), DMA((2,))]
-    if layer:
-        in_specs += [ANY_SPEC, VMEM_SPEC]
-        shapes.append(jax.ShapeDtypeStruct((rows, 3 * sh), BF16))
-        kept.append(pltpu.VMEM(source[1].shape[1:], BF16))
-    return pl.pallas_call(
-        functools.partial(attend_kernel, n, slots, step, layer, side),
-        out_shape=shapes,
-        in_specs=in_specs,
-        out_specs=[VMEM_SPEC] * len(shapes),
-        scratch_shapes=kept + scratch,
-        compiler_params=params(collective_id),
-        name="attend_" + side,
-    )(kpos, qpos, carried, out_all, *source)
-
-
-def attend_back_kernel(n, slots, step, layer, last, *refs):
+    return staged_call(
+        functools.partial(attend_kernel, n, slots, min(rows, 256), layer),
+        "attend",
+        collective_id,
+        (kpos, qpos, carried, out_all, *source),
+        [
+            jax.ShapeDtypeStruct((sh, rows), F32),
+            jax.ShapeDtypeStruct((rows, sh), BF16),
+            jax.ShapeDtypeStruct((slots, rows), F32),
+            jax.ShapeDtypeStruct((rows, 2 * sh), BF16),
+            jax.ShapeDtypeStruct((rows, full), BF16),
+            jax.ShapeDtypeStruct((n * carried.shape[0], full), BF16),
+            jax.ShapeDtypeStruct((rows, 3 * sh), BF16),
+        ],
+        [
+            DMA,
+            DMA,
+            pltpu.VMEM((sh, full), BF16),
+            pltpu.VMEM(source[1].shape[1:], BF16),
+            DMA((2,)),
+        ]
+        + gather_scratch(n),
+        late=(4,),
+        plain=(3, 5),
+        early=(0, 1, 4, 6),
+        raw=(5,),
+    )
+
+
+def attend_back_kernel(n, slots, step, layer, last, home, io, *refs):
     own_ref, oth_ref, resid, att_ref, lse_ref, kpos_ref, qpos_ref, out_all, qkv_all = refs[:9]
     refs = refs[9:]
     if last:
-        part_ref, base_ref, bias_ref = refs[:3]
+        part_ref, base_ref, feats = refs[:3]
         refs = refs[3:]
+    if home:
+        wides, slim, refs = refs[:4], refs[4], refs[5:]
     triple_ref, part_to, refs = refs[0], refs[1], refs[2:]
     if last:
         value_ref, refs = refs[0], refs[1:]
+    if home:
+        wide_to, slim_came, refs = refs[0], refs[1], refs[2:]
     dq_t, dkv_own, dkv_oth, came, kv_ss, kv_rs = refs[:6]
     grad_ref, out_weight, qkv_weight, load_sems = refs[6:10]
     out_load = fetch(out_all.at[layer], out_weight, load_sems.at[0])
@@ -1656,12 +1853,40 @@
     rows = own_ref.shape[0]
     sh = slots * HD
     scale = HD**-0.5
-    greet(p, line=last, sibling=True)
+    greet(p, line=last, sibling=True, spread=home, over=home)
     between = []
     if last:
         scatter = Scatter(p, part_ref, *refs[10:])
         scatter.start()
         between = scatter.steps()
+    if home:
+        wide_sum, wide_pair, a_ss, a_rs, ls, x_ss, x_rs = refs[10:]
+        wide_loads = [
+            [
+                pltpu.make_async_copy(wides[2 * layer + i], wide_pair.at[i], ls.at[1 + i])
+                for i in range(2)
+            ]
+            for layer in range(2)
+        ]
+        for section, loads in enumerate(wide_loads):
+
+            @pl.when(p.s == section)
+            def _():
+                for load in loads:
+                    load.start()
+
+        cross = Cross(p, slim, slim_came, x_ss, x_rs, 1)
+        cross.start()
+        back = Home(p, wide_sum, wide_to, a_ss, a_rs, ls.at[0])
+        for load in wide_loads[0]:
+            load.wait()
+        for k in list(range(1, p.zn)) + [0]:
+            far = p.flip(k)
+            total = wide_pair[0, far].astype(F32) + wide_pair[1, far].astype(F32)
+            wide_sum[far] = total.astype(BF16)
+            back.start(k)
+        between = back.steps()
+    io.need(2)
     out_load.wait()
 
     def enter(first, size):
@@ -1669,6 +1894,7 @@
         grad_ref[some] = dot_t(resid[some], out_weight[...]).astype(BF16)
 
     row_blocks(rows, enter)
+    io.need(0, 1, 3)
 
     def at(base, slot):
         return slice(base + slot * HD, base + (slot + 1) * HD)
@@ -1714,7 +1940,7 @@
         for half in range(HALVES):
             part_rows = slice(half * hr, (half + 1) * hr)
             total = scatter.result(half)
-            value_ref[part_rows] = base_ref[part_rows] + (total + bias_ref[...])
+            value_ref[part_rows] = base_ref[part_rows] + (total + feats[1, 5:6])
         scatter.finish()
 
     swap.wait_recv()
@@ -1726,13 +1952,20 @@
         weight = qkv_weight[...].reshape(part_to.shape[1], 3 * sh)
         part_to[some] = dot_t(triple_ref[some], weight).astype(BF16)
 
+    io.done(0)
     row_blocks(rows, leave)
+    io.done(1)
     if last:
         finish_last()
+    if home:
+        for rest in between:
+            rest()
+        back.finish()
+        cross.finish()
     swap.wait_send()
 
 
-def attend_back_call(n, collective_id, slots, layer, *args, last=()):
+def attend_back_call(n, collective_id, slots, layer, *args, last=(), home=()):
     qkv, out_all, qkv_all = args[0], args[7], args[8]
     rows = qkv.shape[0]
     sh = slots * HD
@@ -1753,15 +1986,26 @@
     if last:
         shapes.append(jax.ShapeDtypeStruct(last[1].shape, F32))
         scratch += scatter_scratch(n, *last[1].shape)
-    return pl.pallas_call(
-        functools.partial(attend_back_kernel, n, slots, step, layer, bool(last)),
-        out_shape=shapes,
-        in_specs=[VMEM_SPEC] * 7 + [ANY_SPEC] * 2 + [VMEM_SPEC] * len(last),
-        out_specs=[VMEM_SPEC] * len(shapes),
-        scratch_shapes=scratch,
-        compiler_params=params(collective_id),
-        name="attend_back",
-    )(*args, *last)
+    if home:
+        wide, slim = home[0].shape, home[4].shape
+        shapes += [
+            jax.ShapeDtypeStruct((n,) + wide[1:], BF16),
+            jax.ShapeDtypeStruct(slim, BF16),
+        ]
+        scratch += [pltpu.VMEM(wide, BF16), pltpu.VMEM((2,) + wide, BF16)]
+        scratch += [DMA((2, n // 2)), DMA((2, n // 2)), DMA((3,)), DMA, DMA]
+    return staged_call(
+        functools.partial(attend_back_kernel, n, slots, step, layer, bool(last), bool(home)),
+        "attend_back",
+        collective_id,
+        args + tuple(last) + tuple(home),
+        shapes,
+        scratch,
+        late=(0, 1, 2, 3),
+        plain=(7, 8) + (tuple(range(9, 14)) if home else ()),
+        early=(0, 1),
+        raw=(2, 3) if home else (),
+    )
 
 
 def windows(width, n):
@@ -1799,32 +2043,6 @@
     half_rows = rows // HALVES
 
     mask = jnp.asarray(np.arange(full)[None] % padded < share, F32)
-    qkv_send, widen_send, out_send, narrow_send, pack, own_tokens, x, own_cot, out_grad, out_sums = (
-        lay_out_call(
-            low,
-            slots,
-            padded,
-            qkv_weight,
-            widen_weight,
-            out_weight,
-            narrow_weight,
-            tokens,
-            cotangent,
-            first_gain[None],
-            first_shift[None],
-            out_bias[None],
-            second_gain[None],
-            second_shift[None],
-            narrow_bias[None],
-            input_bias[None],
-            widen_bias[None],
-        )
-    )
-    hide_full = widen_send.shape[2]
-    normed, qkv, qkv_all, out_all, feats, qkv_bias, widen_biases = start_call(
-        n, low, width, widen_send.shape[2], own_tokens, pack, qkv_send, out_send, mask
-    )
-
     order = block_order.reshape(2, n, HALVES).transpose(0, 2, 1)
     places = order[..., None] * half_rows + jnp.arange(half_rows, dtype=jnp.int32)
     places = places.reshape(2, total_rows)
@@ -1833,45 +2051,64 @@
     kpos = jnp.concatenate([own_places, oth_places])[:, None]
     qpos = own_places[None, :]
 
-    layers = [
-        dict(
-            gain1=feats[layer, 0:1],
-            shift1=feats[layer, 1:2],
-            out_bias=feats[layer, 2:3],
-            gain2=feats[layer, 3:4],
-            shift2=feats[layer, 4:5],
-            narrow_bias=feats[layer, 5:6],
-            qkv_bias=qkv_bias[layer],
-            widen_bias=widen_biases[layer],
-        )
-        for layer in range(2)
-    ]
-
+    (
+        narrow_send,
+        x,
+        own_cot,
+        out_grad,
+        out_sums,
+        normed,
+        qkv,
+        qkv_all,
+        out_all,
+        feats,
+        qkv_bias,
+        widen_biases,
+        *attended,
+        widen_all,
+    ) = open_call(
+        n,
+        low,
+        slots,
+        padded,
+        tokens,
+        cotangent,
+        [
+            member[None]
+            for member in (
+                first_gain,
+                first_shift,
+                out_bias,
+                second_gain,
+                second_shift,
+                narrow_bias,
+                input_bias,
+                widen_bias,
+            )
+        ],
+        (qkv_weight, out_weight, widen_weight, narrow_weight),
+        mask,
+        kpos,
+        qpos,
+    )
     stored = []
     layer_outs = []
     for layer in range(2):
-        w = layers[layer]
         if layer:
-            found = attend_call(
-                n, 2, slots, 1, "gather", kpos, qpos, own_cot, out_all, normed, qkv_all, w["qkv_bias"]
+            *attended, out_low_all, qkv = attend_call(
+                n, 2, slots, 1, kpos, qpos, own_cot, out_all, normed, qkv_all, qkv_bias
             )
-            out_low_all, qkv = found[5:]
-        else:
-            found = attend_call(n, 1, slots, 0, "spread", kpos, qpos, widen_send, out_all, qkv)
-            widen_all = found[5]
-        att, att_low, lse, other, part = found[:5]
+        att, att_low, lse, other, part = attended
         found = forward_call(
             n,
             3 + layer,
             width,
             part,
             x,
-            w["out_bias"],
-            w["gain2"],
-            w["shift2"],
+            feats,
             mask,
             layer=layer,
-            feed=(widen_all, narrow_all if layer else narrow_send, w["widen_bias"]),
+            feed=(widen_all, narrow_all if layer else narrow_send, widen_biases),
             carry=not layer,
         )
         residual, normed_two, hidden_pre, hidden_low, part = found[:5]
@@ -1879,25 +2116,13 @@
         stored[-1] += (hidden_pre, hidden_low)
         if layer == 0:
             narrow_all = found[5]
-            nxt = layers[1]
-            x, normed = forward_call(
-                n,
-                5,
-                width,
-                part,
-                residual,
-                w["narrow_bias"],
-                nxt["gain1"],
-                nxt["shift1"],
-                mask,
-            )
+            x, normed = forward_call(n, 5, width, part, residual, feats, mask)
             layer_outs.append(x)
         else:
-            last = (part, residual, w["narrow_bias"])
+            last = (part, residual, feats)
 
     found = {}
     for layer in (1, 0):
-        w = layers[layer]
         x, normed, qkv, other, att, att_low, lse, residual, normed_two = stored[layer][:9]
         hidden_pre, hidden_low = stored[layer][9:]
         resid_grad, sums_two, resid_low_all, wide, wide_came, slim, pre_sums = resid_call(
@@ -1908,7 +2133,7 @@
             hide,
             residual,
             out_grad,
-            w["gain2"],
+            feats,
             mask,
             normed_two,
             hidden_pre,
@@ -1932,9 +2157,10 @@
             out_all,
             qkv_all,
             last=last if layer else (),
+            home=() if layer else (wide, wide_came) + found[1][:2] + (slim,),
         )
         triple, part = back[:2]
-        local = (part, x, resid_grad, w["gain1"], mask, normed, triple, att_low, resid_low_all)
+        local = (part, x, resid_grad, feats, mask, normed, triple, att_low, resid_low_all)
         found[layer] = (wide, wide_came, slim, sums_two, pre_sums)
         if layer:
             layer_outs.append(back[2])
@@ -1943,18 +2169,16 @@
             )
             out_grad = upper_d_in
     lower, upper = found[0], found[1]
-    d_in, widen_back, narrow_back, qkv_back, out_back, vec, came = finale_call(
+    widen_back, slim_back = back[2:]
+    d_in, narrow_back, qkv_back, out_back, vec, came = finale_call(
         n,
         12,
         width,
         low,
         *local,
-        lower[0],
-        upper[0],
-        lower[1],
-        upper[1],
         lower[2],
         upper[2],
+        slim_back,
         slim_came,
         qkv_grad,
         out_rows,

time: 631 us -> 581 us (0.921)
  Pallas kernels: 617 us -> 569 us
    pallas_call x13 -> x11, Pallas kernels: 603 us -> 557 us  [staged_call(): pl.pallas_call(run, out_shape=shapes, in_specs=[ANY_SPEC if i in late + t...]
where the time goes in v3:
time: 581 us; the launch traced here: 573 us
  Pallas kernels  569 us (98%)
    pallas_call x11, Pallas kernels, staged_call(): pl.pallas_call(run, out_shape=shapes, in_specs=[ANY_SPEC if i in late + t...  557 us

profile of v3, /device:TPU:0, one launch (start us, length us, event | category | flops | bytes accessed | tf_op | source)
XLA Modules:
  0.0 572.8 jit_solution(6595541870173385481)
XLA Ops:
  0.7 0.7 broadcast_multiply_fusion
  1.3 0.1 mul.15
  1.4 0.1 iota_add_fusion
  1.5 0.1 select_n.32
  1.6 0.7 select_n.33.refs_16_.refs_1_.refs_6_
  2.2 0.1 select_n.30
  2.3 1.0 copy.32.refs_15_.refs_0_.refs_5_
  3.4 105.1 %open.1 = (bf16[800,1664]{1,0:T(8,128)(2,1)}, f32[64,1664]{1,0:T(8,128)}, bf16[64,1664]{1,0:T(8,128)(2,1)}, f32[64,1664]{1,0:T(8,128)}, f32[1,1664]{1,0:T(1,128)...) custom-call(bf16[2,64,1600]{2,1,0:T(8,128)(2,1)} %refs_0_.1, ...), custom_call_target="tpu_custom_call" | custom-call | tf_op jit(solution)/shard_map/open/pallas_call | solution.py:712
  108.5 49.0 %forward_rows.3 = (f32[64,1664]{1,0:T(8,128)}, bf16[512,1664]{1,0:T(8,128)(2,1)}, f32[512,896]{1,0:T(8,128)}, bf16[512,896]{1,0:T(8,128)(2,1)}, bf16[512,1664]{1...) custom-call(bf16[512,1664]{1,0:T(8,128)(2,1)} %get-tuple-element.102.refs_0_, f32[64,1664]{1,0:T(8,128)} %get-tuple-element.103.refs_1_, ...), custom_call_target="tpu_custom_call" | custom-call | tf_op jit(solution)/shard_map/forward_rows/pallas_call | solution.py:712
  157.5 42.4 %forward_rows.4 = (f32[64,1664]{1,0:T(8,128)}, bf16[512,1664]{1,0:T(8,128)(2,1)}) custom-call(bf16[512,1664]{1,0:T(8,128)(2,1)} %get-tuple-element.111.refs_0_, f32[64,1664]{1,0:T(8,128)} %get-tuple-element.108.refs_1_.refs_0_, f32[2,16,1664]{2,1,0:T(8,128)} %get-tuple-element.104.refs_2_.refs_11_.refs_3_, f32[1,1664]{1,0:T(1,128)} %constant.12.clone.refs_14_.refs_3_.refs_4_), custom_call_target="tpu_custom_call" | custom-call | tf_op jit(solution)/shard_map/forward_rows/pallas_call | solution.py:712
  200.0 24.8 %attend.1 = (f32[256,512]{1,0:T(8,128)}, bf16[512,256]{1,0:T(8,128)(2,1)}, f32[4,512]{1,0:T(4,128)}, bf16[512,512]{1,0:T(8,128)(2,1)}, bf16[512,1664]{1,0:T(8,12...) custom-call(s32[1024,1]{1,0:T(8,128)} %copy.32.refs_15_.refs_0_.refs_5_, ...), custom_call_target="tpu_custom_call" | custom-call | tf_op jit(solution)/shard_map/attend/pallas_call | solution.py:712
  224.7 47.8 %forward_rows.5 = (f32[64,1664]{1,0:T(8,128)}, bf16[512,1664]{1,0:T(8,128)(2,1)}, f32[512,896]{1,0:T(8,128)}, bf16[512,896]{1,0:T(8,128)(2,1)}, bf16[512,1664]{1,0:T(8,128)(2,1)}) custom-call(bf16[512,1664]{1,0:T(8,128)(2,1)} %get-tuple-element.117.refs_0_, f32[64,1664]{1,0:T(8,128)} %get-tuple-element.118.refs_1_.refs_22_.refs_6_, ...), custom_call_target="tpu_custom_call" | custom-call | tf_op jit(solution)/shard_map/forward_rows/pallas_call | solution.py:712
  272.6 52.6 %back_resid.2 = (f32[64,1664]{1,0:T(8,128)}, f32[3,1664]{1,0:T(4,128)}, bf16[512,1664]{1,0:T(8,128)(2,1)}, bf16[4,208,896]{2,1,0:T(8,128)(2,1)}, bf16[4,208,896]...) custom-call(f32[64,1664]{1,0:T(8,128)} %get-tuple-element.120.refs_0_.refs_10_, ...), custom_call_target="tpu_custom_call" | custom-call | tf_op jit(solution)/shard_map/back_resid/pallas_call | solution.py:712
  325.1 25.7 %attend_back.2 = (bf16[512,768]{1,0:T(8,128)(2,1)}, bf16[512,1664]{1,0:T(8,128)(2,1)}, f32[64,1664]{1,0:T(8,128)}) custom-call(bf16[512,768]{1,0:T(8,128)(2,1)} %get-tuple-element.115.refs_0_, bf16[512,512]{1,0:T(8,128)(2,1)} %get-tuple-element.116.refs_1_, bf16[512,1664]{1,0:T(8,128)(2,1)} %get-tuple-element.126.refs_2_.refs_8_, ...), custom_call_target="tpu_custom_call" | custom-call | tf_op jit(solution)/shard_map/attend_back/pallas_call | solution.py:712
  350.9 44.1 %back_input.1 = (f32[64,1664]{1,0:T(8,128)}, f32[3,1664]{1,0:T(4,128)}, bf16[512,1664]{1,0:T(8,128)(2,1)}, bf16[4,208,768]{2,1,0:T(8,128)(2,1)}, bf16[1,128,1664...) custom-call(bf16[512,1664]{1,0:T(8,128)(2,1)} %get-tuple-element.130.refs_0_, ...), custom_call_target="tpu_custom_call" | custom-call | tf_op jit(solution)/shard_map/back_input/pallas_call | solution.py:712
  395.0 52.9 %back_resid.3 = (f32[64,1664]{1,0:T(8,128)}, f32[3,1664]{1,0:T(4,128)}, bf16[512,1664]{1,0:T(8,128)(2,1)}, bf16[4,208,896]{2,1,0:T(8,128)(2,1)}, bf16[4,208,896]...) custom-call(f32[64,1664]{1,0:T(8,128)} %get-tuple-element.108.refs_1_.refs_0_, ...), custom_call_target="tpu_custom_call" | custom-call | tf_op jit(solution)/shard_map/back_resid/pallas_call | solution.py:712
  447.9 40.4 %attend_back.3 = (bf16[512,768]{1,0:T(8,128)(2,1)}, bf16[512,1664]{1,0:T(8,128)(2,1)}, bf16[8,208,896]{2,1,0:T(8,128)(2,1)}, bf16[1,400,1664]{2,1,0:T(8,128)(2,1)}) custom-call(bf16[512,768]{1,0:T(8,128)(2,1)} %get-tuple-element.100.refs_0_, bf16[512,512]{1,0:T(8,128)(2,1)} %get-tuple-element.101.refs_1_, ...), custom_call_target="tpu_custom_call" | custom-call | tf_op jit(solution)/shard_map/attend_back/pallas_call | solution.py:712
  488.3 72.6 %finale.1 = (f32[64,1664]{1,0:T(8,128)}, bf16[800,1664]{1,0:T(8,128)(2,1)}, bf16[8,208,768]{2,1,0:T(8,128)(2,1)}, bf16[256,1664]{1,0:T(8,128)(2,1)}, f32[8,896]{1,0:T(8,128)}, /*index=5*/bf16[2,64,1664]{2,1,0:T(8,128)(2,1)}) custom-call(bf16[512,1664]{1,0:T(8,128)(2,1)} %get-tuple-element.148.refs_0_, f32[64,1664]{1,0:T(8,128)} %get-tuple-element.103.refs_1_, ...), custom_call_target="tpu_custom_call" | custom-call | tf_op jit(solution)/shard_map/finale/pallas_call | solution.py:712
  560.9 11.4 %settle.1 = (f32[200,4800]{1,0:T(8,128)}, f32[200,6400]{1,0:T(8,128)}, f32[200,1600]{1,0:T(8,128)}, f32[800,1600]{1,0:T(8,128)}, f32[2,64,1600]{2,1,0:T(8,128)},...) custom-call(bf16[8,208,768]{2,1,0:T(8,128)(2,1)} %get-tuple-element., ...), custom_call_target="tpu_custom_call" | custom-call | tf_op jit(solution)/shard_map/settle/pallas_call | solution.py:1096
  (3 shorter events, 0.0 us)

commit v4 on v3

--- a/solution.py
+++ b/solution.py
@@ -686,7 +686,9 @@
             copy.wait()
 
 
-def staged_call(body, name, collective_id, args, shapes, scratch, late=(), plain=(), early=(), raw=()):
+def staged_call(
+    body, name, collective_id, args, shapes, scratch, late=(), plain=(), early=(), raw=(), layers={}
+):
     late, early = tuple(late), tuple(early)
     n_in, n_out, n_scratch = len(args), len(shapes), len(scratch)
 
@@ -698,7 +700,8 @@
         staged_out, sems = rest[: len(early)], rest[len(early) :]
         io = Staging()
         for x, item in enumerate(late):
-            io.loads[item] = fetch(ins[item], staged_in[x], sems[0].at[x])
+            src = ins[item].at[layers[item]] if item in layers else ins[item]
+            io.loads[item] = fetch(src, staged_in[x], sems[0].at[x])
             ins[item] = staged_in[x]
         for x, item in enumerate(early):
             io.stores[item] = (staged_out[x], outs[item], sems[1].at[x])
@@ -706,7 +709,9 @@
         body(io, *ins, *outs, *own)
         io.end()
 
-    stages = [pltpu.VMEM(args[item].shape, args[item].dtype) for item in late]
+    stages = [
+        pltpu.VMEM(args[item].shape[1 if item in layers else 0 :], args[item].dtype) for item in late
+    ]
     stages += [pltpu.VMEM(shapes[item].shape, shapes[item].dtype) for item in early]
     stages += [DMA((max(len(late), 1),)), DMA((max(len(early), 1),))]
     return pl.pallas_call(
@@ -843,17 +848,32 @@
         widen_bias[layer] = wide
 
 
+def feed_forward(low_all, widen, narrow, widen_bias, pre_to, hidden_to, part_to):
+    def block(first, size):
+        rows = pl.ds(first, size)
+        weight = widen[...].reshape(low_all.shape[1], widen.shape[2])
+        pre = dot_n(low_all[rows], weight) + widen_bias
+        pre_to[rows] = pre
+        hidden = (0.5 * pre * (1.0 + gelu_parts(pre)[0])).astype(BF16)
+        hidden_to[rows] = hidden
+        part_to[rows] = dot_n(hidden, narrow[...]).astype(BF16)
+
+    row_blocks(low_all.shape[0], block)
+
+
 def open_kernel(n, low, width, slots, step, io, *refs):
     tok_ref, cot_ref, vectors, refs = refs[0], refs[1], refs[2:10], refs[10:]
     qkv_ref, out_ref, widen_ref, narrow_ref, mask, kpos_ref, qpos_ref = refs[:7]
     refs = refs[7:]
-    narrow_to, x_to, cot_to, grad_to, sums_to, normed_to, own_ref, qkv_all, out_all = refs[:9]
-    feats_to, qkv_bias, widen_bias, att_ref, low_ref, lse_ref, oth_ref, part_to = refs[9:17]
-    widen_all, refs = refs[17], refs[18:]
-    tok_own, pack, qkv_send, out_rows, widen_raw, narrow_raw, widen_send = refs[:7]
-    tok_all, pack_all, refs = refs[7], refs[8], refs[9:]
+    x_to, cot_to, grad_to, sums_to, normed_to, own_ref, qkv_all, out_all = refs[:8]
+    feats_to, qkv_bias, widen_bias, att_ref, low_ref, lse_ref, oth_ref, widen_all = refs[8:16]
+    value_to, tok_all, pre_to, hidden_to, part_to, narrow_all = refs[16:22]
+    refs = refs[22:]
+    tok_own, pack, qkv_send, out_rows, widen_raw, narrow_raw, widen_send, narrow_to = refs[:8]
+    pack_all, widen, refs = refs[8], refs[9], refs[10:]
     g_ss, g_rs, g_ls, p_ss, p_rs, a_ss, a_rs, w_ss, w_rs, o_ss, o_rs, l_sem = refs[:12]
-    kv_ss, kv_rs = refs[12:]
+    kv_ss, kv_rs, n_ss, n_rs, refs = refs[12], refs[13], refs[14], refs[15], refs[16:]
+    scatter_refs, (second_ss, second_rs, second_ls) = refs[:5], refs[5:]
     p = Place(n)
     s, c, h = p.s, p.c, p.h
     widen_load = fetch(widen_ref, widen_raw, l_sem.at[4])
@@ -868,7 +888,8 @@
 
     tokens = Gather(p, tok_own, tok_all, g_ss, g_rs, g_ls)
     qkv = Spread(p, qkv_send, qkv_all, a_ss, a_rs, l_sem.at[1])
-    widen = Spread(p, widen_send, widen_all, w_ss, w_rs, l_sem.at[3])
+    wide = Spread(p, widen_send, widen_all, w_ss, w_rs, l_sem.at[3])
+    narrow = RowSwap(p, narrow_to, narrow_all, n_ss, n_rs, l_sem.at[6])
     out = RowSwap(p, out_rows, out_all, o_ss, o_rs, l_sem.at[2])
     pack_own = pltpu.make_async_copy(pack, pack_all.at[s, h], l_sem.at[0])
     tokens.start()
@@ -911,56 +932,95 @@
     extra = narrow_to.shape[0] - hide
     if extra:
         narrow_to[hide:] = jnp.zeros((extra, n * padded), BF16)
-    io.done(0)
+    for member in range(2):
+        if narrow_all.shape[1] > narrow_to.shape[0]:
+            spare = (narrow_all.shape[1] - narrow_to.shape[0], n * padded)
+            narrow_all[member, narrow_to.shape[0] :] = jnp.zeros(spare, BF16)
     tokens.finish()
-    widen.start()
+    wide.start()
     pack_own.wait()
     for a, b in others(n):
         pack_copy(a, b).wait_recv()
     spread_vectors(n, low, width, pack_all, feats_to, qkv_bias, widen_bias)
 
+    normed = part_to
+
     def first_norm(first, size):
         some = pl.ds(first, size)
         unit = unit_rows(tok_all[some].astype(F32), mask[...], width)[0]
-        normed_to[some] = (unit * feats_to[0, 0:1] + feats_to[0, 1:2]).astype(BF16)
+        normed[some] = (unit * feats_to[0, 0:1] + feats_to[0, 1:2]).astype(BF16)
 
     rows = tok_all.shape[0]
     row_blocks(rows, first_norm)
-    io.done(5)
+    normed_store = fetch(normed, normed_to, l_sem.at[7])
     for rest in qkv_steps:
         rest()
     qkv.finish()
-    io.done(7)
+    narrow.start()
+    io.done(6)
     sh = slots * HD
 
     def project(first, size):
         some = pl.ds(first, size)
         weight = qkv_all[0].reshape(n * padded, 3 * sh)
-        own_ref[some] = (dot_n(normed_to[some], weight) + qkv_bias[0]).astype(BF16)
+        own_ref[some] = (dot_n(normed[some], weight) + qkv_bias[0]).astype(BF16)
 
     row_blocks(rows, project)
     swap = remote(own_ref.at[:, pl.ds(sh, 2 * sh)], oth_ref, kv_ss, kv_rs, p.sibling)
     swap.start()
     swap.wait_recv()
     out.step()
-    between = widen.steps()
+    wide_steps = wide.steps()
     chunk = attention(slots, step, own_ref, oth_ref, kpos_ref, qpos_ref, att_ref, low_ref, lse_ref)
-    in_blocks(rows, step, chunk, between)
+    in_blocks(rows, step, chunk, [])
     out.finish()
-    io.done(6, 8, 12, 13, 15)
+    io.done(5, 7, 11, 12, 14)
+    normed_store.wait()
 
     def give(first, size):
         some = pl.ds(first, size)
         part_to[some] = dot_n(low_ref[some], out_all[0]).astype(BF16)
 
     row_blocks(rows, give)
-    io.done(16)
-    for rest in between:
-        rest()
+
+    scatter = Scatter(p, part_to, *scatter_refs)
+    scatter.start()
+    arrivals, crossings = wide_steps[: p.zn], wide_steps[p.zn :]
+    early = len(arrivals) // 2
+    for arrive in arrivals[:early]:
+        arrive()
+    second = Gather(p, tok_own, tok_all, second_ss, second_rs, second_ls)
+    hr = tok_own.shape[0] // HALVES
+
+    def rows_step(half):
+        some = slice(half * hr, (half + 1) * hr)
+        value = x_to[some] + (scatter.result(half) + feats_to[0, 2:3])
+        value_to[some] = value
+        unit = unit_rows(value, mask[...], width)[0]
+        tok_own[some] = (unit * feats_to[0, 3:4] + feats_to[0, 4:5]).astype(BF16)
+
+    by_halves(scatter, None, lambda half: None, [])
+    for arrive in arrivals[early:]:
+        arrive()
+    for half in range(HALVES):
+        rows_step(half)
+        second.start([half])
+    for second_step in second.steps():
+        second_step()
+    narrow.step()
+    for crossing in crossings:
+        crossing()
+    second.finish()
+    scatter.finish()
     for a, b in others(n):
         pack_copy(a, b).wait_send()
     swap.wait_send()
-    widen.finish()
+    narrow.finish()
+    wide.finish()
+    load = fetch(widen_all.at[0], widen, l_sem.at[4])
+    io.done(17, 21)
+    load.wait()
+    feed_forward(tok_all, widen, narrow_all.at[0], widen_bias[0], pre_to, hidden_to, part_to)
 
 
 def open_call(n, low, slots, padded, tokens, cotangent, vectors, weights, mask, kpos, qpos):
@@ -990,7 +1050,6 @@
         0,
         (tokens, cotangent, *vectors, qkv, out, widen, narrow, mask, kpos, qpos),
         [
-            low_type(-(-hide // 16) * 16, full),
             full_type(rows, full),
             low_type(rows, full),
             full_type(rows, full),
@@ -1006,8 +1065,13 @@
             low_type(total, sh),
             full_type(slots, total),
             low_type(total, 2 * sh),
+            low_type(2, *wide),
+            full_type(rows, full),
             low_type(total, full),
-            low_type(2, *wide),
+            full_type(total, hide_full),
+            low_type(total, hide_full),
+            low_type(total, full),
+            low_type(2, hide_full, full),
         ],
         [
             pltpu.VMEM((rows, full), BF16),
@@ -1017,18 +1081,21 @@
             pltpu.VMEM(widen.shape, BF16),
             pltpu.VMEM(narrow.shape, BF16),
             pltpu.VMEM(wide, BF16),
-            pltpu.VMEM((total, full), BF16),
+            pltpu.VMEM((-(-hide // 16) * 16, full), BF16),
             pltpu.VMEM((2, n, 16, lanes), BF16),
+            pltpu.VMEM(wide, BF16),
         ]
         + gather_scratch(n)
         + [DMA((2, n))] * 2
         + [DMA((4, zn))] * 4
         + [DMA((2,))] * 2
-        + [DMA((6,)), DMA, DMA],
+        + [DMA((8,)), DMA, DMA, DMA((2,)), DMA((2,))]
+        + scatter_scratch(n, rows, full)
+        + gather_scratch(n),
         late=(1, 10, 11),
         plain=(12, 13),
-        early=(0, 5, 6, 7, 8, 12, 13, 15, 16),
-        raw=(17,),
+        early=(5, 6, 7, 11, 12, 14, 17, 18, 19, 20, 21),
+        raw=(4, 15),
     )
 
 
@@ -1052,7 +1119,7 @@
         return jnp.concatenate(pieces, axis=1)
 
     def lay_rows_back(ref, to):
-        to[...] = without_gaps(ref[: to.shape[0]].astype(F32))
+        to[...] = without_gaps(ref[: to.shape[0]]).astype(F32)
 
     def lay_qkv_back():
         qkv_to[...] = jnp.zeros_like(qkv_to)
@@ -1063,8 +1130,8 @@
                 qkv_to[:, first : first + sh] += block.astype(F32)
 
     def lay_widen_back():
-        for j in range(n):
-            widen_to[:, j * hide : (j + 1) * hide] = widen_ref[j, :share, :hide].astype(F32)
+        pieces = [widen_ref[j, :share, :hide] for j in range(n)]
+        widen_to[...] = jnp.concatenate(pieces, axis=1).astype(F32)
 
     makers = (
         lay_qkv_back,
@@ -1125,42 +1192,28 @@
     return (inner - mean - unit * along) * scale
 
 
-def forward_kernel(n, width, layer, side, io, *refs):
+def forward_kernel(n, width, layer, io, *refs):
     middle = layer is not None
     part, base, feats, mask = refs[:4]
     refs = refs[4:]
     if middle:
         bias, gain, shift = (feats[layer, row : row + 1] for row in (2, 3, 4))
-        widen_all, narrow_in, widen_bias, refs = refs[0], refs[1], refs[2], refs[3:]
+        widen_all, narrow_all, widen_bias, refs = refs[0], refs[1], refs[2], refs[3:]
     else:
         bias, gain, shift = feats[0, 5:6], feats[1, 0:1], feats[1, 1:2]
     value_to, low_all, refs = refs[0], refs[1], refs[2:]
     if middle:
         pre_to, hidden_to, part_to, refs = refs[0], refs[1], refs[2], refs[3:]
-    if side:
-        side_out, refs = refs[0], refs[1:]
     own, g_ss, g_rs, g_ls = refs[5:9]
     p = Place(n)
-    greet(p, line=True, over=side, sibling=side)
+    greet(p, line=True)
     scatter = Scatter(p, part, *refs[:5])
     scatter.start()
     loads = []
     if middle:
-        widen, load_sems, rest = refs[9], refs[10], refs[11:]
+        widen, narrow, load_sems = refs[9:]
         loads.append(fetch(widen_all.at[layer], widen, load_sems.at[0]))
-        if side:
-            io.need(5)
-            job = RowSwap(p, narrow_in, side_out, *rest)
-            job.start()
-            filled = narrow_in.shape[0]
-            for member in range(2):
-                if side_out.shape[1] > filled:
-                    spare = (side_out.shape[1] - filled, side_out.shape[2])
-                    side_out[member, filled:] = jnp.zeros(spare, BF16)
-            narrow = side_out.at[layer]
-        else:
-            narrow = rest[0]
-            loads.append(fetch(narrow_in.at[layer], narrow, load_sems.at[1]))
+        loads.append(fetch(narrow_all.at[layer], narrow, load_sems.at[1]))
     gather = Gather(p, own, low_all, g_ss, g_rs, g_ls)
     hr = own.shape[0] // HALVES
 
@@ -1171,27 +1224,12 @@
         own[rows] = (unit_rows(value, mask[...], width)[0] * gain + shift).astype(BF16)
 
     by_halves(scatter, gather, rows_step, [])
-    if side:
-        job.step()
     gather.finish()
     for load in loads:
         load.wait()
-    if side:
-        job.finish()
-        io.done(5)
     if middle:
         io.done(1)
-
-        def block(first, size):
-            rows = pl.ds(first, size)
-            weight = widen[...].reshape(low_all.shape[1], widen.shape[2])
-            pre = dot_n(low_all[rows], weight) + widen_bias[layer]
-            pre_to[rows] = pre
-            hidden = (0.5 * pre * (1.0 + gelu_parts(pre)[0])).astype(BF16)
-            hidden_to[rows] = hidden
-            part_to[rows] = dot_n(hidden, narrow[...]).astype(BF16)
-
-        row_blocks(low_all.shape[0], block)
+        feed_forward(low_all, widen, narrow, widen_bias[layer], pre_to, hidden_to, part_to)
     scatter.finish()
 
 
@@ -1212,7 +1250,7 @@
     return [DMA((4, zn, HALVES)), DMA((4, zn, HALVES)), DMA((HALVES,))]
 
 
-def forward_call(n, collective_id, width, part, *local, layer=None, feed=(), carry=False):
+def forward_call(n, collective_id, width, part, *local, layer=None, feed=()):
     total_rows, full = part.shape
     rows = total_rows // n
     shapes = [
@@ -1221,7 +1259,8 @@
     ]
     scratch = scatter_scratch(n, rows, full)
     scratch += [pltpu.VMEM((rows, full), BF16)] + gather_scratch(n)
-    if layer is not None:
+    middle = layer is not None
+    if middle:
         widen, narrow, _ = feed
         hide = widen.shape[3]
         shapes += [
@@ -1229,23 +1268,16 @@
             jax.ShapeDtypeStruct((total_rows, hide), BF16),
             jax.ShapeDtypeStruct((total_rows, full), BF16),
         ]
-        scratch += [pltpu.VMEM(widen.shape[1:], BF16), DMA((2,))]
-        if carry:
-            shapes.append(jax.ShapeDtypeStruct((2, hide, full), BF16))
-            scratch += [DMA((2,)), DMA((2,)), DMA]
-        else:
-            scratch.append(pltpu.VMEM((hide, full), BF16))
-    middle = layer is not None
+        scratch += [pltpu.VMEM(widen.shape[1:], BF16), pltpu.VMEM((hide, full), BF16), DMA((2,))]
     return staged_call(
-        functools.partial(forward_kernel, n, width, layer, carry),
+        functools.partial(forward_kernel, n, width, layer),
         "forward_rows",
         collective_id,
         (part, *local, *feed),
         shapes,
         scratch,
-        late=(5,) if carry else (),
-        plain=((4,) if carry else (4, 5)) if middle else (),
-        early=((1, 2, 3, 4, 5) if carry else (1, 2, 3, 4)) if middle else (),
+        plain=(4, 5) if middle else (),
+        early=(1, 2, 3, 4) if middle else (),
         raw=() if middle else (1,),
     )
 
@@ -1262,24 +1294,18 @@
 
 
 def resid_kernel(n, width, layer, io, *refs):
-    base, grad, feats, mask, normed, hidden_pre, hidden, outs, widen_all, narrow_all = refs[:10]
+    base, grad, feats, mask, normed, hidden_pre, hidden, outs, widen, narrow = refs[:10]
     gain = feats[layer, 3:4]
     value_to, sums_to, low_all, wide_to, wide_came, slim_to, pre_sums = refs[10:17]
     refs = refs[17:]
     own, g_ss, g_rs, g_ls = refs[5:9]
     wide, wide_in, wide_ss, wide_rs, slim, slim_in, slim_ss, slim_rs, x_ss, x_rs = refs[9:19]
-    part, pre, widen, narrow, load_sems = refs[19:]
+    part, pre = refs[19:]
     p = Place(n)
-    loads = [
-        fetch(narrow_all.at[layer], narrow, load_sems.at[0]),
-        fetch(widen_all.at[layer], widen, load_sems.at[1]),
-    ]
     greet(p, line=True, over=True, sibling=True)
-    for load in loads:
-        load.wait()
-    io.need(5, 7)
-
-    def block(first, size):
+    io.need(9, 7, 5)
+
+    def inner(first, size):
         rows = pl.ds(first, size)
         values = hidden_pre[rows]
         act, square = gelu_parts(values)
@@ -1288,10 +1314,15 @@
         )
         found = (dot_t(outs[rows], narrow[...]) * slope).astype(BF16)
         pre[rows] = found
+
+    def outer(first, size):
+        rows = pl.ds(first, size)
         weight = widen[...].reshape(part.shape[1], widen.shape[2])
-        part[rows] = dot_t(found, weight).astype(BF16)
-
-    row_blocks(part.shape[0], block)
+        part[rows] = dot_t(pre[rows], weight).astype(BF16)
+
+    row_blocks(part.shape[0], inner)
+    io.need(8)
+    row_blocks(part.shape[0], outer)
     scatter = Scatter(p, part, *refs[:5])
     scatter.start()
     gather = Gather(p, own, low_all, g_ss, g_rs, g_ls)
@@ -1333,7 +1364,6 @@
 
 def resid_call(n, collective_id, width, layer, hide, *args):
     base, normed, hidden = args[0], args[4], args[6]
-    widen, narrow = args[8:]
     rows = base.shape[0]
     total_rows, full = normed.shape
     zn = n // 2
@@ -1363,12 +1393,9 @@
         + [
             pltpu.VMEM((total_rows, full), BF16),
             pltpu.VMEM(hidden.shape, BF16),
-            pltpu.VMEM(widen.shape[1:], BF16),
-            pltpu.VMEM(narrow.shape[1:], BF16),
-            DMA((2,)),
         ],
-        late=(4, 5, 6, 7),
-        plain=(8, 9),
+        late=(9, 7, 5, 8, 4, 6),
+        layers={8: layer, 9: layer},
         early=(3, 5),
         raw=(2, 4),
     )
@@ -1454,13 +1481,14 @@
 def finale_kernel(n, width, low, io, *refs):
     part, base, grad, feats, mask, normed, triple, att, resid = refs[:9]
     slims, slim_cames, qkv_far, out_far, vecs = refs[9:11], refs[11:13], refs[13], refs[14], refs[15:22]
-    layer_outs, upper_d_in, refs = refs[22:24], refs[24], refs[25:]
-    value_to, slim_to, qkv_to, out_to, vec_to, streams_to = refs[:6]
-    refs = refs[6:]
+    layer_outs, upper_d_in, wides, refs = refs[22:24], refs[24], refs[25:29], refs[29:]
+    value_to, slim_to, qkv_to, out_to, vec_to, streams_to, wide_to = refs[:7]
+    refs = refs[7:]
     qkv, qkv_fold_in, qkv_ss, qkv_rs, out, out_fold_in, out_ss, out_rs = refs[5:13]
     qkv_own, qkv_in, qkv_sum, out_own, out_in, out_sum = refs[13:19]
     slim_sum, slim_pair, vec, vec_in, vec_sum, vec_sib, streams = refs[19:26]
-    a_ss, a_rs, x_ss, x_rs, v_ss, v_rs, r_ss, r_rs, ls = refs[26:]
+    a_ss, a_rs, x_ss, x_rs, v_ss, v_rs, r_ss, r_rs, ls = refs[26:35]
+    wide_sum, wide_pair, w_ss, w_rs = refs[35:]
     p = Place(n)
     s, c, h, z, zn = p.s, p.c, p.h, p.z, p.zn
     share = width // n
@@ -1468,20 +1496,49 @@
     scatter = Scatter(p, part, *refs[:5])
     scatter.start()
 
-    slim_loads = [
+    first = slim_cames[0].shape[1]
+    rest = slim_pair.shape[2] - first
+    choices = (
         (
-            pltpu.make_async_copy(slims[layer], slim_pair.at[0], ls.at[1]),
-            pltpu.make_async_copy(slim_cames[layer], slim_pair.at[1], ls.at[4]),
-        )
-        for layer in range(2)
-    ]
-    for section, loads in enumerate(slim_loads):
+            (wides[0], wide_pair.at[0], 5),
+            (wides[1], wide_pair.at[1], 6),
+            (slims[0], slim_pair.at[0], 1),
+            (slim_cames[0], slim_pair.at[1, :, pl.ds(0, first)], 4),
+        ),
+        (
+            (wides[2], wide_pair.at[0], 5),
+            (wides[3], wide_pair.at[1], 6),
+            (slims[1], slim_pair.at[0], 1),
+            (slim_cames[1].at[:, pl.ds(0, first)], slim_pair.at[1, :, pl.ds(0, first)], 4),
+            (slim_cames[1].at[:, pl.ds(first, rest)], slim_pair.at[1, :, pl.ds(first, rest)], 7),
+        ),
+    )
+    for section, chosen in enumerate(choices):
 
         @pl.when(s == section)
         def _():
-            for load in loads:
-                load.start()
-
+            for src, dst, item in chosen:
+                pltpu.make_async_copy(src, dst, ls.at[item]).start()
+
+    def chosen_wait(item):
+        src, dst, sem = choices[0][item]
+        pltpu.make_async_copy(src, dst, ls.at[sem]).wait()
+
+    slim_cross = remote(
+        slims[0].at[:, pl.ds(first, rest)],
+        slim_pair.at[1, :, pl.ds(first, rest)],
+        x_ss.at[zn + 2],
+        x_rs.at[zn + 2],
+        p.over,
+    )
+    wide_back = Home(p, wide_sum, wide_to, w_ss, w_rs, ls.at[8])
+    chosen_wait(0)
+    chosen_wait(1)
+    for k in list(range(1, zn)) + [0]:
+        far = p.flip(k)
+        total = wide_pair[0, far].astype(F32) + wide_pair[1, far].astype(F32)
+        wide_sum[far] = total.astype(BF16)
+        wide_back.start(k)
     back = Home(p, qkv_sum, qkv_to, a_ss, a_rs, ls.at[0])
 
     def x_block(k, src=qkv_far):
@@ -1592,8 +1649,24 @@
         back.start(k)
     out_cross().wait_recv()
     add_home(p, out_sum, 0, out_own, out_in, out_far, out_in)
-    for load in slim_loads[0]:
-        load.wait()
+    for k in range(zn):
+        x_block(k).wait_send()
+    chosen_wait(2)
+    chosen_wait(3)
+
+    @pl.when(s == 1)
+    def _():
+        slim_cross.start()
+        src, dst, sem = choices[1][4]
+        pltpu.make_async_copy(src, dst, ls.at[sem]).wait()
+
+    for step in wide_back.steps():
+        step()
+
+    @pl.when(s == 0)
+    def _():
+        slim_cross.wait_recv()
+
     slim_sum[0] = (slim_pair[0, 0].astype(F32) + slim_pair[1, 0].astype(F32)).astype(BF16)
 
     def row_copies(w, src, dst):
@@ -1620,14 +1693,18 @@
     vec_to[...] = total + vec_sib[...]
     vec_share.wait_send()
     back.finish()
+    wide_back.finish()
+
+    @pl.when(s == 1)
+    def _():
+        slim_cross.wait_send()
+
     for w in range(2):
         copies[2 * w].wait()
         copies[2 * w + 1].wait_recv()
         copies[2 * w + 1].wait_send()
     for a, b in others(n):
         vec_copy(a, b).wait_send()
-    for k in range(zn):
-        x_block(k).wait_send()
     out_cross().wait_send()
     stream_cross.wait_recv()
     stream_cross.wait_send()
@@ -1637,7 +1714,7 @@
 
 def finale_call(n, collective_id, width, low, *args):
     part, triple, att = args[0], args[6], args[7]
-    slim, lanes = args[9].shape, args[19].shape[1]
+    slim, lanes, wide = args[9].shape, args[19].shape[1], args[25].shape
     total_rows, full = part.shape
     rows = total_rows // n
     zn = n // 2
@@ -1655,6 +1732,7 @@
             jax.ShapeDtypeStruct((2 * out[1], full), BF16),
             jax.ShapeDtypeStruct((8, lanes), F32),
             jax.ShapeDtypeStruct((2, rows, full), BF16),
+            jax.ShapeDtypeStruct((n,) + wide[1:], BF16),
         ],
         scatter_scratch(n, rows, full)
         + fold_scratch((full, triple.shape[1]), qkv)
@@ -1671,18 +1749,22 @@
             pltpu.VMEM((2, rows, full), BF16),
             DMA((2, zn)),
             DMA((2, zn)),
-            DMA((zn + 2,)),
-            DMA((zn + 2,)),
+            DMA((zn + 3,)),
+            DMA((zn + 3,)),
             DMA((2, n)),
             DMA((2, n)),
             DMA((3,)),
             DMA((3,)),
-            DMA((5,)),
+            DMA((9,)),
+            pltpu.VMEM(wide, BF16),
+            pltpu.VMEM((2,) + wide, BF16),
+            DMA((2, zn)),
+            DMA((2, zn)),
         ],
         late=(5, 6, 7, 8, 13, 14, 22, 23, 24),
-        plain=(9, 10, 11, 12),
+        plain=(9, 10, 11, 12, 25, 26, 27, 28),
         early=(0,),
-        raw=(1, 2, 3, 5),
+        raw=(1, 2, 3, 5, 6),
     )
 
 
@@ -1839,12 +1921,12 @@
         part_ref, base_ref, feats = refs[:3]
         refs = refs[3:]
     if home:
-        wides, slim, refs = refs[:4], refs[4], refs[5:]
+        slim, refs = refs[0], refs[1:]
     triple_ref, part_to, refs = refs[0], refs[1], refs[2:]
     if last:
         value_ref, refs = refs[0], refs[1:]
     if home:
-        wide_to, slim_came, refs = refs[0], refs[1], refs[2:]
+        slim_came, refs = refs[0], refs[1:]
     dq_t, dkv_own, dkv_oth, came, kv_ss, kv_rs = refs[:6]
     grad_ref, out_weight, qkv_weight, load_sems = refs[6:10]
     out_load = fetch(out_all.at[layer], out_weight, load_sems.at[0])
@@ -1853,39 +1935,17 @@
     rows = own_ref.shape[0]
     sh = slots * HD
     scale = HD**-0.5
-    greet(p, line=last, sibling=True, spread=home, over=home)
+    greet(p, line=last, sibling=True, over=home)
     between = []
     if last:
         scatter = Scatter(p, part_ref, *refs[10:])
         scatter.start()
         between = scatter.steps()
     if home:
-        wide_sum, wide_pair, a_ss, a_rs, ls, x_ss, x_rs = refs[10:]
-        wide_loads = [
-            [
-                pltpu.make_async_copy(wides[2 * layer + i], wide_pair.at[i], ls.at[1 + i])
-                for i in range(2)
-            ]
-            for layer in range(2)
-        ]
-        for section, loads in enumerate(wide_loads):
-
-            @pl.when(p.s == section)
-            def _():
-                for load in loads:
-                    load.start()
-
-        cross = Cross(p, slim, slim_came, x_ss, x_rs, 1)
+        x_ss, x_rs = refs[10:]
+        rows_first = slim.at[:, pl.ds(0, slim_came.shape[1])]
+        cross = Cross(p, rows_first, slim_came, x_ss, x_rs, 1)
         cross.start()
-        back = Home(p, wide_sum, wide_to, a_ss, a_rs, ls.at[0])
-        for load in wide_loads[0]:
-            load.wait()
-        for k in list(range(1, p.zn)) + [0]:
-            far = p.flip(k)
-            total = wide_pair[0, far].astype(F32) + wide_pair[1, far].astype(F32)
-            wide_sum[far] = total.astype(BF16)
-            back.start(k)
-        between = back.steps()
     io.need(2)
     out_load.wait()
 
@@ -1958,11 +2018,12 @@
     if last:
         finish_last()
     if home:
-        for rest in between:
-            rest()
-        back.finish()
         cross.finish()
     swap.wait_send()
+
+
+def early_rows(rows):
+    return rows * 2 // 5 // 16 * 16
 
 
 def attend_back_call(n, collective_id, slots, layer, *args, last=(), home=()):
@@ -1987,13 +2048,9 @@
         shapes.append(jax.ShapeDtypeStruct(last[1].shape, F32))
         scratch += scatter_scratch(n, *last[1].shape)
     if home:
-        wide, slim = home[0].shape, home[4].shape
-        shapes += [
-            jax.ShapeDtypeStruct((n,) + wide[1:], BF16),
-            jax.ShapeDtypeStruct(slim, BF16),
-        ]
-        scratch += [pltpu.VMEM(wide, BF16), pltpu.VMEM((2,) + wide, BF16)]
-        scratch += [DMA((2, n // 2)), DMA((2, n // 2)), DMA((3,)), DMA, DMA]
+        slim = home[0].shape
+        shapes.append(jax.ShapeDtypeStruct((1, early_rows(slim[1]), full), BF16))
+        scratch += [DMA, DMA]
     return staged_call(
         functools.partial(attend_back_kernel, n, slots, step, layer, bool(last), bool(home)),
         "attend_back",
@@ -2002,9 +2059,9 @@
         shapes,
         scratch,
         late=(0, 1, 2, 3),
-        plain=(7, 8) + (tuple(range(9, 14)) if home else ()),
+        plain=(7, 8) + ((9,) if home else ()),
         early=(0, 1),
-        raw=(2, 3) if home else (),
+        raw=(2,) if home else (),
     )
 
 
@@ -2052,7 +2109,6 @@
     qpos = own_places[None, :]
 
     (
-        narrow_send,
         x,
         own_cot,
         out_grad,
@@ -2064,8 +2120,13 @@
         feats,
         qkv_bias,
         widen_biases,
-        *attended,
+        att,
+        att_low,
+        lse,
+        other,
         widen_all,
+        *middle,
+        narrow_all,
     ) = open_call(
         n,
         low,
@@ -2095,27 +2156,24 @@
     layer_outs = []
     for layer in range(2):
         if layer:
-            *attended, out_low_all, qkv = attend_call(
+            att, att_low, lse, other, part, out_low_all, qkv = attend_call(
                 n, 2, slots, 1, kpos, qpos, own_cot, out_all, normed, qkv_all, qkv_bias
             )
-        att, att_low, lse, other, part = attended
-        found = forward_call(
-            n,
-            3 + layer,
-            width,
-            part,
-            x,
-            feats,
-            mask,
-            layer=layer,
-            feed=(widen_all, narrow_all if layer else narrow_send, widen_biases),
-            carry=not layer,
-        )
-        residual, normed_two, hidden_pre, hidden_low, part = found[:5]
+            middle = forward_call(
+                n,
+                4,
+                width,
+                part,
+                x,
+                feats,
+                mask,
+                layer=1,
+                feed=(widen_all, narrow_all, widen_biases),
+            )
+        residual, normed_two, hidden_pre, hidden_low, part = middle
         stored.append((x, normed, qkv, other, att, att_low, lse, residual, normed_two))
         stored[-1] += (hidden_pre, hidden_low)
         if layer == 0:
-            narrow_all = found[5]
             x, normed = forward_call(n, 5, width, part, residual, feats, mask)
             layer_outs.append(x)
         else:
@@ -2157,7 +2215,7 @@
             out_all,
             qkv_all,
             last=last if layer else (),
-            home=() if layer else (wide, wide_came) + found[1][:2] + (slim,),
+            home=() if layer else (slim,),
         )
         triple, part = back[:2]
         local = (part, x, resid_grad, feats, mask, normed, triple, att_low, resid_low_all)
@@ -2169,8 +2227,7 @@
             )
             out_grad = upper_d_in
     lower, upper = found[0], found[1]
-    widen_back, slim_back = back[2:]
-    d_in, narrow_back, qkv_back, out_back, vec, came = finale_call(
+    d_in, narrow_back, qkv_back, out_back, vec, came, widen_back = finale_call(
         n,
         12,
         width,
@@ -2178,7 +2235,7 @@
         *local,
         lower[2],
         upper[2],
-        slim_back,
+        back[2],
         slim_came,
         qkv_grad,
         out_rows,
@@ -2191,6 +2248,8 @@
         out_sums,
         *layer_outs,
         upper_d_in,
+        *lower[:2],
+        *upper[:2],
     )
     settled = settle_call(
         low,

time: 581 us -> 554 us (0.954)
  Pallas kernels: 569 us -> 541 us
    pallas_call x11 -> x10, Pallas kernels: 557 us -> 530 us  [staged_call(): pl.pallas_call(run, out_shape=shapes, in_specs=[ANY_SPEC if i in late + t...]
where the time goes in v4:
time: 554 us; the launch traced here: 545 us
  Pallas kernels  541 us (98%)
    pallas_call x10, Pallas kernels, staged_call(): pl.pallas_call(run, out_shape=shapes, in_specs=[ANY_SPEC if i in late + t...  530 us
    pallas_call x1, Pallas kernels, settle_call(): pl.pallas_call(functools.partial(settle_kernel, low, sizes), out_shape=[j...  11.4 us

profile of v4, /device:TPU:0, one launch (start us, length us, event | category | flops | bytes accessed | tf_op | source)
XLA Modules:
  0.0 545.3 jit_solution(8670503886654107107)
XLA Ops:
  0.7 0.7 broadcast_multiply_fusion
  1.3 0.1 mul.15
  1.4 0.1 iota_add_fusion
  1.5 0.1 select_n.32
  1.6 0.7 select_n.33.refs_16_.refs_1_.refs_6_
  2.2 0.1 select_n.30
  2.3 1.0 copy.32.refs_15_.refs_0_.refs_5_
  3.4 134.5 %open.1 = (f32[64,1664]{1,0:T(8,128)}, bf16[64,1664]{1,0:T(8,128)(2,1)}, f32[64,1664]{1,0:T(8,128)}, f32[1,1664]{1,0:T(1,128)}, bf16[512,1664]{1,0:T(8,128)(2,1)...) custom-call(bf16[2,64,1600]{2,1,0:T(8,128)(2,1)} %refs_0_.1, ...), custom_call_target="tpu_custom_call" | custom-call | tf_op jit(solution)/shard_map/open/pallas_call | solution.py:717
  137.9 47.6 %forward_rows.2 = (f32[64,1664]{1,0:T(8,128)}, bf16[512,1664]{1,0:T(8,128)(2,1)}) custom-call(bf16[512,1664]{1,0:T(8,128)(2,1)} %get-tuple-element.103.refs_0_, f32[64,1664]{1,0:T(8,128)} %get-tuple-element.100.refs_1_.refs_0_, f32[2,16,1664]{2,1,0:T(8,128)} %get-tuple-element.104.refs_2_.refs_11_.refs_3_, f32[1,1664]{1,0:T(1,128)} %constant.12.clone.refs_14_.refs_3_.refs_4_), custom_call_target="tpu_custom_call" | custom-call | tf_op jit(solution)/shard_map/forward_rows/pallas_call | solution.py:717
  185.5 24.3 %attend.1 = (f32[256,512]{1,0:T(8,128)}, bf16[512,256]{1,0:T(8,128)(2,1)}, f32[4,512]{1,0:T(4,128)}, bf16[512,512]{1,0:T(8,128)(2,1)}, bf16[512,1664]{1,0:T(8,12...) custom-call(s32[1024,1]{1,0:T(8,128)} %copy.32.refs_15_.refs_0_.refs_5_, ...), custom_call_target="tpu_custom_call" | custom-call | tf_op jit(solution)/shard_map/attend/pallas_call | solution.py:717
  209.8 47.9 %forward_rows.3 = (f32[64,1664]{1,0:T(8,128)}, bf16[512,1664]{1,0:T(8,128)(2,1)}, f32[512,896]{1,0:T(8,128)}, bf16[512,896]{1,0:T(8,128)(2,1)}, bf16[512,1664]{1,0:T(8,128)(2,1)}) custom-call(bf16[512,1664]{1,0:T(8,128)(2,1)} %get-tuple-element.110.refs_0_, f32[64,1664]{1,0:T(8,128)} %get-tuple-element.111.refs_1_.refs_22_.refs_6_, ...), custom_call_target="tpu_custom_call" | custom-call | tf_op jit(solution)/shard_map/forward_rows/pallas_call | solution.py:717
  257.7 50.6 %back_resid.2 = (f32[64,1664]{1,0:T(8,128)}, f32[3,1664]{1,0:T(4,128)}, bf16[512,1664]{1,0:T(8,128)(2,1)}, bf16[4,208,896]{2,1,0:T(8,128)(2,1)}, bf16[4,208,896]...) custom-call(f32[64,1664]{1,0:T(8,128)} %get-tuple-element.115.refs_0_.refs_10_, ...), custom_call_target="tpu_custom_call" | custom-call | tf_op jit(solution)/shard_map/back_resid/pallas_call | solution.py:717
  308.3 25.7 %attend_back.2 = (bf16[512,768]{1,0:T(8,128)(2,1)}, bf16[512,1664]{1,0:T(8,128)(2,1)}, f32[64,1664]{1,0:T(8,128)}) custom-call(bf16[512,768]{1,0:T(8,128)(2,1)} %get-tuple-element.108.refs_0_, bf16[512,512]{1,0:T(8,128)(2,1)} %get-tuple-element.109.refs_1_, bf16[512,1664]{1,0:T(8,128)(2,1)} %get-tuple-element.121.refs_2_.refs_8_, ...), custom_call_target="tpu_custom_call" | custom-call | tf_op jit(solution)/shard_map/attend_back/pallas_call | solution.py:717
  334.1 43.6 %back_input.1 = (f32[64,1664]{1,0:T(8,128)}, f32[3,1664]{1,0:T(4,128)}, bf16[512,1664]{1,0:T(8,128)(2,1)}, bf16[4,208,768]{2,1,0:T(8,128)(2,1)}, bf16[1,128,1664...) custom-call(bf16[512,1664]{1,0:T(8,128)(2,1)} %get-tuple-element.125.refs_0_, ...), custom_call_target="tpu_custom_call" | custom-call | tf_op jit(solution)/shard_map/back_input/pallas_call | solution.py:717
  377.7 51.6 %back_resid.3 = (f32[64,1664]{1,0:T(8,128)}, f32[3,1664]{1,0:T(4,128)}, bf16[512,1664]{1,0:T(8,128)(2,1)}, bf16[4,208,896]{2,1,0:T(8,128)(2,1)}, bf16[4,208,896]...) custom-call(f32[64,1664]{1,0:T(8,128)} %get-tuple-element.100.refs_1_.refs_0_, ...), custom_call_target="tpu_custom_call" | custom-call | tf_op jit(solution)/shard_map/back_resid/pallas_call | solution.py:717
  429.3 15.1 %attend_back.3 = (bf16[512,768]{1,0:T(8,128)(2,1)}, bf16[512,1664]{1,0:T(8,128)(2,1)}, bf16[1,160,1664]{2,1,0:T(8,128)(2,1)}) custom-call(bf16[512,768]{1,0:T(8,128)(2,1)} %get-tuple-element.98.refs_0_, bf16[512,512]{1,0:T(8,128)(2,1)} %get-tuple-element.99.refs_1_, bf16[512,1664]{1,0:T(8,128)(2,1)} %get-tuple-element.135.refs_2_.refs_8_, ...), custom_call_target="tpu_custom_call" | custom-call | tf_op jit(solution)/shard_map/attend_back/pallas_call | solution.py:717
  444.4 89.1 %finale.1 = (f32[64,1664]{1,0:T(8,128)}, bf16[800,1664]{1,0:T(8,128)(2,1)}, bf16[8,208,768]{2,1,0:T(8,128)(2,1)}, bf16[256,1664]{1,0:T(8,128)(2,1)}, f32[8,896]{...) custom-call(bf16[512,1664]{1,0:T(8,128)(2,1)} %get-tuple-element.139.refs_0_, ...), custom_call_target="tpu_custom_call" | custom-call | tf_op jit(solution)/shard_map/finale/pallas_call | solution.py:717
  533.5 11.4 %settle.1 = (f32[200,4800]{1,0:T(8,128)}, f32[200,6400]{1,0:T(8,128)}, f32[200,1600]{1,0:T(8,128)}, f32[800,1600]{1,0:T(8,128)}, f32[2,64,1600]{2,1,0:T(8,128)},...) custom-call(bf16[8,208,768]{2,1,0:T(8,128)(2,1)} %get-tuple-element., ...), custom_call_target="tpu_custom_call" | custom-call | tf_op jit(solution)/shard_map/settle/pallas_call | solution.py:1163
  (3 shorter events, 0.0 us)

commit v5 on v4

--- a/solution.py
+++ b/solution.py
@@ -669,6 +669,8 @@
 
 
 class Staging:
+    greeted, extra = False, {}
+
     def __init__(self):
         self.loads, self.stores, self.running = {}, {}, []
 
@@ -725,6 +727,128 @@
     )(*args)
 
 
+class Mapped:
+    def __init__(self, io, loads, stores, greeted=True, extra={}):
+        self.io, self.loads, self.stores = io, loads, stores
+        self.greeted, self.extra = greeted, extra
+
+    def need(self, *items):
+        for item in items:
+            if self.loads.get(item) in self.io.loads:
+                self.io.need(self.loads[item])
+
+    def done(self, *items):
+        for item in items:
+            if self.stores.get(item) in self.io.stores:
+                self.io.done(self.stores[item])
+
+
+class Result:
+    def __init__(self, step, index):
+        self.step, self.index = step, index
+        self.shape, self.dtype = step.shapes[index].shape, step.shapes[index].dtype
+
+
+class Step:
+    def __init__(self, body, name, collective_id, args, shapes, scratch, greets, **staging):
+        self.body, self.name, self.collective_id = body, name, collective_id
+        self.args, self.shapes, self.scratch, self.greets = tuple(args), shapes, scratch, greets
+        self.late = tuple(staging.get("late", ()))
+        self.plain = tuple(staging.get("plain", ()))
+        self.early = tuple(staging.get("early", ()))
+        self.raw = tuple(staging.get("raw", ()))
+        self.layers = staging.get("layers", {})
+
+
+def run_steps(steps):
+    args, arg_of, out_of, first_out = [], {}, {}, []
+    shapes, scratch, early, raw = [], [], [], []
+    linked = {
+        (id(arg.step), arg.index) for step in steps for arg in step.args if isinstance(arg, Result)
+    }
+    for k, step in enumerate(steps):
+        for i, arg in enumerate(step.args):
+            if isinstance(arg, Result):
+                continue
+            spots = [x for x, known in enumerate(args) if known is arg]
+            if not spots:
+                args.append(arg)
+                spots = [len(args) - 1]
+            arg_of[k, i] = spots[0]
+        first_out.append(len(shapes))
+        for o, shape in enumerate(step.shapes):
+            out_of[k, o] = len(shapes)
+            keep = (id(step), o) in linked
+            if o in step.early or (o in step.raw and keep):
+                early.append(len(shapes))
+            elif o in step.raw:
+                raw.append(len(shapes))
+            shapes.append(shape)
+        scratch += step.scratch
+    direct = {
+        arg_of[k, i]
+        for k, step in enumerate(steps)
+        for i in range(len(step.args))
+        if (k, i) in arg_of and i not in step.late and i not in step.plain
+    }
+    late, layers = [], {}
+    for k, step in enumerate(steps):
+        for i in step.late:
+            spot = arg_of.get((k, i))
+            if spot is not None and spot not in direct and spot not in late:
+                late.append(spot)
+                if i in step.layers:
+                    layers[spot] = step.layers[i]
+    plain = [x for x in range(len(args)) if x not in direct and x not in late]
+    extra = {}
+    for step in steps:
+        extra.update(step.greets)
+
+    def body(io, *refs):
+        ins, outs = refs[: len(args)], refs[len(args) : len(args) + len(shapes)]
+        rest = refs[len(args) + len(shapes) :]
+        for k, step in enumerate(steps):
+            mine = []
+            for i, arg in enumerate(step.args):
+                if isinstance(arg, Result):
+                    mine.append(outs[out_of[steps.index(arg.step), arg.index]])
+                else:
+                    mine.append(ins[arg_of[k, i]])
+            loads = {i: arg_of[k, i] for i in range(len(step.args)) if (k, i) in arg_of}
+            stores = {o: out_of[k, o] for o in range(len(step.shapes))}
+            own = outs[first_out[k] : first_out[k] + len(step.shapes)]
+            count = len(step.scratch)
+            part = Mapped(io, loads, stores, k > 0, extra)
+            step.body(part, *mine, *own, *rest[:count])
+            part.done(*stores)
+            rest = rest[count:]
+
+    found = staged_call(
+        body,
+        "_".join(step.name for step in steps),
+        steps[0].collective_id,
+        args,
+        shapes,
+        scratch,
+        late=late,
+        plain=plain,
+        early=early,
+        raw=raw,
+        layers=layers,
+    )
+    return [
+        found[first : first + len(step.shapes)] for first, step in zip(first_out, steps)
+    ]
+
+
+def follow(merge, first, make_second):
+    if merge:
+        results = [Result(first, i) for i in range(len(first.shapes))]
+        return run_steps([first, make_second(results)])
+    (found,) = run_steps([first])
+    return found, run_steps([make_second(found)])[0]
+
+
 def row_blocks(rows, step):
     size = min(rows, 256)
     count = rows // size
@@ -738,6 +862,12 @@
             return carry
 
         lax.fori_loop(0, count, body, 0)
+
+
+def enter(io, p, **greets):
+    if not io.greeted:
+        greets.update(io.extra)
+        greet(p, **greets)
 
 
 def gelu_parts(values):
@@ -1198,7 +1328,7 @@
     refs = refs[4:]
     if middle:
         bias, gain, shift = (feats[layer, row : row + 1] for row in (2, 3, 4))
-        widen_all, narrow_all, widen_bias, refs = refs[0], refs[1], refs[2], refs[3:]
+        widen, narrow, widen_bias, refs = refs[0], refs[1], refs[2], refs[3:]
     else:
         bias, gain, shift = feats[0, 5:6], feats[1, 0:1], feats[1, 1:2]
     value_to, low_all, refs = refs[0], refs[1], refs[2:]
@@ -1206,14 +1336,9 @@
         pre_to, hidden_to, part_to, refs = refs[0], refs[1], refs[2], refs[3:]
     own, g_ss, g_rs, g_ls = refs[5:9]
     p = Place(n)
-    greet(p, line=True)
+    enter(io, p, line=True)
     scatter = Scatter(p, part, *refs[:5])
     scatter.start()
-    loads = []
-    if middle:
-        widen, narrow, load_sems = refs[9:]
-        loads.append(fetch(widen_all.at[layer], widen, load_sems.at[0]))
-        loads.append(fetch(narrow_all.at[layer], narrow, load_sems.at[1]))
     gather = Gather(p, own, low_all, g_ss, g_rs, g_ls)
     hr = own.shape[0] // HALVES
 
@@ -1225,10 +1350,9 @@
 
     by_halves(scatter, gather, rows_step, [])
     gather.finish()
-    for load in loads:
-        load.wait()
     if middle:
         io.done(1)
+        io.need(4, 5)
         feed_forward(low_all, widen, narrow, widen_bias[layer], pre_to, hidden_to, part_to)
     scatter.finish()
 
@@ -1250,7 +1374,7 @@
     return [DMA((4, zn, HALVES)), DMA((4, zn, HALVES)), DMA((HALVES,))]
 
 
-def forward_call(n, collective_id, width, part, *local, layer=None, feed=()):
+def forward_step(n, collective_id, width, part, *local, layer=None, feed=()):
     total_rows, full = part.shape
     rows = total_rows // n
     shapes = [
@@ -1268,15 +1392,16 @@
             jax.ShapeDtypeStruct((total_rows, hide), BF16),
             jax.ShapeDtypeStruct((total_rows, full), BF16),
         ]
-        scratch += [pltpu.VMEM(widen.shape[1:], BF16), pltpu.VMEM((hide, full), BF16), DMA((2,))]
-    return staged_call(
+    return Step(
         functools.partial(forward_kernel, n, width, layer),
         "forward_rows",
         collective_id,
         (part, *local, *feed),
         shapes,
         scratch,
-        plain=(4, 5) if middle else (),
+        dict(line=True),
+        late=(4, 5) if middle else (),
+        layers={4: layer, 5: layer} if middle else {},
         early=(1, 2, 3, 4) if middle else (),
         raw=() if middle else (1,),
     )
@@ -1302,7 +1427,7 @@
     wide, wide_in, wide_ss, wide_rs, slim, slim_in, slim_ss, slim_rs, x_ss, x_rs = refs[9:19]
     part, pre = refs[19:]
     p = Place(n)
-    greet(p, line=True, over=True, sibling=True)
+    enter(io, p, line=True, over=True, sibling=True)
     io.need(9, 7, 5)
 
     def inner(first, size):
@@ -1362,7 +1487,7 @@
         job.finish()
 
 
-def resid_call(n, collective_id, width, layer, hide, *args):
+def resid_step(n, collective_id, width, layer, hide, *args):
     base, normed, hidden = args[0], args[4], args[6]
     rows = base.shape[0]
     total_rows, full = normed.shape
@@ -1370,7 +1495,7 @@
     wide = (zn, full // n, hidden.shape[1])
     half = -(-hide // 32) * 16
     slim = (1, half, full)
-    return staged_call(
+    return Step(
         functools.partial(resid_kernel, n, width, layer),
         "back_resid",
         collective_id,
@@ -1394,6 +1519,7 @@
             pltpu.VMEM((total_rows, full), BF16),
             pltpu.VMEM(hidden.shape, BF16),
         ],
+        dict(line=True, over=True, sibling=True),
         late=(9, 7, 5, 8, 4, 6),
         layers={8: layer, 9: layer},
         early=(3, 5),
@@ -1409,7 +1535,7 @@
     own, g_ss, g_rs, g_ls = refs[5:9]
     qkv, qkv_in, qkv_ss, qkv_rs, out, out_in, out_ss, out_rs, x_ss, x_rs = refs[9:]
     p = Place(n)
-    greet(p, line=True, over=True, sibling=True)
+    enter(io, p, line=True, over=True, sibling=True)
     scatter = Scatter(p, part, *refs[:5])
     scatter.start()
     cross = Cross(p, slim, slim_came, x_ss, x_rs, source)
@@ -1444,14 +1570,14 @@
         job.finish()
 
 
-def input_call(n, collective_id, width, source, low, part, base, grad, feats, mask, *operands):
+def input_step(n, collective_id, width, source, low, part, base, grad, feats, mask, *operands):
     normed, triple, att, resid, slim = operands
     total_rows, full = part.shape
     rows = total_rows // n
     zn = n // 2
     qkv = (zn, full // n, triple.shape[1])
     out = (1, att.shape[1] // 2, full)
-    return staged_call(
+    return Step(
         functools.partial(input_kernel, n, width, source, low),
         "back_input",
         collective_id,
@@ -1471,6 +1597,7 @@
         + fold_scratch((full, triple.shape[1]), qkv)
         + fold_scratch((att.shape[1], full), out)
         + [DMA, DMA],
+        dict(line=True, over=True, sibling=True),
         late=(5, 6, 7, 8),
         plain=(9,),
         early=(3, 4),
@@ -1478,10 +1605,10 @@
     )
 
 
-def finale_kernel(n, width, low, io, *refs):
+def finale_kernel(n, width, low, between, io, *refs):
     part, base, grad, feats, mask, normed, triple, att, resid = refs[:9]
-    slims, slim_cames, qkv_far, out_far, vecs = refs[9:11], refs[11:13], refs[13], refs[14], refs[15:22]
-    layer_outs, upper_d_in, wides, refs = refs[22:24], refs[24], refs[25:29], refs[29:]
+    slims, slim_came, qkv_far, out_far, vecs = refs[9:11], refs[11], refs[12], refs[13], refs[14:21]
+    layer_outs, upper_d_in, wides, refs = refs[21:23], refs[23], refs[24:28], refs[28:]
     value_to, slim_to, qkv_to, out_to, vec_to, streams_to, wide_to = refs[:7]
     refs = refs[7:]
     qkv, qkv_fold_in, qkv_ss, qkv_rs, out, out_fold_in, out_ss, out_rs = refs[5:13]
@@ -1493,24 +1620,17 @@
     s, c, h, z, zn = p.s, p.c, p.h, p.z, p.zn
     share = width // n
     greet_all(p)
-    scatter = Scatter(p, part, *refs[:5])
-    scatter.start()
-
-    first = slim_cames[0].shape[1]
-    rest = slim_pair.shape[2] - first
     choices = (
         (
             (wides[0], wide_pair.at[0], 5),
             (wides[1], wide_pair.at[1], 6),
             (slims[0], slim_pair.at[0], 1),
-            (slim_cames[0], slim_pair.at[1, :, pl.ds(0, first)], 4),
         ),
         (
             (wides[2], wide_pair.at[0], 5),
             (wides[3], wide_pair.at[1], 6),
             (slims[1], slim_pair.at[0], 1),
-            (slim_cames[1].at[:, pl.ds(0, first)], slim_pair.at[1, :, pl.ds(0, first)], 4),
-            (slim_cames[1].at[:, pl.ds(first, rest)], slim_pair.at[1, :, pl.ds(first, rest)], 7),
+            (slim_came, slim_pair.at[1], 4),
         ),
     )
     for section, chosen in enumerate(choices):
@@ -1521,16 +1641,11 @@
                 pltpu.make_async_copy(src, dst, ls.at[item]).start()
 
     def chosen_wait(item):
-        src, dst, sem = choices[0][item]
+        src, dst, sem = choices[1][item]
         pltpu.make_async_copy(src, dst, ls.at[sem]).wait()
 
-    slim_cross = remote(
-        slims[0].at[:, pl.ds(first, rest)],
-        slim_pair.at[1, :, pl.ds(first, rest)],
-        x_ss.at[zn + 2],
-        x_rs.at[zn + 2],
-        p.over,
-    )
+    slim_cross = Cross(p, slims[0], slim_pair.at[1], x_ss.at[zn + 2], x_rs.at[zn + 2], 1)
+    slim_cross.start()
     wide_back = Home(p, wide_sum, wide_to, w_ss, w_rs, ls.at[8])
     chosen_wait(0)
     chosen_wait(1)
@@ -1539,6 +1654,10 @@
         total = wide_pair[0, far].astype(F32) + wide_pair[1, far].astype(F32)
         wide_sum[far] = total.astype(BF16)
         wide_back.start(k)
+    if between is not None:
+        between()
+    scatter = Scatter(p, part, *refs[:5])
+    scatter.start()
     back = Home(p, qkv_sum, qkv_to, a_ss, a_rs, ls.at[0])
 
     def x_block(k, src=qkv_far):
@@ -1570,7 +1689,7 @@
     qkv_fold = Fold(p, qkv, qkv_fold_in, qkv_own, qkv_ss, qkv_rs)
     out_fold = Fold(p, out, out_fold_in, out_own, out_ss, out_rs)
 
-    io.need(13, 14)
+    io.need(12, 13)
     start_far()
     io.need(5, 6)
     for step in product(normed, triple, qkv):
@@ -1592,7 +1711,7 @@
     for rest in work:
         rest()
 
-    io.need(22, 23, 24)
+    io.need(21, 22, 23)
     streams[0] = jnp.where(s == 0, layer_outs[1][...], layer_outs[0][...]).astype(BF16)
     streams[1] = jnp.where(s == 0, upper_d_in[...], value_to[...]).astype(BF16)
     io.done(0)
@@ -1652,21 +1771,14 @@
     for k in range(zn):
         x_block(k).wait_send()
     chosen_wait(2)
-    chosen_wait(3)
 
     @pl.when(s == 1)
     def _():
-        slim_cross.start()
-        src, dst, sem = choices[1][4]
-        pltpu.make_async_copy(src, dst, ls.at[sem]).wait()
+        chosen_wait(3)
 
     for step in wide_back.steps():
         step()
-
-    @pl.when(s == 0)
-    def _():
-        slim_cross.wait_recv()
-
+    slim_cross.finish()
     slim_sum[0] = (slim_pair[0, 0].astype(F32) + slim_pair[1, 0].astype(F32)).astype(BF16)
 
     def row_copies(w, src, dst):
@@ -1694,11 +1806,6 @@
     vec_share.wait_send()
     back.finish()
     wide_back.finish()
-
-    @pl.when(s == 1)
-    def _():
-        slim_cross.wait_send()
-
     for w in range(2):
         copies[2 * w].wait()
         copies[2 * w + 1].wait_recv()
@@ -1712,20 +1819,15 @@
         job.finish()
 
 
-def finale_call(n, collective_id, width, low, *args):
+def finale_parts(n, *args):
     part, triple, att = args[0], args[6], args[7]
-    slim, lanes, wide = args[9].shape, args[19].shape[1], args[25].shape
+    slim, lanes, wide = args[9].shape, args[18].shape[1], args[24].shape
     total_rows, full = part.shape
     rows = total_rows // n
     zn = n // 2
     qkv = (zn, full // n, triple.shape[1])
     out = (1, att.shape[1] // 2, full)
-    return staged_call(
-        functools.partial(finale_kernel, n, width, low),
-        "finale",
-        collective_id,
-        args,
-        [
+    shapes = [
             jax.ShapeDtypeStruct((rows, full), F32),
             jax.ShapeDtypeStruct((2 * slim[1], full), BF16),
             jax.ShapeDtypeStruct((n,) + qkv[1:], BF16),
@@ -1733,7 +1835,8 @@
             jax.ShapeDtypeStruct((8, lanes), F32),
             jax.ShapeDtypeStruct((2, rows, full), BF16),
             jax.ShapeDtypeStruct((n,) + wide[1:], BF16),
-        ],
+        ]
+    scratch = (
         scatter_scratch(n, rows, full)
         + fold_scratch((full, triple.shape[1]), qkv)
         + fold_scratch((att.shape[1], full), out)
@@ -1760,9 +1863,22 @@
             pltpu.VMEM((2,) + wide, BF16),
             DMA((2, zn)),
             DMA((2, zn)),
-        ],
-        late=(5, 6, 7, 8, 13, 14, 22, 23, 24),
-        plain=(9, 10, 11, 12, 25, 26, 27, 28),
+        ]
+    )
+    return shapes, scratch
+
+
+def finale_call(n, collective_id, width, low, *args):
+    shapes, scratch = finale_parts(n, *args)
+    return staged_call(
+        functools.partial(finale_kernel, n, width, low, None),
+        "finale",
+        collective_id,
+        args,
+        shapes,
+        scratch,
+        late=(5, 6, 7, 8, 12, 13, 21, 22, 23),
+        plain=(9, 10, 11, 24, 25, 26, 27),
         early=(0,),
         raw=(1, 2, 3, 5, 6),
     )
@@ -1847,7 +1963,7 @@
     p = Place(n)
     rows = own_ref.shape[0]
     sh = slots * HD
-    greet(p, line=True, sibling=True)
+    enter(io, p, line=True, sibling=True)
     job = Gather(p, carried, carried_to, *refs[19:])
     job.start()
     qkv_load.wait()
@@ -1881,11 +1997,11 @@
     job.finish()
 
 
-def attend_call(n, collective_id, slots, layer, kpos, qpos, carried, out_all, *source):
+def attend_step(n, collective_id, slots, layer, kpos, qpos, carried, out_all, *source):
     rows = qpos.shape[1]
     sh = slots * HD
     full = out_all.shape[2]
-    return staged_call(
+    return Step(
         functools.partial(attend_kernel, n, slots, min(rows, 256), layer),
         "attend",
         collective_id,
@@ -1907,6 +2023,7 @@
             DMA((2,)),
         ]
         + gather_scratch(n),
+        dict(line=True, sibling=True),
         late=(4,),
         plain=(3, 5),
         early=(0, 1, 4, 6),
@@ -1914,19 +2031,15 @@
     )
 
 
-def attend_back_kernel(n, slots, step, layer, last, home, io, *refs):
+def attend_back_kernel(n, slots, step, layer, last, greeted, io, *refs):
     own_ref, oth_ref, resid, att_ref, lse_ref, kpos_ref, qpos_ref, out_all, qkv_all = refs[:9]
     refs = refs[9:]
     if last:
         part_ref, base_ref, feats = refs[:3]
         refs = refs[3:]
-    if home:
-        slim, refs = refs[0], refs[1:]
     triple_ref, part_to, refs = refs[0], refs[1], refs[2:]
     if last:
         value_ref, refs = refs[0], refs[1:]
-    if home:
-        slim_came, refs = refs[0], refs[1:]
     dq_t, dkv_own, dkv_oth, came, kv_ss, kv_rs = refs[:6]
     grad_ref, out_weight, qkv_weight, load_sems = refs[6:10]
     out_load = fetch(out_all.at[layer], out_weight, load_sems.at[0])
@@ -1935,17 +2048,13 @@
     rows = own_ref.shape[0]
     sh = slots * HD
     scale = HD**-0.5
-    greet(p, line=last, sibling=True, over=home)
+    if not greeted:
+        greet(p, line=last, sibling=True)
     between = []
     if last:
         scatter = Scatter(p, part_ref, *refs[10:])
         scatter.start()
         between = scatter.steps()
-    if home:
-        x_ss, x_rs = refs[10:]
-        rows_first = slim.at[:, pl.ds(0, slim_came.shape[1])]
-        cross = Cross(p, rows_first, slim_came, x_ss, x_rs, 1)
-        cross.start()
     io.need(2)
     out_load.wait()
 
@@ -2017,16 +2126,75 @@
     io.done(1)
     if last:
         finish_last()
-    if home:
-        cross.finish()
     swap.wait_send()
 
 
-def early_rows(rows):
-    return rows * 2 // 5 // 16 * 16
-
-
-def attend_back_call(n, collective_id, slots, layer, *args, last=(), home=()):
+def attend_back_scratch(rows, sh, full, qkv_all):
+    scratch = [pltpu.VMEM((sh, rows), F32)] + [pltpu.VMEM((rows, 2 * sh), F32)] * 3
+    scratch += [DMA, DMA]
+    return scratch + [
+        pltpu.VMEM((rows, sh), BF16),
+        pltpu.VMEM((sh, full), BF16),
+        pltpu.VMEM(qkv_all.shape[1:], BF16),
+        DMA((2,)),
+    ]
+
+
+def closing_kernel(n, width, low, slots, step, io, *refs):
+    back, rest, refs = refs[:9], refs[9 : 9 + 25], refs[34:]
+    outs, refs = refs[:7], refs[7:]
+    back_scratch, triple, part, refs = refs[:10], refs[10], refs[11], refs[12:]
+
+    def between():
+        mapped = Mapped(io, {i: i for i in range(9)}, {})
+        attend_back_kernel(
+            n, slots, step, 0, False, True, mapped, *back, triple, part, *back_scratch
+        )
+
+    numbers = [i for i in range(28) if i not in (0, 6, 8)]
+    places = {i: 9 + x for x, i in enumerate(numbers)}
+    places[8] = 2
+    operands = dict(zip(numbers, rest))
+    operands.update({0: part, 6: triple, 8: back[2]})
+    finale_kernel(
+        n,
+        width,
+        low,
+        between,
+        Mapped(io, places, {i: i for i in range(7)}),
+        *(operands[i] for i in range(28)),
+        *outs,
+        *refs,
+    )
+
+
+def closing_call(n, collective_id, width, low, slots, back, args):
+    qkv, out_all, qkv_all = back[0], back[7], back[8]
+    rows = qkv.shape[0]
+    full = out_all.shape[2]
+    triple = jax.ShapeDtypeStruct((rows, qkv.shape[1]), BF16)
+    part = jax.ShapeDtypeStruct((rows, full), BF16)
+    args = [part] + list(args[:5]) + [triple] + list(args[5:6]) + [back[2]] + list(args[6:])
+    shapes, scratch = finale_parts(n, *args)
+    numbers = [i for i in range(28) if i not in (0, 6, 8)]
+    places = {i: 9 + x for x, i in enumerate(numbers)}
+    return staged_call(
+        functools.partial(closing_kernel, n, width, low, slots, min(rows, 256)),
+        "closing",
+        collective_id,
+        tuple(back) + tuple(args[i] for i in numbers),
+        shapes,
+        attend_back_scratch(rows, slots * HD, full, qkv_all)
+        + [pltpu.VMEM(triple.shape, BF16), pltpu.VMEM(part.shape, BF16)]
+        + scratch,
+        late=(2, 0, 1, 3) + tuple(places[i] for i in (5, 7, 12, 13, 21, 22, 23)),
+        plain=(7, 8) + tuple(places[i] for i in (9, 10, 11, 24, 25, 26, 27)),
+        early=(0,),
+        raw=(1, 2, 3, 5, 6),
+    )
+
+
+def attend_back_call(n, collective_id, slots, layer, *args, last=()):
     qkv, out_all, qkv_all = args[0], args[7], args[8]
     rows = qkv.shape[0]
     sh = slots * HD
@@ -2036,32 +2204,20 @@
         jax.ShapeDtypeStruct((rows, 3 * sh), BF16),
         jax.ShapeDtypeStruct((rows, full), BF16),
     ]
-    scratch = [pltpu.VMEM((sh, rows), F32)] + [pltpu.VMEM((rows, 2 * sh), F32)] * 3
-    scratch += [DMA, DMA]
-    scratch += [
-        pltpu.VMEM((rows, sh), BF16),
-        pltpu.VMEM((sh, full), BF16),
-        pltpu.VMEM(qkv_all.shape[1:], BF16),
-        DMA((2,)),
-    ]
+    scratch = attend_back_scratch(rows, sh, full, qkv_all)
     if last:
         shapes.append(jax.ShapeDtypeStruct(last[1].shape, F32))
         scratch += scatter_scratch(n, *last[1].shape)
-    if home:
-        slim = home[0].shape
-        shapes.append(jax.ShapeDtypeStruct((1, early_rows(slim[1]), full), BF16))
-        scratch += [DMA, DMA]
     return staged_call(
-        functools.partial(attend_back_kernel, n, slots, step, layer, bool(last), bool(home)),
+        functools.partial(attend_back_kernel, n, slots, step, layer, bool(last), False),
         "attend_back",
         collective_id,
-        args + tuple(last) + tuple(home),
+        args + tuple(last),
         shapes,
         scratch,
         late=(0, 1, 2, 3),
-        plain=(7, 8) + ((9,) if home else ()),
+        plain=(7, 8),
         early=(0, 1),
-        raw=(2,) if home else (),
     )
 
 
@@ -2154,88 +2310,98 @@
     )
     stored = []
     layer_outs = []
-    for layer in range(2):
-        if layer:
-            att, att_low, lse, other, part, out_low_all, qkv = attend_call(
-                n, 2, slots, 1, kpos, qpos, own_cot, out_all, normed, qkv_all, qkv_bias
-            )
-            middle = forward_call(
-                n,
-                4,
-                width,
-                part,
-                x,
-                feats,
-                mask,
-                layer=1,
-                feed=(widen_all, narrow_all, widen_biases),
-            )
-        residual, normed_two, hidden_pre, hidden_low, part = middle
-        stored.append((x, normed, qkv, other, att, att_low, lse, residual, normed_two))
-        stored[-1] += (hidden_pre, hidden_low)
-        if layer == 0:
-            x, normed = forward_call(n, 5, width, part, residual, feats, mask)
-            layer_outs.append(x)
-        else:
-            last = (part, residual, feats)
-
-    found = {}
-    for layer in (1, 0):
-        x, normed, qkv, other, att, att_low, lse, residual, normed_two = stored[layer][:9]
-        hidden_pre, hidden_low = stored[layer][9:]
-        resid_grad, sums_two, resid_low_all, wide, wide_came, slim, pre_sums = resid_call(
+    merge = total_rows * full <= 2**20
+    residual, normed_two, hidden_pre, hidden_low, part = middle
+    stored.append((x, normed, qkv, other, att, att_low, lse, residual, normed_two))
+    stored[-1] += (hidden_pre, hidden_low)
+    (x, normed), attended = follow(
+        merge,
+        forward_step(n, 5, width, part, residual, feats, mask),
+        lambda ended: attend_step(
+            n, 2, slots, 1, kpos, qpos, own_cot, out_all, ended[1], qkv_all, qkv_bias
+        ),
+    )
+    layer_outs.append(x)
+    att, att_low, lse, other, part, out_low_all, qkv = attended
+    second_middle = forward_step(
+        n,
+        4,
+        width,
+        part,
+        x,
+        feats,
+        mask,
+        layer=1,
+        feed=(widen_all, narrow_all, widen_biases),
+    )
+
+    def back_middle(layer, residual, grad, normed_two, hidden_pre, hidden_low, low_all):
+        return resid_step(
             n,
             7 + layer,
             width,
             layer,
             hide,
             residual,
-            out_grad,
+            grad,
             feats,
             mask,
             normed_two,
             hidden_pre,
             hidden_low,
-            out_low_all,
+            low_all,
             widen_all,
             narrow_all,
         )
-        back = attend_back_call(
-            n,
-            9 + layer,
-            slots,
-            layer,
-            qkv,
-            other,
-            resid_low_all,
-            att,
-            lse,
-            kpos,
-            qpos,
-            out_all,
-            qkv_all,
-            last=last if layer else (),
-            home=() if layer else (slim,),
-        )
-        triple, part = back[:2]
-        local = (part, x, resid_grad, feats, mask, normed, triple, att_low, resid_low_all)
+
+    middle, back = follow(
+        merge,
+        second_middle,
+        lambda made: back_middle(1, made[0], out_grad, *made[1:4], out_low_all),
+    )
+    residual, normed_two, hidden_pre, hidden_low, part = middle
+    stored.append((x, normed, qkv, other, att, att_low, lse, residual, normed_two))
+    stored[-1] += (hidden_pre, hidden_low)
+    last = (part, residual, feats)
+
+    found = {}
+    for layer in (1, 0):
+        x, normed, qkv, other, att, att_low, lse, residual, normed_two = stored[layer][:9]
+        hidden_pre, hidden_low = stored[layer][9:]
+        resid_grad, sums_two, resid_low_all, wide, wide_came, slim, pre_sums = back
+        operands = (qkv, other, resid_low_all, att, lse, kpos, qpos, out_all, qkv_all)
         found[layer] = (wide, wide_came, slim, sums_two, pre_sums)
         if layer:
-            layer_outs.append(back[2])
-            upper_d_in, sums_one, out_low_all, qkv_grad, out_rows, slim_came, triple_sums = (
-                input_call(n, 11, width, 0, low, *local, slim)
+            triple, part, last_out = attend_back_call(n, 10, slots, 1, *operands, last=last)
+            layer_outs.append(last_out)
+            upper_step = input_step(
+                n,
+                11,
+                width,
+                0,
+                low,
+                part,
+                x,
+                resid_grad,
+                feats,
+                mask,
+                normed,
+                triple,
+                att_low,
+                resid_low_all,
+                slim,
             )
-            out_grad = upper_d_in
+            below = stored[0]
+            ended, back = follow(
+                merge,
+                upper_step,
+                lambda ended: back_middle(0, below[7], ended[0], *below[8:], ended[2]),
+            )
+            upper_d_in, sums_one, _, qkv_grad, out_rows, slim_came, triple_sums = ended
     lower, upper = found[0], found[1]
-    d_in, narrow_back, qkv_back, out_back, vec, came, widen_back = finale_call(
-        n,
-        12,
-        width,
-        low,
-        *local,
+    streams = (
         lower[2],
         upper[2],
-        back[2],
         slim_came,
         qkv_grad,
         out_rows,
@@ -2251,6 +2417,15 @@
         *lower[:2],
         *upper[:2],
     )
+    own = (x, resid_grad, feats, mask, normed)
+    if merge:
+        ended = closing_call(n, 12, width, low, slots, operands, (*own, att_low, *streams))
+    else:
+        triple, part = attend_back_call(n, 9, slots, 0, *operands)
+        ended = finale_call(
+            n, 12, width, low, part, *own, triple, att_low, resid_low_all, *streams
+        )
+    d_in, narrow_back, qkv_back, out_back, vec, came, widen_back = ended
     settled = settle_call(
         low,
         share,

time: 554 us -> 533 us (0.962)
  Pallas kernels: 541 us -> 520 us
    pallas_call x10 -> x6, Pallas kernels: 530 us -> 509 us  [staged_call(): pl.pallas_call(run, out_shape=shapes, in_specs=[ANY_SPEC if i in late + t...]
where the time goes in v5:
time: 533 us; the launch traced here: 524 us
  Pallas kernels  520 us (98%)
    pallas_call x6, Pallas kernels, staged_call(): pl.pallas_call(run, out_shape=shapes, in_specs=[ANY_SPEC if i in late + t...  509 us
    pallas_call x1, Pallas kernels, settle_call(): pl.pallas_call(functools.partial(settle_kernel, low, sizes), out_shape=[j...  11.4 us

profile of v5, /device:TPU:0, one launch (start us, length us, event | category | flops | bytes accessed | tf_op | source)
XLA Modules:
  0.0 524.3 jit_solution(4388559522798901434)
XLA Ops:
  0.7 0.7 broadcast_multiply_fusion
  1.3 0.1 mul.15
  1.4 0.1 iota_add_fusion
  1.5 0.1 select_n.32
  1.6 0.7 select_n.33.refs_16_.refs_5_.refs_6_
  2.2 0.1 select_n.30
  2.3 1.0 copy.32.refs_15_.refs_4_.refs_5_
  3.4 134.6 %open.1 = (f32[64,1664]{1,0:T(8,128)}, bf16[64,1664]{1,0:T(8,128)(2,1)}, f32[64,1664]{1,0:T(8,128)}, f32[1,1664]{1,0:T(1,128)}, bf16[512,1664]{1,0:T(8,128)(2,1)...) custom-call(bf16[2,64,1600]{2,1,0:T(8,128)(2,1)} %refs_0_.1, ...), custom_call_target="tpu_custom_call" | custom-call | tf_op jit(solution)/shard_map/open/pallas_call | solution.py:719
  137.9 67.4 %forward_rows_attend.1 = (f32[64,1664]{1,0:T(8,128)}, bf16[512,1664]{1,0:T(8,128)(2,1)}, f32[256,512]{1,0:T(8,128)}, bf16[512,256]{1,0:T(8,128)(2,1)}, f32[4,512...) custom-call(bf16[512,1664]{1,0:T(8,128)(2,1)} %get-tuple-element.93., ...), custom_call_target="tpu_custom_call" | custom-call | tf_op jit(solution)/shard_map/forward_rows_attend/pallas_call | solution.py:719
  205.3 100.1 %forward_rows_back_resid.1 = (f32[64,1664]{1,0:T(8,128)}, bf16[512,1664]{1,0:T(8,128)(2,1)}, f32[512,896]{1,0:T(8,128)}, bf16[512,896]{1,0:T(8,128)(2,1)}, bf16[...) custom-call(bf16[512,1664]{1,0:T(8,128)(2,1)} %get-tuple-element.102, ...), custom_call_target="tpu_custom_call" | custom-call | tf_op jit(solution)/shard_map/forward_rows_back_resid/pallas_call | solution.py:719
  305.4 25.7 %attend_back.1 = (bf16[512,768]{1,0:T(8,128)(2,1)}, bf16[512,1664]{1,0:T(8,128)(2,1)}, f32[64,1664]{1,0:T(8,128)}) custom-call(bf16[512,768]{1,0:T(8,128)(2,1)} %get-tuple-element.100.refs_0_, bf16[512,512]{1,0:T(8,128)(2,1)} %get-tuple-element.101.refs_1_, bf16[512,1664]{1,0:T(8,128)(2,1)} %get-tuple-element.109.refs_2_.refs_8_, ...), custom_call_target="tpu_custom_call" | custom-call | tf_op jit(solution)/shard_map/attend_back/pallas_call | solution.py:719
  331.1 91.2 %back_input_back_resid.1 = (f32[64,1664]{1,0:T(8,128)}, f32[3,1664]{1,0:T(4,128)}, bf16[512,1664]{1,0:T(8,128)(2,1)}, bf16[4,208,768]{2,1,0:T(8,128)(2,1)}, bf16...) custom-call(bf16[512,1664]{1,0:T(8,128)(2,1)} %get-tuple-element.114, ...), custom_call_target="tpu_custom_call" | custom-call | tf_op jit(solution)/shard_map/back_input_back_resid/pallas_call | solution.py:719
  422.3 90.1 %closing.1 = (f32[64,1664]{1,0:T(8,128)}, bf16[800,1664]{1,0:T(8,128)(2,1)}, bf16[8,208,768]{2,1,0:T(8,128)(2,1)}, bf16[256,1664]{1,0:T(8,128)(2,1)}, f32[8,896]...) custom-call(bf16[512,768]{1,0:T(8,128)(2,1)} %get-tuple-element.91.refs_0_, ...), custom_call_target="tpu_custom_call" | custom-call | tf_op jit(solution)/shard_map/closing/pallas_call | solution.py:719
  512.5 11.4 %settle.1 = (f32[200,4800]{1,0:T(8,128)}, f32[200,6400]{1,0:T(8,128)}, f32[200,1600]{1,0:T(8,128)}, f32[800,1600]{1,0:T(8,128)}, f32[2,64,1600]{2,1,0:T(8,128)},...) custom-call(bf16[8,208,768]{2,1,0:T(8,128)(2,1)} %get-tuple-element., ...), custom_call_target="tpu_custom_call" | custom-call | tf_op jit(solution)/shard_map/settle/pallas_call | solution.py:1293
  (3 shorter events, 0.0 us)

commit v6 on v5

--- a/solution.py
+++ b/solution.py
@@ -689,7 +689,18 @@
 
 
 def staged_call(
-    body, name, collective_id, args, shapes, scratch, late=(), plain=(), early=(), raw=(), layers={}
+    body,
+    name,
+    collective_id,
+    args,
+    shapes,
+    scratch,
+    late=(),
+    plain=(),
+    early=(),
+    raw=(),
+    layers={},
+    scalars=(),
 ):
     late, early = tuple(late), tuple(early)
     n_in, n_out, n_scratch = len(args), len(shapes), len(scratch)
@@ -711,6 +722,11 @@
         body(io, *ins, *outs, *own)
         io.end()
 
+    def place(i):
+        if i in scalars:
+            return pl.BlockSpec(memory_space=pltpu.SMEM)
+        return ANY_SPEC if i in late + tuple(plain) else VMEM_SPEC
+
     stages = [
         pltpu.VMEM(args[item].shape[1 if item in layers else 0 :], args[item].dtype) for item in late
     ]
@@ -719,7 +735,7 @@
     return pl.pallas_call(
         run,
         out_shape=shapes,
-        in_specs=[ANY_SPEC if i in late + tuple(plain) else VMEM_SPEC for i in range(n_in)],
+        in_specs=[place(i) for i in range(n_in)],
         out_specs=[ANY_SPEC if i in early + tuple(raw) else VMEM_SPEC for i in range(n_out)],
         scratch_shapes=list(scratch) + stages,
         compiler_params=params(collective_id),
@@ -841,12 +857,18 @@
     ]
 
 
-def follow(merge, first, make_second):
+def follow(merge, first, *makers):
     if merge:
-        results = [Result(first, i) for i in range(len(first.shapes))]
-        return run_steps([first, make_second(results)])
-    (found,) = run_steps([first])
-    return found, run_steps([make_second(found)])[0]
+        steps, results = [first], [[Result(first, i) for i in range(len(first.shapes))]]
+        for make in makers:
+            step = make(*results)
+            steps.append(step)
+            results.append([Result(step, i) for i in range(len(step.shapes))])
+        return run_steps(steps)
+    found = run_steps([first])
+    for make in makers:
+        found += run_steps([make(*found)])
+    return found
 
 
 def row_blocks(rows, step):
@@ -993,12 +1015,12 @@
 
 def open_kernel(n, low, width, slots, step, io, *refs):
     tok_ref, cot_ref, vectors, refs = refs[0], refs[1], refs[2:10], refs[10:]
-    qkv_ref, out_ref, widen_ref, narrow_ref, mask, kpos_ref, qpos_ref = refs[:7]
-    refs = refs[7:]
+    qkv_ref, out_ref, widen_ref, narrow_ref, mask, order_ref = refs[:6]
+    refs = refs[6:]
     x_to, cot_to, grad_to, sums_to, normed_to, own_ref, qkv_all, out_all = refs[:8]
     feats_to, qkv_bias, widen_bias, att_ref, low_ref, lse_ref, oth_ref, widen_all = refs[8:16]
-    value_to, tok_all, pre_to, hidden_to, part_to, narrow_all = refs[16:22]
-    refs = refs[22:]
+    value_to, tok_all, pre_to, hidden_to, part_to, narrow_all, kpos_ref, qpos_ref = refs[16:24]
+    refs = refs[24:]
     tok_own, pack, qkv_send, out_rows, widen_raw, narrow_raw, widen_send, narrow_to = refs[:8]
     pack_all, widen, refs = refs[8], refs[9], refs[10:]
     g_ss, g_rs, g_ls, p_ss, p_rs, a_ss, a_rs, w_ss, w_rs, o_ss, o_rs, l_sem = refs[:12]
@@ -1036,6 +1058,22 @@
         lay_rows(low, out_ref, out_rows)
         out.start()
 
+    def lay_places():
+        size = tok_own.shape[0] // HALVES
+        down = lax.broadcasted_iota(jnp.int32, (size, 1), 0)
+        along = lax.broadcasted_iota(jnp.int32, (1, size), 1)
+        found = []
+        for part in range(2):
+            core = 1 - c if part else c
+            for half in range(HALVES):
+                for j in range(n):
+                    first = order_ref[core * n + j, half] * size
+                    spot = ((part * HALVES + half) * n + j) * size
+                    kpos_ref[spot : spot + size] = first + down
+                    if not part:
+                        found.append(first + along)
+        qpos_ref[...] = jnp.concatenate(found, axis=1)
+
     def lay_cot():
         values = with_gaps(cot_ref[s], n, padded)
         cot_to[...] = values
@@ -1044,7 +1082,7 @@
         x_to[...] = tok_own[...].astype(F32)
 
     hide = narrow_ref.shape[0]
-    work = [start_out, widen_load.wait]
+    work = [start_out, lay_places, widen_load.wait]
     work += [functools.partial(lay_widen, j, widen_raw, widen_send) for j in range(n)]
     work += [lay_cot, narrow_load.wait]
     work += [
@@ -1153,7 +1191,7 @@
     feed_forward(tok_all, widen, narrow_all.at[0], widen_bias[0], pre_to, hidden_to, part_to)
 
 
-def open_call(n, low, slots, padded, tokens, cotangent, vectors, weights, mask, kpos, qpos):
+def open_call(n, low, slots, padded, tokens, cotangent, vectors, weights, mask, order):
     qkv, out, widen, narrow = weights
     share, hidden = widen.shape
     width = n * share
@@ -1178,7 +1216,7 @@
         functools.partial(open_kernel, n, low, width, slots, min(total, 256)),
         "open",
         0,
-        (tokens, cotangent, *vectors, qkv, out, widen, narrow, mask, kpos, qpos),
+        (tokens, cotangent, *vectors, qkv, out, widen, narrow, mask, order),
         [
             full_type(rows, full),
             low_type(rows, full),
@@ -1202,6 +1240,8 @@
             low_type(total, hide_full),
             low_type(total, full),
             low_type(2, hide_full, full),
+            jax.ShapeDtypeStruct((2 * total, 1), jnp.int32),
+            jax.ShapeDtypeStruct((1, total), jnp.int32),
         ],
         [
             pltpu.VMEM((rows, full), BF16),
@@ -1226,17 +1266,19 @@
         plain=(12, 13),
         early=(5, 6, 7, 11, 12, 14, 17, 18, 19, 20, 21),
         raw=(4, 15),
+        scalars=(15,),
     )
 
 
 def settle_kernel(low, sizes, *refs):
     sources, vec_ref, came_ref, streams, refs = refs[:4], refs[4], refs[5], refs[6:10], refs[10:]
     outs, stream_to, vectors, refs = refs[:4], refs[4:6], refs[6:14], refs[14:]
-    loaded, made, in_sem, out_sem = refs[:4], refs[4:8], refs[8], refs[9]
+    loaded, made, came, in_sem, out_sem = refs[:4], refs[4:8], refs[8], refs[9], refs[10]
     qkv_ref, widen_ref, out_ref, narrow_ref = loaded
     qkv_to, widen_to, out_to, narrow_to = made
     order = (3, 1, 0, 2)
     loads = {i: fetch(sources[i], loaded[i], in_sem.at[i]) for i in order}
+    came_load = fetch(came_ref, came, in_sem.at[4])
     n, padded, _ = widen_ref.shape
     share = out_to.shape[0]
     hide = narrow_to.shape[0]
@@ -1248,20 +1290,20 @@
         pieces = [values[:, j * padded : j * padded + share] for j in range(n)]
         return jnp.concatenate(pieces, axis=1)
 
-    def lay_rows_back(ref, to):
-        to[...] = without_gaps(ref[: to.shape[0]]).astype(F32)
-
-    def lay_qkv_back():
-        qkv_to[...] = jnp.zeros_like(qkv_to)
+    def lay_rows_back(ref, to, rows):
+        to[rows] = without_gaps(ref[rows]).astype(F32)
+
+    def lay_qkv_back(rows):
+        qkv_to[rows] = jnp.zeros((rows.stop - rows.start, 3 * width), F32)
         for j in range(n):
             for t in range(3):
                 first = t * width + HD * low[j]
-                block = qkv_ref[j, :share, t * sh : (t + 1) * sh]
-                qkv_to[:, first : first + sh] += block.astype(F32)
-
-    def lay_widen_back():
-        pieces = [widen_ref[j, :share, :hide] for j in range(n)]
-        widen_to[...] = jnp.concatenate(pieces, axis=1).astype(F32)
+                block = qkv_ref[j, rows, t * sh : (t + 1) * sh]
+                qkv_to[rows, first : first + sh] += block.astype(F32)
+
+    def lay_widen_back(rows):
+        pieces = [widen_ref[j, rows, :hide] for j in range(n)]
+        widen_to[rows] = jnp.concatenate(pieces, axis=1).astype(F32)
 
     makers = (
         lay_qkv_back,
@@ -1269,17 +1311,23 @@
         functools.partial(lay_rows_back, out_ref, out_to),
         functools.partial(lay_rows_back, narrow_ref, narrow_to),
     )
+    stores = []
+    for i in order:
+        loads[i].wait()
+        count = made[i].shape[0]
+        middle = (count // 2 + 15) // 16 * 16 if count % 8 == 0 else count
+        for x, (start, stop) in enumerate(((0, middle), (middle, count))):
+            if stop > start:
+                makers[i](slice(start, stop))
+                part = pl.ds(start, stop - start)
+                stores.append(fetch(made[i].at[part], outs[i].at[part], out_sem.at[2 * i + x]))
+    came_load.wait()
     for item, to in enumerate(stream_to):
         first, second = (ref[...] for ref in streams[2 * item : 2 * item + 2])
         to[s] = without_gaps(jnp.where(s == 0, first, second))
-        to[1 - s] = without_gaps(came_ref[item].astype(F32))
+        to[1 - s] = without_gaps(came[item].astype(F32))
     for row, (size, to) in enumerate(zip(sizes, vectors)):
         to[...] = vec_ref[row : row + 1, :size]
-    stores = []
-    for i in order:
-        loads[i].wait()
-        makers[i]()
-        stores.append(fetch(made[i], outs[i], out_sem.at[i]))
     for store in stores:
         store.wait()
 
@@ -1298,11 +1346,11 @@
             jax.ShapeDtypeStruct((2, rows, width), F32),
         ]
         + [jax.ShapeDtypeStruct((1, size), F32) for size in sizes],
-        in_specs=[ANY_SPEC] * 4 + [VMEM_SPEC] * 6,
+        in_specs=[ANY_SPEC] * 4 + [VMEM_SPEC, ANY_SPEC] + [VMEM_SPEC] * 4,
         out_specs=[ANY_SPEC] * 4 + [VMEM_SPEC] * 10,
         scratch_shapes=[pltpu.VMEM(m.shape, BF16) for m in (qkv, widen, out, narrow)]
         + [pltpu.VMEM(shape, F32) for shape in big]
-        + [DMA((4,)), DMA((4,))],
+        + [pltpu.VMEM(came.shape, BF16), DMA((5,)), DMA((8,))],
         compiler_params=params(),
         name="settle",
     )(qkv, widen, out, narrow, vec, came, *streams)
@@ -1654,10 +1702,8 @@
         total = wide_pair[0, far].astype(F32) + wide_pair[1, far].astype(F32)
         wide_sum[far] = total.astype(BF16)
         wide_back.start(k)
-    if between is not None:
-        between()
+    leave = between() if between is not None else None
     scatter = Scatter(p, part, *refs[:5])
-    scatter.start()
     back = Home(p, qkv_sum, qkv_to, a_ss, a_rs, ls.at[0])
 
     def x_block(k, src=qkv_far):
@@ -1695,6 +1741,9 @@
     for step in product(normed, triple, qkv):
         step()
     qkv_fold.start()
+    if leave is not None:
+        leave()
+    scatter.start()
     io.need(7, 8)
     work = [functools.partial(home_rows, att, resid, out, low, share), out_fold.start]
     work += qkv_fold.steps()
@@ -2049,7 +2098,7 @@
     sh = slots * HD
     scale = HD**-0.5
     if not greeted:
-        greet(p, line=last, sibling=True)
+        enter(io, p, line=last, sibling=True)
     between = []
     if last:
         scatter = Scatter(p, part_ref, *refs[10:])
@@ -2058,11 +2107,11 @@
     io.need(2)
     out_load.wait()
 
-    def enter(first, size):
+    def begin(first, size):
         some = pl.ds(first, size)
         grad_ref[some] = dot_t(resid[some], out_weight[...]).astype(BF16)
 
-    row_blocks(rows, enter)
+    row_blocks(rows, begin)
     io.need(0, 1, 3)
 
     def at(base, slot):
@@ -2122,6 +2171,9 @@
         part_to[some] = dot_t(triple_ref[some], weight).astype(BF16)
 
     io.done(0)
+    if greeted:
+        swap.wait_send()
+        return functools.partial(row_blocks, rows, leave)
     row_blocks(rows, leave)
     io.done(1)
     if last:
@@ -2147,7 +2199,7 @@
 
     def between():
         mapped = Mapped(io, {i: i for i in range(9)}, {})
-        attend_back_kernel(
+        return attend_back_kernel(
             n, slots, step, 0, False, True, mapped, *back, triple, part, *back_scratch
         )
 
@@ -2194,7 +2246,7 @@
     )
 
 
-def attend_back_call(n, collective_id, slots, layer, *args, last=()):
+def attend_back_step(n, collective_id, slots, layer, *args, last=()):
     qkv, out_all, qkv_all = args[0], args[7], args[8]
     rows = qkv.shape[0]
     sh = slots * HD
@@ -2208,13 +2260,14 @@
     if last:
         shapes.append(jax.ShapeDtypeStruct(last[1].shape, F32))
         scratch += scatter_scratch(n, *last[1].shape)
-    return staged_call(
+    return Step(
         functools.partial(attend_back_kernel, n, slots, step, layer, bool(last), False),
         "attend_back",
         collective_id,
         args + tuple(last),
         shapes,
         scratch,
+        dict(line=bool(last), sibling=True),
         late=(0, 1, 2, 3),
         plain=(7, 8),
         early=(0, 1),
@@ -2243,7 +2296,6 @@
         narrow_weight,
         narrow_bias,
     ) = (member[0] for member in vectors_and_weights)
-    c = lax.axis_index("ctx")
     _, rows, width = tokens.shape
     hidden = widen_weight.shape[1]
     share = width // n
@@ -2253,17 +2305,8 @@
     low, slots = windows(width, n)
     sh = slots * HD
     total_rows = n * rows
-    half_rows = rows // HALVES
 
     mask = jnp.asarray(np.arange(full)[None] % padded < share, F32)
-    order = block_order.reshape(2, n, HALVES).transpose(0, 2, 1)
-    places = order[..., None] * half_rows + jnp.arange(half_rows, dtype=jnp.int32)
-    places = places.reshape(2, total_rows)
-    own_places = jnp.where(c == 0, places[0], places[1])
-    oth_places = jnp.where(c == 0, places[1], places[0])
-    kpos = jnp.concatenate([own_places, oth_places])[:, None]
-    qpos = own_places[None, :]
-
     (
         x,
         own_cot,
@@ -2283,6 +2326,8 @@
         widen_all,
         *middle,
         narrow_all,
+        kpos,
+        qpos,
     ) = open_call(
         n,
         low,
@@ -2305,8 +2350,7 @@
         ],
         (qkv_weight, out_weight, widen_weight, narrow_weight),
         mask,
-        kpos,
-        qpos,
+        block_order,
     )
     stored = []
     layer_outs = []
@@ -2354,15 +2398,20 @@
             narrow_all,
         )
 
-    middle, back = follow(
+    upper = (qkv, other, att, lse, kpos, qpos, out_all, qkv_all)
+    middle, back, (triple, part, last_out) = follow(
         merge,
         second_middle,
         lambda made: back_middle(1, made[0], out_grad, *made[1:4], out_low_all),
+        lambda made, back: attend_back_step(
+            n, 10, slots, 1, *upper[:2], back[2], *upper[2:], last=(made[4], made[0], feats)
+        ),
     )
-    residual, normed_two, hidden_pre, hidden_low, part = middle
+    upper_part = part
+    layer_outs.append(last_out)
+    residual, normed_two, hidden_pre, hidden_low, _ = middle
     stored.append((x, normed, qkv, other, att, att_low, lse, residual, normed_two))
     stored[-1] += (hidden_pre, hidden_low)
-    last = (part, residual, feats)
 
     found = {}
     for layer in (1, 0):
@@ -2372,15 +2421,13 @@
         operands = (qkv, other, resid_low_all, att, lse, kpos, qpos, out_all, qkv_all)
         found[layer] = (wide, wide_came, slim, sums_two, pre_sums)
         if layer:
-            triple, part, last_out = attend_back_call(n, 10, slots, 1, *operands, last=last)
-            layer_outs.append(last_out)
             upper_step = input_step(
                 n,
                 11,
                 width,
                 0,
                 low,
-                part,
+                upper_part,
                 x,
                 resid_grad,
                 feats,
@@ -2421,7 +2468,7 @@
     if merge:
         ended = closing_call(n, 12, width, low, slots, operands, (*own, att_low, *streams))
     else:
-        triple, part = attend_back_call(n, 9, slots, 0, *operands)
+        ((triple, part),) = run_steps([attend_back_step(n, 9, slots, 0, *operands)])
         ended = finale_call(
             n, 12, width, low, part, *own, triple, att_low, resid_low_all, *streams
         )

time: 533 us -> 519 us (0.974)
  Pallas kernels: 520 us -> 508 us
    pallas_call x6 -> x5, Pallas kernels: 509 us -> 497 us  [staged_call(): pl.pallas_call(run, out_shape=shapes, in_specs=[place(i) for i in range(n...]
where the time goes in v6:
time: 519 us; the launch traced here: 510 us
  Pallas kernels  508 us (98%)
    pallas_call x5, Pallas kernels, staged_call(): pl.pallas_call(run, out_shape=shapes, in_specs=[place(i) for i in range(n...  497 us
    pallas_call x1, Pallas kernels, settle_call(): pl.pallas_call(functools.partial(settle_kernel, low, sizes), out_shape=[j...  10.5 us

profile of v6, /device:TPU:0, one launch (start us, length us, event | category | flops | bytes accessed | tf_op | source)
XLA Modules:
  0.0 510.4 jit_solution(5257781530843582653)
XLA Ops:
  0.6 1.4 copy.30.refs_15_
  2.0 134.5 %open.1 = (f32[64,1664]{1,0:T(8,128)}, bf16[64,1664]{1,0:T(8,128)(2,1)}, f32[64,1664]{1,0:T(8,128)}, f32[1,1664]{1,0:T(1,128)}, bf16[512,1664]{1,0:T(8,128)(2,1)...) custom-call(bf16[2,64,1600]{2,1,0:T(8,128)(2,1)} %refs_0_.1, ...), custom_call_target="tpu_custom_call" | custom-call | tf_op jit(solution)/shard_map/open/pallas_call | solution.py:735
  136.5 67.3 %forward_rows_attend.1 = (f32[64,1664]{1,0:T(8,128)}, bf16[512,1664]{1,0:T(8,128)(2,1)}, f32[256,512]{1,0:T(8,128)}, bf16[512,256]{1,0:T(8,128)(2,1)}, f32[4,512...) custom-call(bf16[512,1664]{1,0:T(8,128)(2,1)} %get-tuple-element.93., ...), custom_call_target="tpu_custom_call" | custom-call | tf_op jit(solution)/shard_map/forward_rows_attend/pallas_call | solution.py:735
  203.8 115.2 %forward_rows_back_resid_attend_back.1 = (f32[64,1664]{1,0:T(8,128)}, bf16[512,1664]{1,0:T(8,128)(2,1)}, f32[512,896]{1,0:T(8,128)}, bf16[512,896]{1,0:T(8,128)(...) custom-call(bf16[512,1664]{1,0:T(8,128)(2,1)} %get-tuple-element.102, ...), custom_call_target="tpu_custom_call" | custom-call | tf_op jit(solution)/shard_map/forward_rows_back_resid_attend_back/pallas_call | solution.py:735
  319.0 90.6 %back_input_back_resid.1 = (f32[64,1664]{1,0:T(8,128)}, f32[3,1664]{1,0:T(4,128)}, bf16[512,1664]{1,0:T(8,128)(2,1)}, bf16[4,208,768]{2,1,0:T(8,128)(2,1)}, bf16...) custom-call(bf16[512,1664]{1,0:T(8,128)(2,1)} %get-tuple-element.113, ...), custom_call_target="tpu_custom_call" | custom-call | tf_op jit(solution)/shard_map/back_input_back_resid/pallas_call | solution.py:735
  409.6 89.9 %closing.1 = (f32[64,1664]{1,0:T(8,128)}, bf16[800,1664]{1,0:T(8,128)(2,1)}, bf16[8,208,768]{2,1,0:T(8,128)(2,1)}, bf16[256,1664]{1,0:T(8,128)(2,1)}, f32[8,896]...) custom-call(bf16[512,768]{1,0:T(8,128)(2,1)} %get-tuple-element.91.refs_0_, ...), custom_call_target="tpu_custom_call" | custom-call | tf_op jit(solution)/shard_map/closing/pallas_call | solution.py:735
  499.4 10.5 %settle.1 = (f32[200,4800]{1,0:T(8,128)}, f32[200,6400]{1,0:T(8,128)}, f32[200,1600]{1,0:T(8,128)}, f32[800,1600]{1,0:T(8,128)}, f32[2,64,1600]{2,1,0:T(8,128)},...) custom-call(bf16[8,208,768]{2,1,0:T(8,128)(2,1)} %get-tuple-element., ...), custom_call_target="tpu_custom_call" | custom-call | tf_op jit(solution)/shard_map/settle/pallas_call | solution.py:1341

commit v7 on v6

--- a/solution.py
+++ b/solution.py
@@ -1692,8 +1692,16 @@
         src, dst, sem = choices[1][item]
         pltpu.make_async_copy(src, dst, ls.at[sem]).wait()
 
-    slim_cross = Cross(p, slims[0], slim_pair.at[1], x_ss.at[zn + 2], x_rs.at[zn + 2], 1)
-    slim_cross.start()
+    count = slims[0].shape[1]
+    first = count * 3 // 5 // 16 * 16
+
+    def slim_rows(item, start, size):
+        rows = pl.ds(start, size)
+        sems = (x_ss.at[zn + 2 + item], x_rs.at[zn + 2 + item])
+        return Cross(p, slims[0].at[:, rows], slim_pair.at[1, :, rows], *sems, 1)
+
+    slim_crosses = (slim_rows(0, 0, first), slim_rows(1, first, count - first))
+    slim_crosses[0].start()
     wide_back = Home(p, wide_sum, wide_to, w_ss, w_rs, ls.at[8])
     chosen_wait(0)
     chosen_wait(1)
@@ -1819,6 +1827,7 @@
     add_home(p, out_sum, 0, out_own, out_in, out_far, out_in)
     for k in range(zn):
         x_block(k).wait_send()
+    slim_crosses[1].start()
     chosen_wait(2)
 
     @pl.when(s == 1)
@@ -1827,7 +1836,8 @@
 
     for step in wide_back.steps():
         step()
-    slim_cross.finish()
+    for cross in slim_crosses:
+        cross.finish()
     slim_sum[0] = (slim_pair[0, 0].astype(F32) + slim_pair[1, 0].astype(F32)).astype(BF16)
 
     def row_copies(w, src, dst):
@@ -1901,8 +1911,8 @@
             pltpu.VMEM((2, rows, full), BF16),
             DMA((2, zn)),
             DMA((2, zn)),
-            DMA((zn + 3,)),
-            DMA((zn + 3,)),
+            DMA((zn + 4,)),
+            DMA((zn + 4,)),
             DMA((2, n)),
             DMA((2, n)),
             DMA((3,)),

time: 519 us -> 524 us (level)
  no operation moved by 1% of the time
where the time goes in v7:
time: 524 us; the launch traced here: 516 us
  Pallas kernels  513 us (98%)
    pallas_call x5, Pallas kernels, staged_call(): pl.pallas_call(run, out_shape=shapes, in_specs=[place(i) for i in range(n...  503 us
    pallas_call x1, Pallas kernels, settle_call(): pl.pallas_call(functools.partial(settle_kernel, low, sizes), out_shape=[j...  10.5 us

profile of v7, /device:TPU:0, one launch (start us, length us, event | category | flops | bytes accessed | tf_op | source)
XLA Modules:
  0.0 515.6 jit_solution(14035351152522164892)
XLA Ops:
  0.6 1.4 copy.30.refs_15_
  2.0 134.5 %open.1 = (f32[64,1664]{1,0:T(8,128)}, bf16[64,1664]{1,0:T(8,128)(2,1)}, f32[64,1664]{1,0:T(8,128)}, f32[1,1664]{1,0:T(1,128)}, bf16[512,1664]{1,0:T(8,128)(2,1)...) custom-call(bf16[2,64,1600]{2,1,0:T(8,128)(2,1)} %refs_0_.1, ...), custom_call_target="tpu_custom_call" | custom-call | tf_op jit(solution)/shard_map/open/pallas_call | solution.py:735
  136.5 67.3 %forward_rows_attend.1 = (f32[64,1664]{1,0:T(8,128)}, bf16[512,1664]{1,0:T(8,128)(2,1)}, f32[256,512]{1,0:T(8,128)}, bf16[512,256]{1,0:T(8,128)(2,1)}, f32[4,512...) custom-call(bf16[512,1664]{1,0:T(8,128)(2,1)} %get-tuple-element.93., ...), custom_call_target="tpu_custom_call" | custom-call | tf_op jit(solution)/shard_map/forward_rows_attend/pallas_call | solution.py:735
  203.8 115.2 %forward_rows_back_resid_attend_back.1 = (f32[64,1664]{1,0:T(8,128)}, bf16[512,1664]{1,0:T(8,128)(2,1)}, f32[512,896]{1,0:T(8,128)}, bf16[512,896]{1,0:T(8,128)(...) custom-call(bf16[512,1664]{1,0:T(8,128)(2,1)} %get-tuple-element.102, ...), custom_call_target="tpu_custom_call" | custom-call | tf_op jit(solution)/shard_map/forward_rows_back_resid_attend_back/pallas_call | solution.py:735
  319.0 90.6 %back_input_back_resid.1 = (f32[64,1664]{1,0:T(8,128)}, f32[3,1664]{1,0:T(4,128)}, bf16[512,1664]{1,0:T(8,128)(2,1)}, bf16[4,208,768]{2,1,0:T(8,128)(2,1)}, bf16...) custom-call(bf16[512,1664]{1,0:T(8,128)(2,1)} %get-tuple-element.113, ...), custom_call_target="tpu_custom_call" | custom-call | tf_op jit(solution)/shard_map/back_input_back_resid/pallas_call | solution.py:735
  409.6 95.0 %closing.1 = (f32[64,1664]{1,0:T(8,128)}, bf16[800,1664]{1,0:T(8,128)(2,1)}, bf16[8,208,768]{2,1,0:T(8,128)(2,1)}, bf16[256,1664]{1,0:T(8,128)(2,1)}, f32[8,896]...) custom-call(bf16[512,768]{1,0:T(8,128)(2,1)} %get-tuple-element.91.refs_0_, ...), custom_call_target="tpu_custom_call" | custom-call | tf_op jit(solution)/shard_map/closing/pallas_call | solution.py:735
  504.6 10.5 %settle.1 = (f32[200,4800]{1,0:T(8,128)}, f32[200,6400]{1,0:T(8,128)}, f32[200,1600]{1,0:T(8,128)}, f32[800,1600]{1,0:T(8,128)}, f32[2,64,1600]{2,1,0:T(8,128)},...) custom-call(bf16[8,208,768]{2,1,0:T(8,128)(2,1)} %get-tuple-element., ...), custom_call_target="tpu_custom_call" | custom-call | tf_op jit(solution)/shard_map/settle/pallas_call | solution.py:1341
